TPU v7x, 32 devices: a whole 2x2x4 slice. The times are simulated.
32 devices in a mesh: filt: 16 (over z, y, core), space: 2 (over x).
Axes of the slice: x: 2, y: 2, z: 4, core: 2. Of those that a mesh axis runs over, the one named last changes fastest.
Arguments:
- volume: bfloat16 [256, 8, 4, 128], P('filt', 'space'), may hold values from -6 to 6
- kernel: bfloat16 [512, 3, 3, 3, 256], P('filt'), may hold values from -0.078125 to 0.078125
- filter_bias: bfloat16 [512], P('filt'), may hold values from -3 to 3
Outputs:
- pooled: bfloat16 [512, 4, 2, 64], P('filt', 'space')
All inputs are finite; a program needn't handle non-finite values.
Results may differ from a plain program's by a relative error of at most 0.001.
Values may be sent and summed in bfloat16 or wider, within the bound.
No kernel may reach another device: no remote copies, remote signals or barrier semaphores. Data moves between devices by JAX's collectives and lax.ppermute only.
A program may use at most 64 MiB of HBM per device.

v0:
```python
import jax
import jax.numpy as jnp
from jax import lax
from jax.sharding import PartitionSpec as P

slope = 0.3


def with_halo(block, sides, width):
    for axis, dim in sides:
        count = lax.axis_size(axis)
        forward = [(i, i + 1) for i in range(count - 1)]
        backward = [(target, source) for source, target in forward]
        low = lax.ppermute(
            lax.slice_in_dim(block, block.shape[dim] - width, None, axis=dim), axis, forward
        )
        high = lax.ppermute(lax.slice_in_dim(block, 0, width, axis=dim), axis, backward)
        block = jnp.concatenate([low, block, high], axis=dim)
    return block


def convolve(inputs, weights, padding):
    return lax.conv_general_dilated(
        inputs[None],
        weights,
        (1, 1, 1),
        padding,
        dimension_numbers=("NCDHW", "ODHWI", "NCDHW"),
        preferred_element_type=jnp.float32,
    )[0]


def finish(summed, filter_bias):
    activated = summed + filter_bias.astype(jnp.float32)[:, None, None, None]
    activated = jnp.where(activated > 0, activated, slope * activated)
    filters, depth, height, across = activated.shape
    blocked = activated.reshape(filters, depth // 2, 2, height // 2, 2, across // 2, 2)
    return jnp.max(blocked, axis=(2, 4, 6)).astype(jnp.bfloat16)


def on_device(volume, kernel, filter_bias):
    local_in, slab_depth, height, across = volume.shape
    padded = with_halo(volume, (("space", 1),), 1)
    zeroed = jnp.zeros((kernel.shape[0], slab_depth, height, across), jnp.float32)
    summed = zeroed + convolve(
        lax.all_gather(padded, "filt", axis=0, tiled=True), kernel, ((0, 0), (1, 1), (1, 1))
    )
    return finish(summed, filter_bias)


def solution(mesh):
    in_specs = (P("filt", "space", None, None), P("filt", None, None, None, None), P("filt"))
    out_specs = P("filt", "space", None, None)
    return jax.shard_map(
        on_device, mesh=mesh, in_specs=in_specs, out_specs=out_specs, check_vma=False
    )
```

profile of v0, /device:TPU:0, one launch (start us, length us, event | category | flops | bytes accessed | tf_op | source)
XLA Modules:
  0.0 81.8 jit_solution(3691272180576459420)
XLA Ops:
  6.5 0.0 copy-start
  6.5 0.0 all-gather.2.cloned.1.call-start
  6.5 0.8 fusion.16
  7.3 4.8 %collective-permute-start = (bf16[16,1,4,128]{3,2,1,0:T(4,128)(2,1)S(1)}, bf16[16,1,4,128]{3,2,1,0:T(4,128)(2,1)S(1)}, u32[]{:S(2)}, u32[]{:S(2)}) collective-permute-start(bf16[16,1,4,128]{3,2,1,0:T(4,128)(2,1)S(1)} %get-tuple-element.5), channel_id=1, source_target_pairs={{0,1},{2,3},{4,5},{6,7},{8,9},{10,11},{12,13},{14,15},{16,17},{18,... | collective-permute-start | bytes 49160 | tf_op jit(solution)/shard_map/ppermute | solution.py:14
  12.2 1.3 %collective-permute-start.1 = (bf16[16,1,4,128]{3,2,1,0:T(4,128)(2,1)S(1)}, bf16[16,1,4,128]{3,2,1,0:T(4,128)(2,1)S(1)}, u32[]{:S(2)}, u32[]{:S(2)}) collective-permute-start(bf16[16,1,4,128]{3,2,1,0:T(4,128)(2,1)S(1)} %get-tuple-element.6), channel_id=1, source_target_pairs={{1,0},{3,2},{5,4},{7,6},{9,8},{11,10},{13,12},{15,14},{17,16},{19,... | collective-permute-start | bytes 49160 | tf_op jit(solution)/shard_map/ppermute | solution.py:17
  13.5 0.1 collective-permute-done
  13.6 4.2 %collective-permute-done.1 = bf16[16,1,4,128]{3,2,1,0:T(4,128)(2,1)S(1)} collective-permute-done((bf16[16,1,4,128]{3,2,1,0:T(4,128)(2,1)S(1)}, bf16[16,1,4,128]{3,2,1,0:T(4,128)(2,1)S(1)}, u32[]{:S(2)}, u32[]{:S(2)}) %collective-permute-start.1) | collective-permute-done | bytes 16416 | tf_op jit(solution)/shard_map/ppermute | solution.py:17
  17.8 1.5 %pad_maximum_fusion = bf16[16,6,4,128]{3,2,1,0:T(4,128)(2,1)} fusion(bf16[16,1,4,128]{3,2,1,0:T(4,128)(2,1)S(1)} %collective-permute-done.1, bf16[16,4,4,128]{3,2,1,0:T(4,128)(2,1)} %param.3, bf16[16,1,4,128]{3,2,1,0:T(4,128)(2,1)S(1)} %collective-permute-done), kind=kLoop, calls=%fused_computation.12 | loop fusion | flops 98304 | bytes 196608 | tf_op jit(solution)/shard_map/concatenate | solution.py:18
  19.4 0.0 all-gather.2.cloned.1.call-update
  19.4 0.7 convert_element_type.6
  20.1 39.5 %all-gather.2.cloned.1.call-done = bf16[256,6,4,128]{3,2,1,0:T(4,128)(2,1)} async-done(((bf16[16,6,4,128]{3,2,1,0:T(4,128)(2,1)}), bf16[256,6,4,128]{3,2,1,0:T(4,128)(2,1)}) %all-gather.2.cloned.1.call-update) | async-done | bytes 1572880 | tf_op jit(solution)/shard_map/all_gather | solution.py:46
  59.6 3.2 %copy.19 = bf16[256,6,4,1,128]{0,2,4,1,3:T(4,128)(2,1)S(1)} copy(bf16[256,6,4,1,128]{4,2,1,0,3:T(4,128)(2,1)} %bitcast.15) | data formatting | bytes 3145728
  62.8 0.6 pad.clone
  63.4 0.0 copy-start.1
  63.4 0.2 copy.15
  63.7 0.0 copy-done
  63.7 0.4 copy-done.1
  64.1 8.3 %fusion.8 = f32[4,4,8,17,32]{4,2,3,1,0:T(8,128)S(1)} fusion(bf16[32,3,3,3,256]{4,0,3,2,1:T(8,128)(2,1)S(1)} %copy-done, bf16[256,6,4,1,7,2]{0,4,5,2,1,3:T(8,128)(2,1)S(1)} %slice.10, bf16[256,6,4,1,8,17]{0,4,5,2,1,3:T(8,128)(2,1)S(1)} %copy.15, pred[8,17]{0,1:T(8,128)(4,1)S(1)} %copy-done.1), kind=kOutput, calls=%fused_computation.9 | convolution fusion | flops 807833600 | bytes 2564232 | tf_op jit(solution)/shard_map/conv_general_dilated | solution.py:23
  72.5 0.3 copy.16
  72.8 0.1 slice.11
  72.8 1.4 %fusion.11 = bf16[32,2,2,64]{0,2,3,1:T(2,128)(2,1)S(1)} fusion(f32[32,2,2,2,2,64,2]{0,4,3,6,5,2,1:T(2,128)S(1)} %bitcast.14, f32[32]{0:T(128)S(1)} %convert_element_type.6), kind=kLoop, calls=%fused_computation.10 | loop fusion | flops 319488 | bytes 278656 | tf_op jit(solution)/shard_map/reduce_max | solution.py:38
  74.2 0.1 copy.17
  74.3 0.6 copy.18
  (1 shorter events, 0.0 us)
Async XLA Ops:
  6.5 57.2 %copy-start = (bf16[32,3,3,3,256]{4,0,3,2,1:T(8,128)(2,1)S(1)}, bf16[32,3,3,3,256]{4,0,3,2,1:T(8,128)(2,1)}, u32[]{:S(2)}) copy-start(bf16[32,3,3,3,256]{4,0,3,2,1:T(8,128)(2,1)} %param.4) | copy-start | bytes 1327108
  6.5 53.0 %all-gather.2.cloned.1.call-start = ((), (), s32[]{:S(2)}) async-start(), calls=%async_computation | async-start | bytes 1671168 | tf_op jit(solution)/shard_map/all_gather | solution.py:46
  7.3 6.3 %collective-permute-start = (bf16[16,1,4,128]{3,2,1,0:T(4,128)(2,1)S(1)}, bf16[16,1,4,128]{3,2,1,0:T(4,128)(2,1)S(1)}, u32[]{:S(2)}, u32[]{:S(2)}) collective-permute-start(bf16[16,1,4,128]{3,2,1,0:T(4,128)(2,1)S(1)} %get-tuple-element.5), channel_id=1, source_target_pairs={{0,1},{2,3},{4,5},{6,7},{8,9},{10,11},{12,13},{14,15},{16,17},{18,... | collective-permute-start | bytes 49160 | tf_op jit(solution)/shard_map/ppermute | solution.py:14
  12.2 5.6 %collective-permute-start.1 = (bf16[16,1,4,128]{3,2,1,0:T(4,128)(2,1)S(1)}, bf16[16,1,4,128]{3,2,1,0:T(4,128)(2,1)S(1)}, u32[]{:S(2)}, u32[]{:S(2)}) collective-permute-start(bf16[16,1,4,128]{3,2,1,0:T(4,128)(2,1)S(1)} %get-tuple-element.6), channel_id=1, source_target_pairs={{1,0},{3,2},{5,4},{7,6},{9,8},{11,10},{13,12},{15,14},{17,16},{19,... | collective-permute-start | bytes 49160 | tf_op jit(solution)/shard_map/ppermute | solution.py:17
  63.4 0.7 copy-start.1
Sparse Core Ops, SparseCore 0:
  19.5 39.9 all-gather.1
where the time goes:
time: 82.1 us; the launch traced here: 81.8 us
  waiting for transfers between devices  43.8 us (53%)
  between operations  13.5 us (16%)
  matrix products  8.33 us (10%)
  local copies, waits for them, and re-layouts  6.42 us (8%)
  starting transfers between devices  6.14 us (7%)
  other arithmetic  3.57 us (4%)
    all_gather x1, waiting for transfers between devices, on_device(): lax.all_gather(padded, 'filt', axis=0, tiled=True)  39.5 us
    conv_general_dilated x1, matrix products, convolve(): lax.conv_general_dilated(inputs[None], weights, (1, 1, 1), padding, dimen...  8.33 us
    ppermute x1, starting transfers between devices, with_halo(): lax.ppermute(lax.slice_in_dim(block, block.shape[dim] - width, None, axis...  4.84 us
    ppermute x1, waiting for transfers between devices, with_halo(): lax.ppermute(lax.slice_in_dim(block, 0, width, axis=dim), axis, backward)  4.21 us
    unnamed x5, local copies, waits for them, and re-layouts  3.63 us
  transfers between devices with their start and end apart: 3, of which 3 were waited for; matrix products, arithmetic and copies ran while one was open for 1% of the time, Pallas kernels for 0%

commit v1 on v0

v1 whole, which is shorter than its diff:
```python
import jax
import jax.numpy as jnp
from jax import lax
from jax.experimental import pallas as pl
from jax.experimental.pallas import tpu as pltpu
from jax.sharding import PartitionSpec as P

slope = 0.3
f32, bf16 = jnp.float32, jnp.bfloat16


def boundary_planes(volume):
    count = lax.axis_size("space")
    depth = volume.shape[1]
    first = lax.slice_in_dim(volume, 0, 1, axis=1)
    last = lax.slice_in_dim(volume, depth - 1, depth, axis=1)
    if count == 2:
        here = lax.axis_index("space")
        got = lax.ppermute(jnp.where(here == 0, last, first), "space", [(0, 1), (1, 0)])
        return [got]
    forward = [(i, i + 1) for i in range(count - 1)]
    low = lax.ppermute(last, "space", forward)
    high = lax.ppermute(first, "space", [(t, s) for s, t in forward])
    return [low, high]


def rows_of(ref, row):
    return jnp.concatenate([ref[k, row] for k in range(ref.shape[0])], axis=0)


def make_padded(vol_ref, pad_ref, flags_ref, depth, height):
    across = vol_ref.shape[-1]
    channels = pad_ref.shape[1]
    extra = vol_ref.shape[1] // height - depth
    zero = jnp.zeros((channels, across), bf16)
    for plane in range(depth + 2):
        pad_ref[plane, :, 0:across] = zero
        pad_ref[plane, :, (height + 1) * across :] = zero
        for y in range(height):
            if 1 <= plane <= depth:
                rows = rows_of(vol_ref, (plane - 1) * height + y)
            else:
                which = 0 if plane == 0 or extra == 1 else 1
                rows = rows_of(vol_ref, (depth + which) * height + y)
                keep = flags_ref[1 if plane == 0 else 2]
                rows = jnp.where(keep > 0, rows, zero)
            pad_ref[plane, :, (y + 1) * across : (y + 2) * across] = rows


def taps_product(weights, pad_ref, z, y, across):
    left = jnp.concatenate([weights[a][b] for a in range(3) for b in range(3)], axis=1)
    right = jnp.concatenate(
        [
            pad_ref[z + a, :, (y + b) * across : (y + b + 2) * across]
            for a in range(3)
            for b in range(3)
        ],
        axis=0,
    )
    return jnp.dot(left, right, preferred_element_type=f32)


def own_half(flags_ref, w_ref, vol_ref, sum_ref, w_out_ref, pad_ref, *, depth, height, block):
    across = vol_ref.shape[-1]
    cin = w_ref.shape[1]
    half = cin // 2
    core = flags_ref[0]
    source = lax.broadcasted_iota(jnp.int32, (cin, cin), 0)
    target = lax.broadcasted_iota(jnp.int32, (cin, cin), 1)
    place = target & (half - 1)
    part = jnp.where(target < half, core, 1 - core)
    wanted = ((place & ~(block - 1)) << 1) + part * block + (place & (block - 1))
    shuffle = jnp.where(source == wanted, 1.0, 0.0).astype(bf16)
    ordered = jnp.dot(w_ref[...], shuffle, preferred_element_type=f32).astype(bf16)
    w_out_ref[...] = ordered[:, half:]
    rows = w_ref.shape[0] // 9
    weights = [
        [ordered[(a * 3 + b) * rows : (a * 3 + b + 1) * rows, :half] for b in range(3)]
        for a in range(3)
    ]
    make_padded(vol_ref, pad_ref, flags_ref, depth, height)
    for z in range(depth):
        for y in range(0, height, 2):
            sum_ref[z * (height // 2) + y // 2] = taps_product(weights, pad_ref, z, y, across)


def other_half(flags_ref, w_ref, vol_ref, sum_ref, bias_ref, out_ref, pad_ref, *, depth, height):
    across = vol_ref.shape[-1]
    rows = w_ref.shape[0] // 9
    filters = rows // 3
    weights = [
        [w_ref[(a * 3 + b) * rows : (a * 3 + b + 1) * rows] for b in range(3)] for a in range(3)
    ]
    make_padded(vol_ref, pad_ref, flags_ref, depth, height)
    lane = lax.broadcasted_iota(jnp.int32, (filters, across), 1)
    bias = bias_ref[...]
    pooled = {}
    for z in range(depth):
        for y in range(0, height, 2):
            total = taps_product(weights, pad_ref, z, y, across)
            total += sum_ref[z * (height // 2) + y // 2]
            for k in range(2):
                part = total[:, k * across : (k + 1) * across]
                left = pltpu.roll(part[:filters], 1, 1)
                right = pltpu.roll(part[2 * filters :], across - 1, 1)
                v = part[filters : 2 * filters] + bias
                v += jnp.where(lane > 0, left, 0.0)
                v += jnp.where(lane < across - 1, right, 0.0)
                v = jnp.where(v > 0, v, slope * v)
                key = (z // 2, y // 2)
                pooled[key] = v if key not in pooled else jnp.maximum(pooled[key], v)
    stacked = jnp.concatenate(
        [pooled[z, y] for z in range(depth // 2) for y in range(height // 2)], axis=0
    )
    stacked = jnp.maximum(stacked, pltpu.roll(stacked, across - 1, 1)).astype(bf16)
    cells = (depth // 2) * (height // 2)
    count = cells * filters
    target = lax.broadcasted_iota(jnp.int32, (count, count), 0)
    source = lax.broadcasted_iota(jnp.int32, (count, count), 1)
    wanted = (target & (cells - 1)) * filters + target // cells
    rows_pick = jnp.where(source == wanted, 1.0, 0.0).astype(bf16)
    lane_from = lax.broadcasted_iota(jnp.int32, (across, across // 2), 0)
    lane_to = lax.broadcasted_iota(jnp.int32, (across, across // 2), 1)
    lanes_pick = jnp.where(lane_from == 2 * lane_to, 1.0, 0.0).astype(bf16)
    picked = jnp.dot(stacked, lanes_pick, preferred_element_type=f32).astype(bf16)
    out_ref[...] = jnp.dot(rows_pick, picked, preferred_element_type=f32).astype(bf16)


def on_device(volume, kernel, filter_bias):
    block, depth, height, across = volume.shape
    filters, cin = kernel.shape[0], kernel.shape[-1]
    count = lax.axis_size("filt")
    spaces = lax.axis_size("space")
    here = lax.axis_index("space")
    core = lax.axis_index("filt") % 2
    flags = jnp.stack([core, here, spaces - 1 - here]).astype(jnp.int32)

    planes = jnp.concatenate([volume] + boundary_planes(volume), axis=1)
    planes = planes.transpose(1, 2, 0, 3).reshape(-1, block, across)
    same_core = [[2 * i + c for i in range(count // 2)] for c in range(2)]
    copies = jnp.broadcast_to(planes[None], (count // 2,) + planes.shape)
    mine = lax.all_to_all(copies, "filt", 0, 0, axis_index_groups=same_core)
    theirs = lax.ppermute(mine, "filt", [(i, i ^ 1) for i in range(count)])

    bias = jnp.broadcast_to(filter_bias.astype(f32)[:, None], (filters, across))
    weights = kernel.transpose(1, 2, 3, 0, 4).reshape(27 * filters, cin)
    vmem = pl.BlockSpec(memory_space=pltpu.VMEM)
    smem = pl.BlockSpec(memory_space=pltpu.SMEM)
    padded = pltpu.VMEM((depth + 2, cin // 2, (height + 2) * across), bf16)
    sums = (depth * height // 2, 3 * filters, 2 * across)
    params = pltpu.CompilerParams(vmem_limit_bytes=24 << 20)
    flops = 27 * filters * cin * depth * height * across

    def own(flags_ref, w_ref, vol_ref, sum_ref, w_out_ref, pad_ref):
        own_half(
            flags_ref, w_ref, vol_ref, sum_ref, w_out_ref, pad_ref,
            depth=depth, height=height, block=block,
        )

    def other(flags_ref, w_ref, vol_ref, sum_ref, bias_ref, out_ref, pad_ref):
        other_half(
            flags_ref, w_ref, vol_ref, sum_ref, bias_ref, out_ref, pad_ref,
            depth=depth, height=height,
        )

    partial, w_other = pl.pallas_call(
        own,
        out_shape=(
            jax.ShapeDtypeStruct(sums, f32),
            jax.ShapeDtypeStruct((27 * filters, cin // 2), bf16),
        ),
        in_specs=[smem, vmem, vmem],
        out_specs=(vmem, vmem),
        scratch_shapes=[padded],
        compiler_params=params,
        cost_estimate=pl.CostEstimate(flops=flops, bytes_accessed=2 << 20, transcendentals=0),
    )(flags, weights, mine)
    pooled = pl.pallas_call(
        other,
        out_shape=jax.ShapeDtypeStruct((filters * depth * height // 4, across // 2), bf16),
        in_specs=[smem, vmem, vmem, vmem, vmem],
        out_specs=vmem,
        scratch_shapes=[padded],
        compiler_params=params,
        cost_estimate=pl.CostEstimate(flops=flops, bytes_accessed=2 << 20, transcendentals=0),
    )(flags, w_other, theirs, partial, bias)
    return pooled.reshape(filters, depth // 2, height // 2, across // 2)


def solution(mesh):
    in_specs = (P("filt", "space", None, None), P("filt", None, None, None, None), P("filt"))
    out_specs = P("filt", "space", None, None)
    return jax.shard_map(
        on_device, mesh=mesh, in_specs=in_specs, out_specs=out_specs, check_vma=False
    )
```

time: 82.1 us -> 34.1 us (0.42)
  waiting for transfers between devices: 43.8 us -> 2.01 us
  blocking collectives: 0 us -> 22.8 us
  between operations: 13.5 us -> 0.04 us
  matrix products: 8.33 us -> 0 us
  local copies, waits for them, and re-layouts: 6.42 us -> 1.68 us
  Pallas kernels: 0 us -> 4.29 us
  other arithmetic: 3.57 us -> 0.09 us
  starting transfers between devices: 6.14 us -> 3.01 us
    all_gather x1 -> x0, waiting for transfers between devices: 39.5 us -> none  [on_device(): lax.all_gather(padded, 'filt', axis=0, tiled=True)]
    all_to_all x0 -> x1, blocking collectives: none -> 22.8 us  [on_device(): mine = lax.all_to_all(copies, 'filt', 0, 0, axis_index_groups=same_core)]
    conv_general_dilated x1 -> x0, matrix products: 8.33 us -> none  [convolve(): lax.conv_general_dilated(inputs[None], weights, (1, 1, 1), padding, dimen...]
    pallas_call x0 -> x2, Pallas kernels: none -> 4.29 us  [the longest x1 2.57 us: on_device(): pl.pallas_call(other, out_shape=jax.ShapeDtypeStruct((filters * depth * h...]
    ppermute x2, starting transfers between devices: 6.14 us -> 3.01 us  [the longest x1 3 us: boundary_planes(): lax.ppermute(jnp.where(here == 0, last, first), 'space', [(0, 1), (1, 0)])]
    ppermute x2, waiting for transfers between devices: 4.33 us -> 2.01 us  [the longest x1 1.72 us: boundary_planes(): lax.ppermute(jnp.where(here == 0, last, first), 'space', [(0, 1), (1, 0)])]
    unnamed x5, local copies, waits for them, and re-layouts: 3.63 us -> 1.52 us
    concatenate x1, other arithmetic: 1.55 us -> 0.01 us  [on_device(): planes = jnp.concatenate([volume] + boundary_planes(volume), axis=1)]
  transfers between devices with their start and end apart: 3 -> 2, of which waited for: 3 -> 2; matrix products, arithmetic and copies ran while one was open for 1% -> 0% of each run, Pallas kernels for 0% -> 5%
where the time goes in v1:
time: 34.1 us; the launch traced here: 33.9 us
  blocking collectives  22.8 us (67%)
  Pallas kernels  4.29 us (13%)
  starting transfers between devices  3.01 us (9%)
  waiting for transfers between devices  2.01 us (6%)
  local copies, waits for them, and re-layouts  1.68 us (5%)
    all_to_all x1, blocking collectives, on_device(): mine = lax.all_to_all(copies, 'filt', 0, 0, axis_index_groups=same_core)  22.8 us
    ppermute x1, starting transfers between devices, boundary_planes(): lax.ppermute(jnp.where(here == 0, last, first), 'space', [(0, 1), (1, 0)])  3 us
    pallas_call x1, Pallas kernels, on_device(): pl.pallas_call(other, out_shape=jax.ShapeDtypeStruct((filters * depth * h...  2.57 us
    pallas_call x1, Pallas kernels, on_device(): pl.pallas_call(own, out_shape=(jax.ShapeDtypeStruct(sums, f32), jax.Shape...  1.72 us
    ppermute x1, waiting for transfers between devices, boundary_planes(): lax.ppermute(jnp.where(here == 0, last, first), 'space', [(0, 1), (1, 0)])  1.72 us
    unnamed x5, local copies, waits for them, and re-layouts  1.52 us
  transfers between devices with their start and end apart: 2, of which 2 were waited for; matrix products, arithmetic and copies ran while one was open for 0% of the time, Pallas kernels for 5%

profile of v1, /device:TPU:0, one launch (start us, length us, event | category | flops | bytes accessed | tf_op | source)
XLA Modules:
  0.0 33.9 jit_solution(17879814492212057584)
XLA Ops:
  0.0 0.9 %copy.7 = bf16[16,4,4,128]{3,0,2,1:T(8,128)(2,1)S(1)} copy(bf16[16,4,4,128]{3,2,1,0:T(4,128)(2,1)} %param.3) | data formatting | bytes 131072 | tf_op args[0]
  0.9 3.0 %collective-permute-start = (bf16[16,1,4,128]{3,0,2,1:T(8,128)(2,1)S(1)}, bf16[16,1,4,128]{3,0,2,1:T(8,128)(2,1)S(1)}, u32[]{:S(2)}, u32[]{:S(2)}) collective-permute-start(bf16[16,1,4,128]{3,0,2,1:T(8,128)(2,1)S(1)} %slice_select_fusion), channel_id=1, source_target_pairs={{0,1},{1,0},{2,3},{3,2},{4,5},{5,4},{6,7},{7,6},{8,9},{9,8},{10,11... | collective-permute-start | bytes 49160 | tf_op jit(solution)/shard_map/ppermute | solution.py:19
  3.9 1.7 %collective-permute-done = bf16[16,1,4,128]{3,0,2,1:T(8,128)(2,1)S(1)} collective-permute-done((bf16[16,1,4,128]{3,0,2,1:T(8,128)(2,1)S(1)}, bf16[16,1,4,128]{3,0,2,1:T(8,128)(2,1)S(1)}, u32[]{:S(2)}, u32[]{:S(2)}) %collective-permute-start) | collective-permute-done | bytes 16416 | tf_op jit(solution)/shard_map/ppermute | solution.py:19
  5.6 0.1 broadcast_in_dim.14
  5.7 0.0 copy-start
  5.7 22.8 %all_to_all.5.vol_ref = bf16[8,20,16,128]{3,2,1,0:T(8,128)(2,1)S(1)} all-to-all(bf16[8,20,16,128]{3,2,1,0:T(8,128)(2,1)S(1)} %broadcast_in_dim.14), channel_id=1, replica_groups={{0,4,8,12,16,20,24,28},{2,6,10,14,18,22,26,30},{1,5,9,13,17,21,25,29},{..., dimensions={0} | all-to-all | bytes 1310720 | tf_op jit(solution)/shard_map/all_to_all | solution.py:142
  28.5 0.0 collective-permute-start.1
  28.5 0.1 pad_add_fusion.flags_ref
  28.6 0.0 copy-done
  28.6 1.7 %shard_map.37 = (f32[8,96,256]{2,1,0:T(8,128)S(1)}, bf16[864,128]{1,0:T(8,128)(2,1)S(1)}) custom-call(s32[3]{0:T(128)S(1)} %pad_add_fusion.flags_ref, bf16[864,256]{1,0:T(8,128)(2,1)S(1)} %bitcast.10, bf16[8,20,16,128]{3,2,1,0:T(8,128)(2,1)S(1)} %all_to_all.5.vol_ref), custom_call_target="tpu_custom_call" | custom-call | flops 452984832 | bytes 2097152 | tf_op jit(solution)/shard_map/pallas_call | solution.py:166
  30.3 0.3 collective-permute-done.1.vol_ref
  30.6 0.0 copy-start.1
  30.6 0.7 %copy-done.1 = bf16[32]{0:T(256)(128)(2,1)S(1)} copy-done((bf16[32]{0:T(256)(128)(2,1)S(1)}, bf16[32]{0:T(256)(128)(2,1)}, u32[]{:S(2)}) %copy-start.1) | copy-done | bytes 88
  31.3 0.1 broadcast_in_dim.15.bias_ref
  31.4 2.6 %shard_map.38 = bf16[128,64]{1,0:T(8,128)(2,1)} custom-call(s32[3]{0:T(128)S(1)} %pad_add_fusion.flags_ref, bf16[864,128]{1,0:T(8,128)(2,1)S(1)} %get-tuple-element.7.w_ref, bf16[8,20,16,128]{3,2,1,0:T(8,128)(2,1)S(1)} %collective-permute-done.1.vol_ref, f32[8,96,256]{2,1,0:T(8,128)S(1)} %get-tuple-element.8.sum_ref, f32[32,128]{1,0:T(8,128)S(1)} %broadcast_in_dim.15.bias_ref), custom_call_target="tpu_custom_call" | custom-call | flops 452984832 | bytes 2097152 | tf_op jit(solution)/shard_map/pallas_call | solution.py:178
  (2 shorter events, 0.0 us)
Async XLA Ops:
  0.9 4.7 %collective-permute-start = (bf16[16,1,4,128]{3,0,2,1:T(8,128)(2,1)S(1)}, bf16[16,1,4,128]{3,0,2,1:T(8,128)(2,1)S(1)}, u32[]{:S(2)}, u32[]{:S(2)}) collective-permute-start(bf16[16,1,4,128]{3,0,2,1:T(8,128)(2,1)S(1)} %slice_select_fusion), channel_id=1, source_target_pairs={{0,1},{1,0},{2,3},{3,2},{4,5},{5,4},{6,7},{7,6},{8,9},{9,8},{10,11... | collective-permute-start | bytes 49160 | tf_op jit(solution)/shard_map/ppermute | solution.py:19
  5.7 22.9 %copy-start = (bf16[32,3,3,3,256]{4,0,3,2,1:T(8,128)(2,1)S(1)}, bf16[32,3,3,3,256]{4,0,3,2,1:T(8,128)(2,1)}, u32[]{:S(2)}) copy-start(bf16[32,3,3,3,256]{4,0,3,2,1:T(8,128)(2,1)} %param.4) | copy-start | bytes 1327108
  28.5 2.1 %collective-permute-start.1 = (bf16[8,20,16,128]{3,2,1,0:T(8,128)(2,1)S(1)}, bf16[8,20,16,128]{3,2,1,0:T(8,128)(2,1)S(1)}, u32[]{:S(2)}, u32[]{:S(2)}) collective-permute-start(bf16[8,20,16,128]{3,2,1,0:T(8,128)(2,1)S(1)} %all_to_all.5.vol_ref), channel_id=1, source_target_pairs={{0,2},{2,0},{4,6},{6,4},{8,10},{10,8},{12,14},{14,12},{16,18},{18,... | collective-permute-start | bytes 1966088 | tf_op jit(solution)/shard_map/ppermute | solution.py:143
  30.6 0.7 %copy-start.1 = (bf16[32]{0:T(256)(128)(2,1)S(1)}, bf16[32]{0:T(256)(128)(2,1)}, u32[]{:S(2)}) copy-start(bf16[32]{0:T(256)(128)(2,1)} %param.5) | copy-start | bytes 196

commit v2 on v0

v2 whole, which is shorter than its diff:
```python
import functools

import jax
import jax.numpy as jnp
from jax import lax
from jax.experimental import pallas as pl
from jax.experimental.pallas import tpu as pltpu
from jax.sharding import PartitionSpec as P

slope = 0.3
f32, bf16 = jnp.float32, jnp.bfloat16


def prepare(flags_ref, kernel_ref, bias_ref, w_mine_ref, w_theirs_ref, bias_out_ref, *, block):
    cin = kernel_ref.shape[-1]
    half = cin // 2
    core, group = flags_ref[0], flags_ref[1]
    source = lax.broadcasted_iota(jnp.int32, (cin, cin), 0)
    target = lax.broadcasted_iota(jnp.int32, (cin, cin), 1)
    place = target & (half - 1)
    part = jnp.where(target < half, core, 1 - core)
    wanted = (((place // block) ^ group) * 2 + part) * block + (place & (block - 1))
    shuffle = jnp.where(source == wanted, 1.0, 0.0).astype(bf16)
    ordered = jnp.dot(kernel_ref[...], shuffle, preferred_element_type=f32).astype(bf16)
    w_mine_ref[...] = ordered[:, :half].reshape(w_mine_ref.shape)
    w_theirs_ref[...] = ordered[:, half:].reshape(w_theirs_ref.shape)
    filters = bias_ref.shape[1]
    row = lax.broadcasted_iota(jnp.int32, (filters, filters), 0)
    column = lax.broadcasted_iota(jnp.int32, (filters, filters), 1)
    spread = jnp.where(row == column, bias_ref[...].astype(f32), 0.0)
    bias_out_ref[...] = jnp.broadcast_to(
        jnp.sum(spread, axis=1, keepdims=True), bias_out_ref.shape
    )


def rows_of(ref, row):
    return jnp.concatenate([ref[k, row] for k in range(ref.shape[0])], axis=0)


def pad_rows(rows):
    zero = jnp.zeros_like(rows[0])
    return jnp.concatenate([zero] + rows + [zero], axis=1)


def interior(w_ref, vol_ref, pad_ref, z, y, depth, height):
    across = vol_ref.shape[-1]
    taps = [(a, b) for a in range(3) for b in range(3) if 0 <= z + a - 1 < depth]
    left = jnp.concatenate([w_ref[a * 3 + b] for a, b in taps], axis=1)
    right = jnp.concatenate(
        [pad_ref[z + a - 1, :, (y + b) * across : (y + b + 2) * across] for a, b in taps], axis=0
    )
    return jnp.dot(left, right, preferred_element_type=f32)


def fill_pad(vol_ref, pad_ref, depth, height):
    for z in range(depth):
        pad_ref[z] = pad_rows([rows_of(vol_ref, z * height + y) for y in range(height)])


def boundary(w_ref, vol_ref, plane, tap, y, height):
    across = vol_ref.shape[-1]
    rows = [rows_of(vol_ref, plane * height + k) for k in range(height)]
    padded = pad_rows(rows)
    left = jnp.concatenate([w_ref[tap * 3 + b] for b in range(3)], axis=1)
    right = jnp.concatenate(
        [padded[:, (y + b) * across : (y + b + 2) * across] for b in range(3)], axis=0
    )
    return jnp.dot(left, right, preferred_element_type=f32)


def combine(total, k, filters, across):
    part = total[:, k * across : (k + 1) * across]
    lane = lax.broadcasted_iota(jnp.int32, (filters, across), 1)
    left = pltpu.roll(part[:filters], 1, 1)
    right = pltpu.roll(part[2 * filters :], across - 1, 1)
    v = part[filters : 2 * filters]
    v += jnp.where(lane > 0, left, 0.0)
    return v + jnp.where(lane < across - 1, right, 0.0)


def edges_of(flags_ref, count, depth):
    if count == 2:
        up = flags_ref[2] == 0
        return [(jnp.where(up, depth - 1, 0), jnp.where(up, 0, 2))]
    return [(depth - 1, 0), (0, 2)]


def first_half(
    flags_ref, w_ref, vol_ref, sum_ref, edge_ref, pad_ref, *, depth, height, count
):
    fill_pad(vol_ref, pad_ref, depth, height)
    pairs = height // 2
    for k, (plane, tap) in enumerate(edges_of(flags_ref, count, depth)):
        for y in range(pairs):
            edge_ref[k * pairs + y] = boundary(w_ref, vol_ref, plane, tap, 2 * y, height)
    for z in range(depth):
        for y in range(pairs):
            sum_ref[z * pairs + y] = interior(w_ref, vol_ref, pad_ref, z, 2 * y, depth, height)


def send_edges(flags_ref, w_ref, vol_ref, edge_ref, out_ref, *, depth, height, count):
    across = vol_ref.shape[-1]
    filters = out_ref.shape[2]
    pairs = height // 2
    for k, (plane, tap) in enumerate(edges_of(flags_ref, count, depth)):
        for y in range(pairs):
            total = boundary(w_ref, vol_ref, plane, tap, 2 * y, height)
            total += edge_ref[k * pairs + y]
            for j in range(2):
                out_ref[k, 2 * y + j] = combine(total, j, filters, across)


def second_half(w_ref, vol_ref, sum_ref, bias_ref, out_ref, pad_ref, *, depth, height):
    across = vol_ref.shape[-1]
    filters = bias_ref.shape[0]
    pairs = height // 2
    fill_pad(vol_ref, pad_ref, depth, height)
    for z in range(depth):
        for y in range(pairs):
            total = interior(w_ref, vol_ref, pad_ref, z, 2 * y, depth, height)
            total += sum_ref[z * pairs + y]
            for j in range(2):
                v = combine(total, j, filters, across) + bias_ref[...]
                out_ref[z * height + 2 * y + j] = v


def finish(flags_ref, v_ref, *refs, depth, height, count):
    got_refs, out_ref = refs[:-1], refs[-1]
    filters, across = v_ref.shape[1:]
    pooled = {}
    for z in range(depth):
        for y in range(height):
            v = v_ref[z * height + y]
            if z == 0:
                beside = got_refs[0][0, y]
                v += jnp.where(flags_ref[2] > 0, beside, 0.0)
            if z == depth - 1:
                beside = got_refs[-1][0, y]
                v += jnp.where(flags_ref[3] > 0, beside, 0.0)
            v = jnp.where(v > 0, v, slope * v)
            key = (z // 2, y // 2)
            pooled[key] = v if key not in pooled else jnp.maximum(pooled[key], v)
    stacked = jnp.concatenate(
        [pooled[z, y] for z in range(depth // 2) for y in range(height // 2)], axis=0
    )
    stacked = jnp.maximum(stacked, pltpu.roll(stacked, across - 1, 1)).astype(bf16)
    cells = (depth // 2) * (height // 2)
    size = cells * filters
    target = lax.broadcasted_iota(jnp.int32, (size, size), 0)
    source = lax.broadcasted_iota(jnp.int32, (size, size), 1)
    wanted = (target & (cells - 1)) * filters + target // cells
    rows_pick = jnp.where(source == wanted, 1.0, 0.0).astype(bf16)
    lane_from = lax.broadcasted_iota(jnp.int32, (across, across // 2), 0)
    lane_to = lax.broadcasted_iota(jnp.int32, (across, across // 2), 1)
    lanes_pick = jnp.where(lane_from == 2 * lane_to, 1.0, 0.0).astype(bf16)
    picked = jnp.dot(stacked, lanes_pick, preferred_element_type=f32).astype(bf16)
    out_ref[...] = jnp.dot(rows_pick, picked, preferred_element_type=f32).astype(bf16)


def gather(block, size):
    def swapped(x, r):
        pairs = [(i, i ^ (2 * r)) for i in range(size)]
        return lax.ppermute(x, "filt", pairs)

    far = size // 4
    held = {0: block}
    held[far] = swapped(block, far)
    for r in range(1, far):
        held[r] = swapped(block, r)
    for r in range(1, far):
        held[far ^ r] = swapped(held[far], r)
    return jnp.stack([held[r] for r in range(size // 2)])


def on_device(volume, kernel, filter_bias):
    block, depth, height, across = volume.shape
    filters, cin = kernel.shape[0], kernel.shape[-1]
    size = lax.axis_size("filt")
    count = lax.axis_size("space")
    here = lax.axis_index("space")
    place = lax.axis_index("filt")
    flags = jnp.stack([place & 1, place >> 1, here, count - 1 - here]).astype(jnp.int32)

    vmem = pl.BlockSpec(memory_space=pltpu.VMEM)
    smem = pl.BlockSpec(memory_space=pltpu.SMEM)
    shape = jax.ShapeDtypeStruct
    macs = 27 * filters * cin * depth * height * across
    padded = pltpu.VMEM((depth, cin // 2, (height + 2) * across), bf16)
    pairs = height // 2
    edges = 1 if count == 2 else 2

    def call(body, outs, ins, args, cost, scratch=()):
        return pl.pallas_call(
            body,
            out_shape=outs,
            in_specs=ins,
            out_specs=jax.tree.map(lambda _: vmem, outs),
            scratch_shapes=scratch,
            compiler_params=pltpu.CompilerParams(vmem_limit_bytes=16 << 20),
            cost_estimate=pl.CostEstimate(
                flops=int(cost * macs), bytes_accessed=1 << 20, transcendentals=0
            ),
        )(*args)

    blocks = volume.transpose(1, 2, 0, 3).reshape(depth * height, block, across)
    mine = gather(blocks, size)
    theirs = lax.ppermute(mine, "filt", [(i, i ^ 1) for i in range(size)])

    ordered = shape((9, 3 * filters, cin // 2), bf16)
    w_mine, w_theirs, bias = call(
        functools.partial(prepare, block=block),
        (ordered, ordered, shape((filters, across), f32)),
        [smem, vmem, vmem],
        (flags, kernel.transpose(1, 2, 3, 0, 4).reshape(-1, cin), filter_bias[None]),
        0.2,
    )
    dims = dict(depth=depth, height=height)
    partial, edge = call(
        functools.partial(first_half, count=count, **dims),
        (
            shape((depth * pairs, 3 * filters, 2 * across), f32),
            shape((edges * pairs, 3 * filters, 2 * across), f32),
        ),
        [smem, vmem, vmem],
        (flags, w_mine, mine),
        1.0,
        [padded],
    )
    sums = call(
        functools.partial(send_edges, count=count, **dims),
        shape((edges, height, filters, across), f32),
        [smem, vmem, vmem, vmem],
        (flags, w_theirs, theirs, edge),
        0.2,
    )
    if count == 2:
        got = [lax.ppermute(sums, "space", [(0, 1), (1, 0)])]
    else:
        up = [(i, i + 1) for i in range(count - 1)]
        down = [(t, s) for s, t in up]
        got = [lax.ppermute(sums[:1], "space", up), lax.ppermute(sums[1:], "space", down)]
    v = call(
        functools.partial(second_half, **dims),
        shape((depth * height, filters, across), f32),
        [vmem, vmem, vmem, vmem],
        (w_theirs, theirs, partial, bias),
        1.0,
        [padded],
    )
    pooled = call(
        functools.partial(finish, count=count, **dims),
        shape((filters * depth * height // 4, across // 2), bf16),
        [smem, vmem] + [vmem] * len(got),
        (flags, v, *got),
        0.2,
    )
    return pooled.reshape(filters, depth // 2, height // 2, across // 2)


def solution(mesh):
    in_specs = (P("filt", "space", None, None), P("filt", None, None, None, None), P("filt"))
    out_specs = P("filt", "space", None, None)
    return jax.shard_map(
        on_device, mesh=mesh, in_specs=in_specs, out_specs=out_specs, check_vma=False
    )
```

time: 82.1 us -> 29.8 us (0.36)
  waiting for transfers between devices: 43.8 us -> 9.23 us
  between operations: 13.5 us -> 0.09 us
  matrix products: 8.33 us -> 0 us
  starting transfers between devices: 6.14 us -> 13.2 us
  Pallas kernels: 0 us -> 5.45 us
  local copies, waits for them, and re-layouts: 6.42 us -> 1.61 us
  other arithmetic: 3.57 us -> 0.08 us
    all_gather x1 -> x0, waiting for transfers between devices: 39.5 us -> none  [on_device(): lax.all_gather(padded, 'filt', axis=0, tiled=True)]
    conv_general_dilated x1 -> x0, matrix products: 8.33 us -> none  [convolve(): lax.conv_general_dilated(inputs[None], weights, (1, 1, 1), padding, dimen...]
    ppermute x2 -> x9, starting transfers between devices: 6.14 us -> 13.2 us  [the longest x7 11.6 us: swapped(): return lax.ppermute(x, 'filt', pairs)]
    pallas_call x0 -> x5, Pallas kernels: none -> 5.45 us  [call(): pl.pallas_call(body, out_shape=outs, in_specs=ins, out_specs=jax.tree.map...]
    ppermute x2 -> x9, waiting for transfers between devices: 4.33 us -> 9.23 us  [the longest x7 7.09 us: swapped(): return lax.ppermute(x, 'filt', pairs)]
    unnamed x5 -> x11, local copies, waits for them, and re-layouts: 3.63 us -> 0.74 us
    concatenate x1 -> x0, other arithmetic: 1.55 us -> none  [with_halo(): block = jnp.concatenate([low, block, high], axis=dim)]
    reduce_max x1 -> x0, other arithmetic: 1.36 us -> none  [finish(): return jnp.max(blocked, axis=(2, 4, 6)).astype(jnp.bfloat16)]
  transfers between devices with their start and end apart: 3 -> 9, of which waited for: 3 -> 5; matrix products, arithmetic and copies ran while one was open for 1% -> 1% of each run, Pallas kernels for 0% -> 10%
where the time goes in v2:
time: 29.8 us; the launch traced here: 29.7 us
  starting transfers between devices  13.2 us (44%)
  waiting for transfers between devices  9.23 us (31%)
  Pallas kernels  5.45 us (18%)
  local copies, waits for them, and re-layouts  1.61 us (5%)
    ppermute x7, starting transfers between devices, swapped(): return lax.ppermute(x, 'filt', pairs)  11.6 us
    ppermute x7, waiting for transfers between devices, swapped(): return lax.ppermute(x, 'filt', pairs)  7.09 us
    pallas_call x5, Pallas kernels, call(): pl.pallas_call(body, out_shape=outs, in_specs=ins, out_specs=jax.tree.map...  5.45 us
    ppermute x1, waiting for transfers between devices, on_device(): got = [lax.ppermute(sums, 'space', [(0, 1), (1, 0)])]  2.13 us
    ppermute x1, starting transfers between devices, on_device(): got = [lax.ppermute(sums, 'space', [(0, 1), (1, 0)])]  1.55 us
    transpose x1, local copies, waits for them, and re-layouts, on_device(): blocks = volume.transpose(1, 2, 0, 3).reshape(depth * height, block, across)  0.86 us
    unnamed x11, local copies, waits for them, and re-layouts  0.74 us
  transfers between devices with their start and end apart: 9, of which 5 were waited for; matrix products, arithmetic and copies ran while one was open for 1% of the time, Pallas kernels for 10%

profile of v2, /device:TPU:0, one launch (start us, length us, event | category | flops | bytes accessed | tf_op | source)
XLA Modules:
  0.0 29.7 jit_solution(2158181395511457109)
XLA Ops:
  0.0 0.9 %copy.4 = bf16[4,4,16,128]{3,2,1,0:T(8,128)(2,1)S(1)} copy(bf16[4,4,16,128]{3,1,0,2:T(4,128)(2,1)} %bitcast.35) | data formatting | bytes 131072 | tf_op jit(solution)/shard_map/transpose | solution.py:205
  0.9 3.0 %collective-permute-start = (bf16[16,16,128]{2,1,0:T(8,128)(2,1)S(1)}, bf16[16,16,128]{2,1,0:T(8,128)(2,1)S(1)}, u32[]{:S(2)}, u32[]{:S(2)}) collective-permute-start(bf16[16,16,128]{2,1,0:T(8,128)(2,1)S(1)} %bitcast.30), channel_id=1, source_target_pairs={{0,4},{2,6},{4,0},{6,2},{8,12},{10,14},{12,8},{14,10},{16,20},{18,... | collective-permute-start | bytes 196616 | tf_op jit(solution)/shard_map/ppermute | solution.py:163
  3.9 1.6 %collective-permute-start.1 = (bf16[16,16,128]{2,1,0:T(8,128)(2,1)S(1)}, bf16[16,16,128]{2,1,0:T(8,128)(2,1)S(1)}, u32[]{:S(2)}, u32[]{:S(2)}) collective-permute-start(bf16[16,16,128]{2,1,0:T(8,128)(2,1)S(1)} %bitcast.31), channel_id=1, source_target_pairs={{0,8},{2,10},{4,12},{6,14},{8,0},{10,2},{12,4},{14,6},{16,24},{18,... | collective-permute-start | bytes 196616 | tf_op jit(solution)/shard_map/ppermute | solution.py:163
  5.5 3.0 %collective-permute-start.3 = (bf16[16,16,128]{2,1,0:T(8,128)(2,1)S(1)}, bf16[16,16,128]{2,1,0:T(8,128)(2,1)S(1)}, u32[]{:S(2)}, u32[]{:S(2)}) collective-permute-start(bf16[16,16,128]{2,1,0:T(8,128)(2,1)S(1)} %bitcast.33), channel_id=1, source_target_pairs={{0,16},{2,18},{4,20},{6,22},{8,24},{10,26},{12,28},{14,30},{16,0},... | collective-permute-start | bytes 196616 | tf_op jit(solution)/shard_map/ppermute | solution.py:163
  8.5 2.4 %collective-permute-done.3 = bf16[16,16,128]{2,1,0:T(8,128)(2,1)S(1)} collective-permute-done((bf16[16,16,128]{2,1,0:T(8,128)(2,1)S(1)}, bf16[16,16,128]{2,1,0:T(8,128)(2,1)S(1)}, u32[]{:S(2)}, u32[]{:S(2)}) %collective-permute-start.3) | collective-permute-done | bytes 65568 | tf_op jit(solution)/shard_map/ppermute | solution.py:163
  10.9 2.1 %collective-permute-start.4 = (bf16[16,16,128]{2,1,0:T(8,128)(2,1)S(1)}, bf16[16,16,128]{2,1,0:T(8,128)(2,1)S(1)}, u32[]{:S(2)}, u32[]{:S(2)}) collective-permute-start(bf16[16,16,128]{2,1,0:T(8,128)(2,1)S(1)} %collective-permute-done.3), channel_id=1, source_target_pairs={{0,4},{2,6},{4,0},{6,2},{8,12},{10,14},{12,8},{14,10},{16,20},{18,... | collective-permute-start | bytes 196616 | tf_op jit(solution)/shard_map/ppermute | solution.py:163
  12.9 1.6 %collective-permute-start.5 = (bf16[16,16,128]{2,1,0:T(8,128)(2,1)S(1)}, bf16[16,16,128]{2,1,0:T(8,128)(2,1)S(1)}, u32[]{:S(2)}, u32[]{:S(2)}) collective-permute-start(bf16[16,16,128]{2,1,0:T(8,128)(2,1)S(1)} %collective-permute-done.3), channel_id=1, source_target_pairs={{0,8},{2,10},{4,12},{6,14},{8,0},{10,2},{12,4},{14,6},{16,24},{18,... | collective-permute-start | bytes 196616 | tf_op jit(solution)/shard_map/ppermute | solution.py:163
  14.5 0.0 collective-permute-done
  14.5 0.4 %collective-permute-start.6 = (bf16[16,16,128]{2,1,0:T(8,128)(2,1)S(1)}, bf16[16,16,128]{2,1,0:T(8,128)(2,1)S(1)}, u32[]{:S(2)}, u32[]{:S(2)}) collective-permute-start(bf16[16,16,128]{2,1,0:T(8,128)(2,1)S(1)} %collective-permute-done.3), channel_id=1, source_target_pairs={{0,12},{2,14},{4,8},{6,10},{8,4},{10,6},{12,0},{14,2},{16,28},{18,... | collective-permute-start | bytes 196616 | tf_op jit(solution)/shard_map/ppermute | solution.py:163
  14.9 0.0 collective-permute-done.1
  14.9 0.0 collective-permute-done.2
  14.9 0.2 collective-permute-done.4
  15.2 2.0 %collective-permute-done.5 = bf16[16,16,128]{2,1,0:T(8,128)(2,1)S(1)} collective-permute-done((bf16[16,16,128]{2,1,0:T(8,128)(2,1)S(1)}, bf16[16,16,128]{2,1,0:T(8,128)(2,1)S(1)}, u32[]{:S(2)}, u32[]{:S(2)}) %collective-permute-start.5) | collective-permute-done | bytes 65568 | tf_op jit(solution)/shard_map/ppermute | solution.py:163
  17.2 2.4 %collective-permute-done.6 = bf16[16,16,128]{2,1,0:T(8,128)(2,1)S(1)} collective-permute-done((bf16[16,16,128]{2,1,0:T(8,128)(2,1)S(1)}, bf16[16,16,128]{2,1,0:T(8,128)(2,1)S(1)}, u32[]{:S(2)}, u32[]{:S(2)}) %collective-permute-start.6) | collective-permute-done | bytes 65568 | tf_op jit(solution)/shard_map/ppermute | solution.py:163
  19.7 0.1 collective-permute-start.7
  19.8 0.1 pad_add_fusion.flags_ref
  19.8 0.7 %copy-done.1 = bf16[32]{0:T(256)(128)(2,1)S(1)} copy-done((bf16[32]{0:T(256)(128)(2,1)S(1)}, bf16[32]{0:T(256)(128)(2,1)}, u32[]{:S(2)}) %copy-start.1) | copy-done | bytes 88
  20.5 0.8 %shard_map.37 = (bf16[9,96,128]{2,1,0:T(8,128)(2,1)S(1)}, bf16[9,96,128]{2,1,0:T(8,128)(2,1)S(1)}, f32[32,128]{1,0:T(8,128)S(1)}) custom-call(s32[4]{0:T(128)S(1)} %pad_add_fusion.flags_ref, bf16[864,256]{1,0:T(8,128)(2,1)S(1)} %bitcast.28, bf16[1,32]{1,0:T(2,128)(2,1)S(1)} %bitcast.29), custom_call_target="tpu_custom_call" | custom-call | flops 90596968 | bytes 1048576 | tf_op jit(solution)/shard_map/pallas_call | solution.py:193
  21.3 1.4 %shard_map.38 = (f32[8,96,256]{2,1,0:T(8,128)S(1)}, f32[2,96,256]{2,1,0:T(8,128)S(1)}) custom-call(s32[4]{0:T(128)S(1)} %pad_add_fusion.flags_ref, bf16[9,96,128]{2,1,0:T(8,128)(2,1)S(1)} %get-tuple-element.11.w_ref, bf16[8,16,16,128]{3,2,1,0:T(8,128)(2,1)S(1)} %bitcast_dynamic-update-slice_fusion.vol_ref), custom_call_target="tpu_custom_call" | custom-call | flops 452984832 | bytes 1048576 | tf_op jit(solution)/shard_map/pallas_call | solution.py:193
  22.7 0.8 %shard_map.40 = f32[1,4,32,128]{3,2,1,0:T(8,128)S(1)} custom-call(s32[4]{0:T(128)S(1)} %pad_add_fusion.flags_ref, bf16[9,96,128]{2,1,0:T(8,128)(2,1)S(1)} %get-tuple-element.10.w_ref, bf16[8,16,16,128]{3,2,1,0:T(8,128)(2,1)S(1)} %collective-permute-done.7.vol_ref, f32[2,96,256]{2,1,0:T(8,128)S(1)} %get-tuple-element.14.edge_ref), custom_call_target="tpu_custom_call" | custom-call | flops 90596968 | bytes 1048576 | tf_op jit(solution)/shard_map/pallas_call | solution.py:193
  23.6 1.6 %collective-permute-start.8 = (f32[1,4,32,128]{3,2,1,0:T(8,128)S(1)}, f32[1,4,32,128]{3,2,1,0:T(8,128)S(1)}, u32[]{:S(2)}, u32[]{:S(2)}) collective-permute-start(f32[1,4,32,128]{3,2,1,0:T(8,128)S(1)} %shard_map.40), channel_id=1, source_target_pairs={{0,1},{1,0},{2,3},{3,2},{4,5},{5,4},{6,7},{7,6},{8,9},{9,8},{10,11... | collective-permute-start | bytes 196616 | tf_op jit(solution)/shard_map/ppermute | solution.py:237
  25.1 0.9 %shard_map.39.v_ref = f32[16,32,128]{2,1,0:T(8,128)S(1)} custom-call(bf16[9,96,128]{2,1,0:T(8,128)(2,1)S(1)} %get-tuple-element.10.w_ref, bf16[8,16,16,128]{3,2,1,0:T(8,128)(2,1)S(1)} %collective-permute-done.7.vol_ref, f32[8,96,256]{2,1,0:T(8,128)S(1)} %get-tuple-element.12.sum_ref, f32[32,128]{1,0:T(8,128)S(1)} %get-tuple-element.13.bias_ref), custom_call_target="tpu_custom_call" | custom-call | flops 452984832 | bytes 1048576 | tf_op jit(solution)/shard_map/pallas_call | solution.py:193
  26.0 2.1 %collective-permute-done.8.refs_0_ = f32[1,4,32,128]{3,2,1,0:T(8,128)S(1)} collective-permute-done((f32[1,4,32,128]{3,2,1,0:T(8,128)S(1)}, f32[1,4,32,128]{3,2,1,0:T(8,128)S(1)}, u32[]{:S(2)}, u32[]{:S(2)}) %collective-permute-start.8) | collective-permute-done | bytes 65568 | tf_op jit(solution)/shard_map/ppermute | solution.py:237
  28.1 1.5 %shard_map.41 = bf16[128,64]{1,0:T(8,128)(2,1)} custom-call(s32[4]{0:T(128)S(1)} %pad_add_fusion.flags_ref, f32[16,32,128]{2,1,0:T(8,128)S(1)} %shard_map.39.v_ref, f32[1,4,32,128]{3,2,1,0:T(8,128)S(1)} %collective-permute-done.8.refs_0_), custom_call_target="tpu_custom_call" | custom-call | flops 90596968 | bytes 1048576 | tf_op jit(solution)/shard_map/pallas_call | solution.py:193
  (13 shorter events, 0.1 us)
Async XLA Ops:
  0.9 13.6 %collective-permute-start = (bf16[16,16,128]{2,1,0:T(8,128)(2,1)S(1)}, bf16[16,16,128]{2,1,0:T(8,128)(2,1)S(1)}, u32[]{:S(2)}, u32[]{:S(2)}) collective-permute-start(bf16[16,16,128]{2,1,0:T(8,128)(2,1)S(1)} %bitcast.30), channel_id=1, source_target_pairs={{0,4},{2,6},{4,0},{6,2},{8,12},{10,14},{12,8},{14,10},{16,20},{18,... | collective-permute-start | bytes 196616 | tf_op jit(solution)/shard_map/ppermute | solution.py:163
  3.9 11.0 %collective-permute-start.1 = (bf16[16,16,128]{2,1,0:T(8,128)(2,1)S(1)}, bf16[16,16,128]{2,1,0:T(8,128)(2,1)S(1)}, u32[]{:S(2)}, u32[]{:S(2)}) collective-permute-start(bf16[16,16,128]{2,1,0:T(8,128)(2,1)S(1)} %bitcast.31), channel_id=1, source_target_pairs={{0,8},{2,10},{4,12},{6,14},{8,0},{10,2},{12,4},{14,6},{16,24},{18,... | collective-permute-start | bytes 196616 | tf_op jit(solution)/shard_map/ppermute | solution.py:163
  5.5 9.4 %collective-permute-start.2 = (bf16[16,16,128]{2,1,0:T(8,128)(2,1)S(1)}, bf16[16,16,128]{2,1,0:T(8,128)(2,1)S(1)}, u32[]{:S(2)}, u32[]{:S(2)}) collective-permute-start(bf16[16,16,128]{2,1,0:T(8,128)(2,1)S(1)} %bitcast.32), channel_id=1, source_target_pairs={{0,12},{2,14},{4,8},{6,10},{8,4},{10,6},{12,0},{14,2},{16,28},{18,... | collective-permute-start | bytes 196616 | tf_op jit(solution)/shard_map/ppermute | solution.py:163
  5.5 5.4 %collective-permute-start.3 = (bf16[16,16,128]{2,1,0:T(8,128)(2,1)S(1)}, bf16[16,16,128]{2,1,0:T(8,128)(2,1)S(1)}, u32[]{:S(2)}, u32[]{:S(2)}) collective-permute-start(bf16[16,16,128]{2,1,0:T(8,128)(2,1)S(1)} %bitcast.33), channel_id=1, source_target_pairs={{0,16},{2,18},{4,20},{6,22},{8,24},{10,26},{12,28},{14,30},{16,0},... | collective-permute-start | bytes 196616 | tf_op jit(solution)/shard_map/ppermute | solution.py:163
  8.5 11.4 %copy-start = (bf16[32,3,3,3,256]{4,0,3,2,1:T(8,128)(2,1)S(1)}, bf16[32,3,3,3,256]{4,0,3,2,1:T(8,128)(2,1)}, u32[]{:S(2)}) copy-start(bf16[32,3,3,3,256]{4,0,3,2,1:T(8,128)(2,1)} %param.4) | copy-start | bytes 1327108
  10.9 4.3 %collective-permute-start.4 = (bf16[16,16,128]{2,1,0:T(8,128)(2,1)S(1)}, bf16[16,16,128]{2,1,0:T(8,128)(2,1)S(1)}, u32[]{:S(2)}, u32[]{:S(2)}) collective-permute-start(bf16[16,16,128]{2,1,0:T(8,128)(2,1)S(1)} %collective-permute-done.3), channel_id=1, source_target_pairs={{0,4},{2,6},{4,0},{6,2},{8,12},{10,14},{12,8},{14,10},{16,20},{18,... | collective-permute-start | bytes 196616 | tf_op jit(solution)/shard_map/ppermute | solution.py:163
  12.9 4.3 %collective-permute-start.5 = (bf16[16,16,128]{2,1,0:T(8,128)(2,1)S(1)}, bf16[16,16,128]{2,1,0:T(8,128)(2,1)S(1)}, u32[]{:S(2)}, u32[]{:S(2)}) collective-permute-start(bf16[16,16,128]{2,1,0:T(8,128)(2,1)S(1)} %collective-permute-done.3), channel_id=1, source_target_pairs={{0,8},{2,10},{4,12},{6,14},{8,0},{10,2},{12,4},{14,6},{16,24},{18,... | collective-permute-start | bytes 196616 | tf_op jit(solution)/shard_map/ppermute | solution.py:163
  14.5 5.2 %collective-permute-start.6 = (bf16[16,16,128]{2,1,0:T(8,128)(2,1)S(1)}, bf16[16,16,128]{2,1,0:T(8,128)(2,1)S(1)}, u32[]{:S(2)}, u32[]{:S(2)}) collective-permute-start(bf16[16,16,128]{2,1,0:T(8,128)(2,1)S(1)} %collective-permute-done.3), channel_id=1, source_target_pairs={{0,12},{2,14},{4,8},{6,10},{8,4},{10,6},{12,0},{14,2},{16,28},{18,... | collective-permute-start | bytes 196616 | tf_op jit(solution)/shard_map/ppermute | solution.py:163
  19.7 3.1 %collective-permute-start.7 = (bf16[8,16,16,128]{3,2,1,0:T(8,128)(2,1)S(1)}, bf16[8,16,16,128]{3,2,1,0:T(8,128)(2,1)S(1)}, u32[]{:S(2)}, u32[]{:S(2)}) collective-permute-start(bf16[8,16,16,128]{3,2,1,0:T(8,128)(2,1)S(1)} %bitcast_dynamic-update-slice_fusion.vol_ref), channel_id=1, source_target_pairs={{0,2},{2,0},{4,6},{6,4},{8,10},{10,8},{12,14},{14,12},{16,18},{18,... | collective-permute-start | bytes 1572872 | tf_op jit(solution)/shard_map/ppermute | solution.py:207
  19.8 0.7 %copy-start.1 = (bf16[32]{0:T(256)(128)(2,1)S(1)}, bf16[32]{0:T(256)(128)(2,1)}, u32[]{:S(2)}) copy-start(bf16[32]{0:T(256)(128)(2,1)} %param.5) | copy-start | bytes 196
  23.6 4.6 %collective-permute-start.8 = (f32[1,4,32,128]{3,2,1,0:T(8,128)S(1)}, f32[1,4,32,128]{3,2,1,0:T(8,128)S(1)}, u32[]{:S(2)}, u32[]{:S(2)}) collective-permute-start(f32[1,4,32,128]{3,2,1,0:T(8,128)S(1)} %shard_map.40), channel_id=1, source_target_pairs={{0,1},{1,0},{2,3},{3,2},{4,5},{5,4},{6,7},{7,6},{8,9},{9,8},{10,11... | collective-permute-start | bytes 196616 | tf_op jit(solution)/shard_map/ppermute | solution.py:237

commit v3 on v2

v3 whole, which is shorter than its diff:
```python
import functools

import jax
import jax.numpy as jnp
from jax import lax
from jax.experimental import pallas as pl
from jax.experimental.pallas import tpu as pltpu
from jax.sharding import PartitionSpec as P

slope = 0.3
f32, bf16 = jnp.float32, jnp.bfloat16


def one_hot(shape, wanted):
    target = lax.broadcasted_iota(jnp.int32, shape, 0)
    source = lax.broadcasted_iota(jnp.int32, shape, 1)
    return jnp.where(source == wanted(target), 1.0, 0.0).astype(bf16)


def begin(flags_ref, vol_ref, own_ref, *plane_refs, count):
    depth = vol_ref.shape[1]
    own_ref[...] = vol_ref[...]
    if count == 2:
        plane_refs[0][...] = vol_ref[:, pl.ds(jnp.where(flags_ref[2] == 0, depth - 1, 0), 1)]
    else:
        plane_refs[0][...] = vol_ref[:, depth - 1 : depth]
        plane_refs[1][...] = vol_ref[:, 0:1]


def prepare(flags_ref, kernel_ref, bias_ref, w_mine_ref, w_theirs_ref, bias_out_ref, *, block):
    cin = kernel_ref.shape[-1]
    half = cin // 2
    far = half // block // 2
    core, group = flags_ref[0], flags_ref[1]
    source = lax.broadcasted_iota(jnp.int32, (cin, cin), 0)
    target = lax.broadcasted_iota(jnp.int32, (cin, cin), 1)
    place = target & (half - 1)
    part = jnp.where(target < half, core, 1 - core)
    slot = place // block
    relative = (slot >> 1) | ((slot & 1) * far)
    wanted = ((relative ^ group) * 2 + part) * block + (place & (block - 1))
    shuffle = jnp.where(source == wanted, 1.0, 0.0).astype(bf16)
    ordered = jnp.dot(kernel_ref[...], shuffle, preferred_element_type=f32).astype(bf16)
    w_mine_ref[...] = ordered[:, :half].reshape(w_mine_ref.shape)
    w_theirs_ref[...] = ordered[:, half:].reshape(w_theirs_ref.shape)
    filters = bias_ref.shape[1]
    row = lax.broadcasted_iota(jnp.int32, (filters, filters), 0)
    column = lax.broadcasted_iota(jnp.int32, (filters, filters), 1)
    spread = jnp.where(row == column, bias_ref[...].astype(f32), 0.0)
    bias_out_ref[...] = jnp.broadcast_to(
        jnp.sum(spread, axis=1, keepdims=True), bias_out_ref.shape
    )


def assemble(*refs, block, per_block):
    in_refs, out_ref = refs[:-2], refs[-1]
    parts = len(in_refs) // 2
    across = out_ref.shape[1]
    at = 0
    for k in range(parts):
        own, far = in_refs[k], in_refs[parts + k]
        rows = own.shape[0]
        cells = rows // block
        pick = one_hot((rows, rows), lambda t: (t & (block - 1)) * cells + t // block)
        both = jnp.concatenate([own[...], far[...]], axis=1)
        moved = jnp.dot(pick, both, preferred_element_type=f32).astype(bf16)
        out_ref[at : at + rows] = moved[:, :across]
        out_ref[per_block + at : per_block + at + rows] = moved[:, across:]
        at += rows


def rows_of(ref, row):
    return jnp.concatenate([ref[k, row] for k in range(ref.shape[0])], axis=0)


def fill_pad(flags_ref, vol_ref, pad_ref, depth, height):
    extra = vol_ref.shape[1] // height - depth
    for plane in range(depth + 2):
        if 1 <= plane <= depth:
            rows = [rows_of(vol_ref, (plane - 1) * height + y) for y in range(height)]
        else:
            which = 0 if plane == 0 or extra == 1 else 1
            rows = [rows_of(vol_ref, (depth + which) * height + y) for y in range(height)]
            keep = flags_ref[2 if plane == 0 else 3] > 0
            rows = [jnp.where(keep, r, jnp.zeros_like(r)) for r in rows]
        zero = jnp.zeros_like(rows[0])
        pad_ref[plane] = jnp.concatenate([zero] + rows + [zero], axis=1)


def product(w_ref, pad_ref, z, y, across):
    taps = [(a, b) for a in range(3) for b in range(3)]
    left = jnp.concatenate([w_ref[a * 3 + b] for a, b in taps], axis=1)
    right = jnp.concatenate(
        [pad_ref[z + a, :, (y + b) * across : (y + b + 2) * across] for a, b in taps], axis=0
    )
    return jnp.dot(left, right, preferred_element_type=f32)


def combine(total, k, filters, across):
    part = total[:, k * across : (k + 1) * across]
    lane = lax.broadcasted_iota(jnp.int32, (filters, across), 1)
    left = pltpu.roll(part[:filters], 1, 1)
    right = pltpu.roll(part[2 * filters :], across - 1, 1)
    v = part[filters : 2 * filters]
    v += jnp.where(lane > 0, left, 0.0)
    return v + jnp.where(lane < across - 1, right, 0.0)


def first_half(flags_ref, w_ref, vol_ref, sum_ref, pad_ref, *, depth, height):
    across = vol_ref.shape[-1]
    pairs = height // 2
    fill_pad(flags_ref, vol_ref, pad_ref, depth, height)
    for z in range(depth):
        for y in range(pairs):
            sum_ref[z * pairs + y] = product(w_ref, pad_ref, z, 2 * y, across)


def second_half(
    flags_ref, w_ref, vol_ref, sum_ref, bias_ref, out_ref, pad_ref, *, depth, height
):
    across = vol_ref.shape[-1]
    filters = bias_ref.shape[0]
    pairs = height // 2
    fill_pad(flags_ref, vol_ref, pad_ref, depth, height)
    pooled = {}
    for z in range(depth):
        for y in range(pairs):
            total = product(w_ref, pad_ref, z, 2 * y, across) + sum_ref[z * pairs + y]
            for j in range(2):
                v = combine(total, j, filters, across) + bias_ref[...]
                v = jnp.where(v > 0, v, slope * v)
                key = (z // 2, y)
                pooled[key] = v if key not in pooled else jnp.maximum(pooled[key], v)
    stacked = jnp.concatenate(
        [pooled[z, y] for z in range(depth // 2) for y in range(pairs)], axis=0
    )
    stacked = jnp.maximum(stacked, pltpu.roll(stacked, across - 1, 1)).astype(bf16)
    cells = (depth // 2) * pairs
    size = cells * filters
    rows_pick = one_hot((size, size), lambda t: (t & (cells - 1)) * filters + t // cells)
    lane_from = lax.broadcasted_iota(jnp.int32, (across, across // 2), 0)
    lane_to = lax.broadcasted_iota(jnp.int32, (across, across // 2), 1)
    lanes_pick = jnp.where(lane_from == 2 * lane_to, 1.0, 0.0).astype(bf16)
    picked = jnp.dot(stacked, lanes_pick, preferred_element_type=f32).astype(bf16)
    out_ref[...] = jnp.dot(rows_pick, picked, preferred_element_type=f32).astype(bf16)


def shifted(x, relative, step, size, count):
    pairs = []
    for f in range(size):
        for s in range(count):
            t = 1 - s if step == "swap" else s + step
            if 0 <= t < count:
                pairs.append((f * count + s, (f ^ (2 * relative)) * count + t))
    return lax.ppermute(x, ("filt", "space"), pairs)


def on_device(volume, kernel, filter_bias):
    block, depth, height, across = volume.shape
    filters, cin = kernel.shape[0], kernel.shape[-1]
    size = lax.axis_size("filt")
    count = lax.axis_size("space")
    here = lax.axis_index("space")
    place = lax.axis_index("filt")
    flags = jnp.stack([place & 1, place >> 1, here, count - 1 - here]).astype(jnp.int32)
    far = size // 4
    pairs = height // 2

    vmem = pl.BlockSpec(memory_space=pltpu.VMEM)
    smem = pl.BlockSpec(memory_space=pltpu.SMEM)
    shape = jax.ShapeDtypeStruct
    macs = 27 * filters * cin * depth * height * across
    padded = pltpu.VMEM((depth + 2, cin // 2, (height + 2) * across), bf16)

    def call(body, outs, ins, args, cost, scratch=()):
        return pl.pallas_call(
            body,
            out_shape=outs,
            in_specs=ins,
            out_specs=jax.tree.map(lambda _: vmem, outs),
            scratch_shapes=scratch,
            compiler_params=pltpu.CompilerParams(vmem_limit_bytes=16 << 20),
            cost_estimate=pl.CostEstimate(
                flops=int(cost * macs), bytes_accessed=1 << 20, transcendentals=0
            ),
        )(*args)

    far_block = shifted(volume, far, 0, size, count)
    plane = shape((block, 1, height, across), bf16)
    steps = ["swap"] if count == 2 else [1, -1]
    own_block, *edges = call(
        functools.partial(begin, count=count),
        [shape(volume.shape, bf16)] + [plane] * len(steps),
        [smem, vmem],
        (flags, volume),
        0.01,
    )
    sends = list(zip(edges, steps))
    own_planes = [shifted(x, 0, step, size, count) for x, step in sends]
    far_planes = [shifted(x, far, step, size, count) for x, step in sends]

    ordered = shape((9, 3 * filters, cin // 2), bf16)
    w_mine, w_theirs, bias = call(
        functools.partial(prepare, block=block),
        (ordered, ordered, shape((filters, across), f32)),
        [smem, vmem, vmem],
        (flags, kernel.transpose(1, 2, 3, 0, 4).reshape(-1, cin), filter_bias[None]),
        0.1,
    )

    rows = [x.reshape(-1, across) for x in [own_block] + own_planes + [far_block] + far_planes]
    cells = (depth + len(sends)) * height
    per_block = cells * block
    pair = call(
        functools.partial(assemble, block=block, per_block=per_block),
        shape((2 * per_block, across), bf16),
        [vmem] * len(rows) + [pl.BlockSpec(memory_space=pl.ANY)],
        rows + [w_mine],
        0.1,
    ).reshape(2, cells, block, across)
    near = [pair] + [shifted(pair, r, 0, size, count) for r in range(1, far)]
    mine = jnp.concatenate(near, axis=0)

    theirs = lax.ppermute(mine, "filt", [(i, i ^ 1) for i in range(size)])
    dims = dict(depth=depth, height=height)
    partial = call(
        functools.partial(first_half, **dims),
        shape((depth * pairs, 3 * filters, 2 * across), f32),
        [smem, vmem, vmem],
        (flags, w_mine, mine),
        8.0,
        [padded],
    )
    pooled = call(
        functools.partial(second_half, **dims),
        shape((filters * depth * height // 4, across // 2), bf16),
        [smem, vmem, vmem, vmem, vmem],
        (flags, w_theirs, theirs, partial, bias),
        1.0,
        [padded],
    )
    return pooled.reshape(filters, depth // 2, height // 2, across // 2)


def solution(mesh):
    in_specs = (P("filt", "space", None, None), P("filt", None, None, None, None), P("filt"))
    out_specs = P("filt", "space", None, None)
    return jax.shard_map(
        on_device, mesh=mesh, in_specs=in_specs, out_specs=out_specs, check_vma=False
    )
```

time: 29.8 us -> 25.3 us (0.85)
  starting transfers between devices: 13.2 us -> 9.3 us
  waiting for transfers between devices: 9.23 us -> 7.58 us
  local copies, waits for them, and re-layouts: 1.61 us -> 2.51 us
    ppermute x8 -> x6, starting transfers between devices: 13.1 us -> 9.22 us  [shifted(): return lax.ppermute(x, ('filt', 'space'), pairs)]
    ppermute x8 -> x6, waiting for transfers between devices: 9.22 us -> 6.96 us  [shifted(): return lax.ppermute(x, ('filt', 'space'), pairs)]
    unnamed x11 -> x6, local copies, waits for them, and re-layouts: 0.74 us -> 2.51 us
    transpose x1 -> x0, local copies, waits for them, and re-layouts: 0.86 us -> none  [on_device(): blocks = volume.transpose(1, 2, 0, 3).reshape(depth * height, block, across)]
    ppermute x1, waiting for transfers between devices: 0.01 us -> 0.62 us  [on_device(): theirs = lax.ppermute(mine, 'filt', [(i, i ^ 1) for i in range(size)])]
  transfers between devices with their start and end apart: 9 -> 7, of which waited for: 5 -> 4; matrix products, arithmetic and copies ran while one was open for 1% -> 0% of each run, Pallas kernels for 10% -> 11%
where the time goes in v3:
time: 25.3 us; the launch traced here: 25.1 us
  starting transfers between devices  9.3 us (37%)
  waiting for transfers between devices  7.58 us (30%)
  Pallas kernels  5.52 us (22%)
  local copies, waits for them, and re-layouts  2.51 us (10%)
    ppermute x6, starting transfers between devices, shifted(): return lax.ppermute(x, ('filt', 'space'), pairs)  9.22 us
    ppermute x6, waiting for transfers between devices, shifted(): return lax.ppermute(x, ('filt', 'space'), pairs)  6.96 us
    pallas_call x5, Pallas kernels, call(): pl.pallas_call(body, out_shape=outs, in_specs=ins, out_specs=jax.tree.map...  5.52 us
    unnamed x6, local copies, waits for them, and re-layouts  2.51 us
    ppermute x1, waiting for transfers between devices, on_device(): theirs = lax.ppermute(mine, 'filt', [(i, i ^ 1) for i in range(size)])  0.62 us
  transfers between devices with their start and end apart: 7, of which 4 were waited for; matrix products, arithmetic and copies ran while one was open for 0% of the time, Pallas kernels for 11%

profile of v3, /device:TPU:0, one launch (start us, length us, event | category | flops | bytes accessed | tf_op | source)
XLA Modules:
  0.0 25.1 jit_solution(6859289365165392119)
XLA Ops:
  0.0 4.0 %collective-permute-start.1 = (bf16[16,4,4,128]{3,2,1,0:T(4,128)(2,1)}, bf16[16,4,4,128]{3,2,1,0:T(4,128)(2,1)S(1)}, u32[]{:S(2)}, u32[]{:S(2)}) collective-permute-start(bf16[16,4,4,128]{3,2,1,0:T(4,128)(2,1)} %vol_ref.1), channel_id=1, source_target_pairs={{0,16},{1,17},{2,18},{3,19},{4,20},{5,21},{6,22},{7,23},{8,24},{9,... | collective-permute-start | bytes 196616 | tf_op jit(solution)/shard_map/ppermute | solution.py:155
  4.0 0.1 pad_add_fusion.flags_ref
  4.1 0.8 %copy-done.1 = bf16[16,4,4,128]{3,2,1,0:T(4,128)(2,1)S(1)} copy-done((bf16[16,4,4,128]{3,2,1,0:T(4,128)(2,1)S(1)}, bf16[16,4,4,128]{3,2,1,0:T(4,128)(2,1)}, u32[]{:S(2)}) %copy-start.1) | copy-done | bytes 65560
  5.0 0.6 %shard_map.38 = (bf16[16,4,4,128]{3,2,1,0:T(4,128)(2,1)S(1)}, bf16[16,1,4,128]{3,2,1,0:T(4,128)(2,1)S(1)}) custom-call(s32[4]{0:T(128)S(1)} %pad_add_fusion.flags_ref, bf16[16,4,4,128]{3,2,1,0:T(4,128)(2,1)S(1)} %copy-done.1), custom_call_target="tpu_custom_call" | custom-call | flops 4529848 | bytes 1048576 | tf_op jit(solution)/shard_map/pallas_call | solution.py:176
  5.5 1.3 %collective-permute-start.2 = (bf16[16,1,4,128]{3,2,1,0:T(4,128)(2,1)S(1)}, bf16[16,1,4,128]{3,2,1,0:T(4,128)(2,1)S(1)}, u32[]{:S(2)}, u32[]{:S(2)}) collective-permute-start(bf16[16,1,4,128]{3,2,1,0:T(4,128)(2,1)S(1)} %get-tuple-element.12), channel_id=1, source_target_pairs={{0,17},{1,16},{2,19},{3,18},{4,21},{5,20},{6,23},{7,22},{8,25},{9,... | collective-permute-start | bytes 49160 | tf_op jit(solution)/shard_map/ppermute | solution.py:155
  6.8 0.3 %collective-permute-start = (bf16[16,1,4,128]{3,2,1,0:T(4,128)(2,1)S(1)}, bf16[16,1,4,128]{3,2,1,0:T(4,128)(2,1)S(1)}, u32[]{:S(2)}, u32[]{:S(2)}) collective-permute-start(bf16[16,1,4,128]{3,2,1,0:T(4,128)(2,1)S(1)} %get-tuple-element.12), channel_id=1, source_target_pairs={{0,1},{1,0},{2,3},{3,2},{4,5},{5,4},{6,7},{7,6},{8,9},{9,8},{10,11... | collective-permute-start | bytes 49160 | tf_op jit(solution)/shard_map/ppermute | solution.py:155
  7.2 0.7 %copy-done.2 = bf16[32]{0:T(256)(128)(2,1)S(1)} copy-done((bf16[32]{0:T(256)(128)(2,1)S(1)}, bf16[32]{0:T(256)(128)(2,1)}, u32[]{:S(2)}) %copy-start.2) | copy-done | bytes 88
  7.8 1.0 %copy-done = bf16[32,3,3,3,256]{4,0,3,2,1:T(8,128)(2,1)S(1)} copy-done((bf16[32,3,3,3,256]{4,0,3,2,1:T(8,128)(2,1)S(1)}, bf16[32,3,3,3,256]{4,0,3,2,1:T(8,128)(2,1)}, u32[]{:S(2)}) %copy-start) | copy-done | bytes 442392
  8.8 0.8 %shard_map.37 = (bf16[9,96,128]{2,1,0:T(8,128)(2,1)S(1)}, bf16[9,96,128]{2,1,0:T(8,128)(2,1)S(1)}, f32[32,128]{1,0:T(8,128)S(1)}) custom-call(s32[4]{0:T(128)S(1)} %pad_add_fusion.flags_ref, bf16[864,256]{1,0:T(8,128)(2,1)S(1)} %bitcast.18, bf16[1,32]{1,0:T(2,128)(2,1)S(1)} %bitcast.23), custom_call_target="tpu_custom_call" | custom-call | flops 45298484 | bytes 1048576 | tf_op jit(solution)/shard_map/pallas_call | solution.py:176
  9.7 1.5 %collective-permute-done.2 = bf16[16,1,4,128]{3,2,1,0:T(4,128)(2,1)S(1)} collective-permute-done((bf16[16,1,4,128]{3,2,1,0:T(4,128)(2,1)S(1)}, bf16[16,1,4,128]{3,2,1,0:T(4,128)(2,1)S(1)}, u32[]{:S(2)}, u32[]{:S(2)}) %collective-permute-start.2) | collective-permute-done | bytes 16416 | tf_op jit(solution)/shard_map/ppermute | solution.py:155
  11.1 0.0 collective-permute-done
  11.1 0.0 collective-permute-done.1
  11.1 0.2 shard_map.39
  11.3 2.6 %collective-permute-start.5 = (bf16[2,20,16,128]{3,2,1,0:T(8,128)(2,1)S(1)}, bf16[2,20,16,128]{3,2,1,0:T(8,128)(2,1)S(1)}, u32[]{:S(2)}, u32[]{:S(2)}) collective-permute-start(bf16[2,20,16,128]{3,2,1,0:T(8,128)(2,1)S(1)} %bitcast.14), channel_id=1, source_target_pairs={{0,12},{1,13},{2,14},{3,15},{4,8},{5,9},{6,10},{7,11},{8,4},{9,5},... | collective-permute-start | bytes 491528 | tf_op jit(solution)/shard_map/ppermute | solution.py:155
  13.9 0.4 %collective-permute-start.4 = (bf16[2,20,16,128]{3,2,1,0:T(8,128)(2,1)S(1)}, bf16[2,20,16,128]{3,2,1,0:T(8,128)(2,1)S(1)}, u32[]{:S(2)}, u32[]{:S(2)}) collective-permute-start(bf16[2,20,16,128]{3,2,1,0:T(8,128)(2,1)S(1)} %bitcast.15), channel_id=1, source_target_pairs={{0,8},{1,9},{2,10},{3,11},{4,12},{5,13},{6,14},{7,15},{8,0},{9,1},... | collective-permute-start | bytes 491528 | tf_op jit(solution)/shard_map/ppermute | solution.py:155
  14.4 0.5 %collective-permute-start.3 = (bf16[2,20,16,128]{3,2,1,0:T(8,128)(2,1)S(1)}, bf16[2,20,16,128]{3,2,1,0:T(8,128)(2,1)S(1)}, u32[]{:S(2)}, u32[]{:S(2)}) collective-permute-start(bf16[2,20,16,128]{3,2,1,0:T(8,128)(2,1)S(1)} %bitcast.16), channel_id=1, source_target_pairs={{0,4},{1,5},{2,6},{3,7},{4,0},{5,1},{6,2},{7,3},{8,12},{9,13},{10,... | collective-permute-start | bytes 491528 | tf_op jit(solution)/shard_map/ppermute | solution.py:155
  14.9 3.7 %collective-permute-done.5 = bf16[2,20,16,128]{3,2,1,0:T(8,128)(2,1)S(1)} collective-permute-done((bf16[2,20,16,128]{3,2,1,0:T(8,128)(2,1)S(1)}, bf16[2,20,16,128]{3,2,1,0:T(8,128)(2,1)S(1)}, u32[]{:S(2)}, u32[]{:S(2)}) %collective-permute-start.5) | collective-permute-done | bytes 163872 | tf_op jit(solution)/shard_map/ppermute | solution.py:155
  18.6 1.7 %collective-permute-done.4 = bf16[2,20,16,128]{3,2,1,0:T(8,128)(2,1)S(1)} collective-permute-done((bf16[2,20,16,128]{3,2,1,0:T(8,128)(2,1)S(1)}, bf16[2,20,16,128]{3,2,1,0:T(8,128)(2,1)S(1)}, u32[]{:S(2)}, u32[]{:S(2)}) %collective-permute-start.4) | collective-permute-done | bytes 163872 | tf_op jit(solution)/shard_map/ppermute | solution.py:155
  20.4 0.0 collective-permute-done.3
  20.4 0.1 pad_maximum_fusion.vol_ref
  20.5 0.1 collective-permute-start.6
  20.5 1.5 %shard_map.40.sum_ref = f32[8,96,256]{2,1,0:T(8,128)S(1)} custom-call(s32[4]{0:T(128)S(1)} %pad_add_fusion.flags_ref, bf16[9,96,128]{2,1,0:T(8,128)(2,1)S(1)} %get-tuple-element.13.refs_4_.w_ref, bf16[8,20,16,128]{3,2,1,0:T(8,128)(2,1)S(1)} %pad_maximum_fusion.vol_ref), custom_call_target="tpu_custom_call" | custom-call | flops 3623878656 | bytes 1048576 | tf_op jit(solution)/shard_map/pallas_call | solution.py:176
  22.0 0.6 %collective-permute-done.6.vol_ref = bf16[8,20,16,128]{3,2,1,0:T(8,128)(2,1)S(1)} collective-permute-done((bf16[8,20,16,128]{3,2,1,0:T(8,128)(2,1)S(1)}, bf16[8,20,16,128]{3,2,1,0:T(8,128)(2,1)S(1)}, u32[]{:S(2)}, u32[]{:S(2)}) %collective-permute-start.6) | collective-permute-done | bytes 655392 | tf_op jit(solution)/shard_map/ppermute | solution.py:224
  22.6 2.5 %shard_map.41 = bf16[128,64]{1,0:T(8,128)(2,1)} custom-call(s32[4]{0:T(128)S(1)} %pad_add_fusion.flags_ref, bf16[9,96,128]{2,1,0:T(8,128)(2,1)S(1)} %get-tuple-element.10.w_ref, bf16[8,20,16,128]{3,2,1,0:T(8,128)(2,1)S(1)} %collective-permute-done.6.vol_ref, f32[8,96,256]{2,1,0:T(8,128)S(1)} %shard_map.40.sum_ref, f32[32,128]{1,0:T(8,128)S(1)} %get-tuple-element.14.bias_ref), custom_call_target="tpu_custom_call" | custom-call | flops 452984832 | bytes 1048576 | tf_op jit(solution)/shard_map/pallas_call | solution.py:176
  (3 shorter events, 0.0 us)
Async XLA Ops:
  0.0 11.1 %collective-permute-start.1 = (bf16[16,4,4,128]{3,2,1,0:T(4,128)(2,1)}, bf16[16,4,4,128]{3,2,1,0:T(4,128)(2,1)S(1)}, u32[]{:S(2)}, u32[]{:S(2)}) collective-permute-start(bf16[16,4,4,128]{3,2,1,0:T(4,128)(2,1)} %vol_ref.1), channel_id=1, source_target_pairs={{0,16},{1,17},{2,18},{3,19},{4,20},{5,21},{6,22},{7,23},{8,24},{9,... | collective-permute-start | bytes 196616 | tf_op jit(solution)/shard_map/ppermute | solution.py:155
  4.1 0.8 %copy-start.1 = (bf16[16,4,4,128]{3,2,1,0:T(4,128)(2,1)S(1)}, bf16[16,4,4,128]{3,2,1,0:T(4,128)(2,1)}, u32[]{:S(2)}) copy-start(bf16[16,4,4,128]{3,2,1,0:T(4,128)(2,1)} %vol_ref.1) | copy-start | bytes 196612
  5.5 5.6 %collective-permute-start.2 = (bf16[16,1,4,128]{3,2,1,0:T(4,128)(2,1)S(1)}, bf16[16,1,4,128]{3,2,1,0:T(4,128)(2,1)S(1)}, u32[]{:S(2)}, u32[]{:S(2)}) collective-permute-start(bf16[16,1,4,128]{3,2,1,0:T(4,128)(2,1)S(1)} %get-tuple-element.12), channel_id=1, source_target_pairs={{0,17},{1,16},{2,19},{3,18},{4,21},{5,20},{6,23},{7,22},{8,25},{9,... | collective-permute-start | bytes 49160 | tf_op jit(solution)/shard_map/ppermute | solution.py:155
  6.8 4.3 %collective-permute-start = (bf16[16,1,4,128]{3,2,1,0:T(4,128)(2,1)S(1)}, bf16[16,1,4,128]{3,2,1,0:T(4,128)(2,1)S(1)}, u32[]{:S(2)}, u32[]{:S(2)}) collective-permute-start(bf16[16,1,4,128]{3,2,1,0:T(4,128)(2,1)S(1)} %get-tuple-element.12), channel_id=1, source_target_pairs={{0,1},{1,0},{2,3},{3,2},{4,5},{5,4},{6,7},{7,6},{8,9},{9,8},{10,11... | collective-permute-start | bytes 49160 | tf_op jit(solution)/shard_map/ppermute | solution.py:155
  7.2 0.7 %copy-start.2 = (bf16[32]{0:T(256)(128)(2,1)S(1)}, bf16[32]{0:T(256)(128)(2,1)}, u32[]{:S(2)}) copy-start(bf16[32]{0:T(256)(128)(2,1)} %param.5) | copy-start | bytes 196
  7.8 1.0 %copy-start = (bf16[32,3,3,3,256]{4,0,3,2,1:T(8,128)(2,1)S(1)}, bf16[32,3,3,3,256]{4,0,3,2,1:T(8,128)(2,1)}, u32[]{:S(2)}) copy-start(bf16[32,3,3,3,256]{4,0,3,2,1:T(8,128)(2,1)} %param.4) | copy-start | bytes 1327108
  11.3 7.3 %collective-permute-start.5 = (bf16[2,20,16,128]{3,2,1,0:T(8,128)(2,1)S(1)}, bf16[2,20,16,128]{3,2,1,0:T(8,128)(2,1)S(1)}, u32[]{:S(2)}, u32[]{:S(2)}) collective-permute-start(bf16[2,20,16,128]{3,2,1,0:T(8,128)(2,1)S(1)} %bitcast.14), channel_id=1, source_target_pairs={{0,12},{1,13},{2,14},{3,15},{4,8},{5,9},{6,10},{7,11},{8,4},{9,5},... | collective-permute-start | bytes 491528 | tf_op jit(solution)/shard_map/ppermute | solution.py:155
  13.9 6.4 %collective-permute-start.4 = (bf16[2,20,16,128]{3,2,1,0:T(8,128)(2,1)S(1)}, bf16[2,20,16,128]{3,2,1,0:T(8,128)(2,1)S(1)}, u32[]{:S(2)}, u32[]{:S(2)}) collective-permute-start(bf16[2,20,16,128]{3,2,1,0:T(8,128)(2,1)S(1)} %bitcast.15), channel_id=1, source_target_pairs={{0,8},{1,9},{2,10},{3,11},{4,12},{5,13},{6,14},{7,15},{8,0},{9,1},... | collective-permute-start | bytes 491528 | tf_op jit(solution)/shard_map/ppermute | solution.py:155
  14.4 6.0 %collective-permute-start.3 = (bf16[2,20,16,128]{3,2,1,0:T(8,128)(2,1)S(1)}, bf16[2,20,16,128]{3,2,1,0:T(8,128)(2,1)S(1)}, u32[]{:S(2)}, u32[]{:S(2)}) collective-permute-start(bf16[2,20,16,128]{3,2,1,0:T(8,128)(2,1)S(1)} %bitcast.16), channel_id=1, source_target_pairs={{0,4},{1,5},{2,6},{3,7},{4,0},{5,1},{6,2},{7,3},{8,12},{9,13},{10,... | collective-permute-start | bytes 491528 | tf_op jit(solution)/shard_map/ppermute | solution.py:155
  20.5 2.2 %collective-permute-start.6 = (bf16[8,20,16,128]{3,2,1,0:T(8,128)(2,1)S(1)}, bf16[8,20,16,128]{3,2,1,0:T(8,128)(2,1)S(1)}, u32[]{:S(2)}, u32[]{:S(2)}) collective-permute-start(bf16[8,20,16,128]{3,2,1,0:T(8,128)(2,1)S(1)} %pad_maximum_fusion.vol_ref), channel_id=1, source_target_pairs={{0,2},{2,0},{4,6},{6,4},{8,10},{10,8},{12,14},{14,12},{16,18},{18,... | collective-permute-start | bytes 1966088 | tf_op jit(solution)/shard_map/ppermute | solution.py:224

commit v4 on v3

v4 whole, which is shorter than its diff:
```python
import functools

import jax
import jax.numpy as jnp
from jax import lax
from jax.experimental import pallas as pl
from jax.experimental.pallas import tpu as pltpu
from jax.sharding import PartitionSpec as P

slope = 0.3
f32, bf16 = jnp.float32, jnp.bfloat16


def one_hot(shape, wanted):
    target = lax.broadcasted_iota(jnp.int32, shape, 0)
    source = lax.broadcasted_iota(jnp.int32, shape, 1)
    return jnp.where(source == wanted(target), 1.0, 0.0).astype(bf16)


def sort_rows(x, block):
    rows = x.shape[0]
    cells = rows // block
    pick = one_hot((rows, rows), lambda t: (t & (block - 1)) * cells + t // block)
    return jnp.dot(pick, x, preferred_element_type=f32).astype(bf16)


def begin(flags_ref, vol_ref, own_ref, *plane_refs, block, depth, count):
    own_ref[...] = sort_rows(vol_ref[...], block)
    rows = own_ref.shape[0] // depth
    if count == 2:
        at = jnp.where(flags_ref[2] == 0, (depth - 1) * rows, 0)
        plane_refs[0][...] = own_ref[pl.ds(pl.multiple_of(at, rows), rows)]
    else:
        plane_refs[0][...] = own_ref[(depth - 1) * rows :]
        plane_refs[1][...] = own_ref[:rows]


def prepare(flags_ref, kernel_ref, bias_ref, w_first_ref, w_last_ref, bias_out_ref, *, block):
    cin = kernel_ref.shape[-1]
    chunk, quarter = cin // 2, cin // 4
    far = chunk // block // 2
    core, group = flags_ref[0], flags_ref[1]
    source = lax.broadcasted_iota(jnp.int32, (cin, cin), 0)
    target = lax.broadcasted_iota(jnp.int32, (cin, cin), 1)
    part = jnp.where((target & quarter) == 0, core, 1 - core)
    place = target & (quarter - 1)
    slot = place // block
    near = (target // chunk) * (far // 2) + (slot >> 1)
    relative = near | ((slot & 1) * far)
    wanted = ((relative ^ group) * 2 + part) * block + (place & (block - 1))
    shuffle = jnp.where(source == wanted, 1.0, 0.0).astype(bf16)
    ordered = jnp.dot(kernel_ref[...], shuffle, preferred_element_type=f32).astype(bf16)
    w_first_ref[...] = ordered[:, :chunk].reshape(w_first_ref.shape)
    w_last_ref[...] = ordered[:, chunk:].reshape(w_last_ref.shape)
    filters = bias_ref.shape[1]
    row = lax.broadcasted_iota(jnp.int32, (filters, filters), 0)
    column = lax.broadcasted_iota(jnp.int32, (filters, filters), 1)
    spread = jnp.where(row == column, bias_ref[...].astype(f32), 0.0)
    bias_out_ref[...] = jnp.broadcast_to(
        jnp.sum(spread, axis=1, keepdims=True), bias_out_ref.shape
    )


def assemble(*refs, block):
    in_refs, pair_ref = refs[:-1], refs[-1]
    own_ref, far_ref = in_refs[0], in_refs[-1]
    size = own_ref.shape[0]
    at = size
    pair_ref[:size] = own_ref[...]
    for ref in in_refs[1:-1]:
        rows = ref.shape[0]
        pair_ref[at : at + rows] = ref[...]
        at += rows
    pair_ref[at:] = sort_rows(far_ref[...], block)


def join(*refs):
    in_refs, out_ref = refs[1:-1], refs[-1]
    at = 0
    for ref in in_refs:
        out_ref[at : at + ref.shape[0]] = ref[...]
        at += ref.shape[0]


def row_of(refs, plane, y, depth, height, extra):
    size, beside = depth * height, extra * height
    per_pair = 2 * (size + beside)
    pieces = []
    for ref in refs:
        for pair in range(ref.shape[0] // per_pair):
            for far in range(2):
                if 0 <= plane < depth:
                    at = far * (size + 2 * beside) + plane * height + y
                else:
                    which = 1 if plane == depth and extra == 2 else 0
                    at = size + far * beside + which * height + y
                pieces.append(ref[pair * per_pair + at])
    return jnp.concatenate(pieces, axis=0)


def products(flags_ref, w_ref, refs, depth, height, extra):
    zero = jnp.zeros((w_ref.shape[-1], refs[0].shape[-1]), bf16)
    weights = [w_ref[k] for k in range(9)]
    none = jnp.zeros_like(weights[0])
    for z in range(depth):
        left = []
        for a in range(3):
            for b in range(3):
                w = weights[a * 3 + b]
                if z + a - 1 < 0:
                    w = jnp.where(flags_ref[2] > 0, w, none)
                if z + a - 1 == depth:
                    w = jnp.where(flags_ref[3] > 0, w, none)
                left.append(w)
        left = jnp.concatenate(left, axis=1)
        rows = [
            [zero] + [row_of(refs, z + a - 1, y, depth, height, extra) for y in range(height)] + [zero]
            for a in range(3)
        ]
        for y in range(0, height, 2):
            right = jnp.concatenate(
                [
                    jnp.concatenate([rows[a][y + b], rows[a][y + b + 1]], axis=1)
                    for a in range(3)
                    for b in range(3)
                ],
                axis=0,
            )
            yield z, y, jnp.dot(left, right, preferred_element_type=f32)


def combine(total, k, filters, across):
    part = total[:, k * across : (k + 1) * across]
    lane = lax.broadcasted_iota(jnp.int32, (filters, across), 1)
    left = pltpu.roll(part[:filters], 1, 1)
    right = pltpu.roll(part[2 * filters :], across - 1, 1)
    v = part[filters : 2 * filters]
    v += jnp.where(lane > 0, left, 0.0)
    return v + jnp.where(lane < across - 1, right, 0.0)


def first_chunk(flags_ref, w_ref, mine_ref, theirs_ref, sum_ref, *, depth, height, extra):
    pairs = height // 2
    for z, y, total in products(flags_ref, w_ref, (mine_ref, theirs_ref), depth, height, extra):
        sum_ref[z * pairs + y // 2] = total


def last_chunk(
    flags_ref, w_ref, mine_ref, theirs_ref, sum_ref, bias_ref, out_ref, *, depth, height, extra
):
    across = mine_ref.shape[-1]
    filters = bias_ref.shape[0]
    pairs = height // 2
    pooled = {}
    for z, y, total in products(flags_ref, w_ref, (mine_ref, theirs_ref), depth, height, extra):
        total += sum_ref[z * pairs + y // 2]
        for j in range(2):
            v = combine(total, j, filters, across) + bias_ref[...]
            v = jnp.where(v > 0, v, slope * v)
            key = (z // 2, y // 2)
            pooled[key] = v if key not in pooled else jnp.maximum(pooled[key], v)
    stacked = jnp.concatenate(
        [pooled[z, y] for z in range(depth // 2) for y in range(pairs)], axis=0
    )
    stacked = jnp.maximum(stacked, pltpu.roll(stacked, across - 1, 1)).astype(bf16)
    cells = (depth // 2) * pairs
    size = cells * filters
    rows_pick = one_hot((size, size), lambda t: (t & (cells - 1)) * filters + t // cells)
    lane_from = lax.broadcasted_iota(jnp.int32, (across, across // 2), 0)
    lane_to = lax.broadcasted_iota(jnp.int32, (across, across // 2), 1)
    lanes_pick = jnp.where(lane_from == 2 * lane_to, 1.0, 0.0).astype(bf16)
    picked = jnp.dot(stacked, lanes_pick, preferred_element_type=f32).astype(bf16)
    out_ref[...] = jnp.dot(rows_pick, picked, preferred_element_type=f32).astype(bf16)


def shifted(x, relative, step, size, count):
    pairs = []
    for f in range(size):
        for s in range(count):
            t = 1 - s if step == "swap" else s + step
            if 0 <= t < count:
                pairs.append((f * count + s, (f ^ (2 * relative)) * count + t))
    return lax.ppermute(x, ("filt", "space"), pairs)


def on_device(volume, kernel, filter_bias):
    block, depth, height, across = volume.shape
    filters, cin = kernel.shape[0], kernel.shape[-1]
    size = lax.axis_size("filt")
    count = lax.axis_size("space")
    here = lax.axis_index("space")
    place = lax.axis_index("filt")
    flags = jnp.stack([place & 1, place >> 1, here, count - 1 - here]).astype(jnp.int32)
    far = size // 4
    pairs = height // 2

    vmem = pl.BlockSpec(memory_space=pltpu.VMEM)
    smem = pl.BlockSpec(memory_space=pltpu.SMEM)
    anywhere = pl.BlockSpec(memory_space=pl.ANY)
    shape = jax.ShapeDtypeStruct
    macs = 27 * filters * cin * depth * height * across

    def call(body, outs, ins, args, cost):
        return pl.pallas_call(
            body,
            out_shape=outs,
            in_specs=ins,
            out_specs=jax.tree.map(lambda _: vmem, outs),
            compiler_params=pltpu.CompilerParams(vmem_limit_bytes=16 << 20),
            cost_estimate=pl.CostEstimate(
                flops=int(cost * macs) >> 12, bytes_accessed=1 << 8, transcendentals=0
            ),
        )(*args)

    far_block = shifted(volume, far, 0, size, count)
    cells = depth * height * block
    beside = height * block
    steps = ["swap"] if count == 2 else [1, -1]
    extra = len(steps)
    own_block, *edges = call(
        functools.partial(begin, block=block, depth=depth, count=count),
        [shape((cells, across), bf16)] + [shape((beside, across), bf16)] * extra,
        [smem, vmem],
        (flags, volume.reshape(cells, across)),
        0.01,
    )
    sends = list(zip(edges, steps))
    far_planes = [shifted(x, far, step, size, count) for x, step in sends]
    own_planes = [shifted(x, 0, step, size, count) for x, step in sends]

    per_pair = 2 * (cells + extra * beside)
    pair = call(
        functools.partial(assemble, block=block),
        shape((per_pair, across), bf16),
        [vmem] * (2 + 2 * extra),
        [own_block] + own_planes + far_planes + [far_block.reshape(cells, across)],
        0.05,
    )
    near = [pair] + [shifted(pair, r, 0, size, count) for r in range(1, far)]

    ordered = shape((9, 3 * filters, cin // 2), bf16)
    w_first, w_last, bias = call(
        functools.partial(prepare, block=block),
        (ordered, ordered, shape((filters, across), f32)),
        [smem, vmem, vmem],
        (flags, kernel.transpose(1, 2, 3, 0, 4).reshape(-1, cin), filter_bias[None]),
        0.1,
    )

    def both_cores(parts):
        mine = call(
            join,
            shape((far // 2 * per_pair, across), bf16),
            [anywhere] + [vmem] * len(parts),
            [w_first] + parts,
            0.05,
        ).reshape(-1, block, across)
        return mine, lax.ppermute(mine, "filt", [(i, i ^ 1) for i in range(size)])

    dims = dict(depth=depth, height=height, extra=extra)
    mine, theirs = both_cores(near[: far // 2])
    partial = call(
        functools.partial(first_chunk, **dims),
        shape((depth * pairs, 3 * filters, 2 * across), f32),
        [smem, vmem, vmem, vmem],
        (flags, w_first, mine, theirs),
        4.0,
    )
    mine, theirs = both_cores(near[far // 2 :])
    pooled = call(
        functools.partial(last_chunk, **dims),
        shape((filters * depth * height // 4, across // 2), bf16),
        [smem, vmem, vmem, vmem, vmem, vmem],
        (flags, w_last, mine, theirs, partial, bias),
        1.0,
    )
    return pooled.reshape(filters, depth // 2, height // 2, across // 2)


def solution(mesh):
    in_specs = (P("filt", "space", None, None), P("filt", None, None, None, None), P("filt"))
    out_specs = P("filt", "space", None, None)
    return jax.shard_map(
        on_device, mesh=mesh, in_specs=in_specs, out_specs=out_specs, check_vma=False
    )
```

time: 25.3 us -> 26.8 us (1.059)
  waiting for transfers between devices: 7.58 us -> 9.01 us
    ppermute x6, waiting for transfers between devices: 6.96 us -> 8.86 us  [shifted(): return lax.ppermute(x, ('filt', 'space'), pairs)]
    ppermute x1 -> x2, waiting for transfers between devices: 0.62 us -> 0.15 us  [both_cores(): return (mine, lax.ppermute(mine, 'filt', [(i, i ^ 1) for i in range(size)]))]
    pallas_call x5 -> x7, Pallas kernels: 5.52 us -> 5.68 us  [call(): pl.pallas_call(body, out_shape=outs, in_specs=ins, out_specs=jax.tree.map...]
  transfers between devices with their start and end apart: 7 -> 8, of which waited for: 4 -> 6; matrix products, arithmetic and copies ran while one was open for 0% -> 0% of each run, Pallas kernels for 11% -> 11%
where the time goes in v4:
time: 26.8 us; the launch traced here: 26.6 us
  starting transfers between devices  9.29 us (35%)
  waiting for transfers between devices  9.01 us (34%)
  Pallas kernels  5.68 us (21%)
  local copies, waits for them, and re-layouts  2.51 us (9%)
    ppermute x6, starting transfers between devices, shifted(): return lax.ppermute(x, ('filt', 'space'), pairs)  9.15 us
    ppermute x6, waiting for transfers between devices, shifted(): return lax.ppermute(x, ('filt', 'space'), pairs)  8.86 us
    pallas_call x7, Pallas kernels, call(): pl.pallas_call(body, out_shape=outs, in_specs=ins, out_specs=jax.tree.map...  5.68 us
    unnamed x6, local copies, waits for them, and re-layouts  2.51 us
  transfers between devices with their start and end apart: 8, of which 6 were waited for; matrix products, arithmetic and copies ran while one was open for 0% of the time, Pallas kernels for 11%

profile of v4, /device:TPU:0, one launch (start us, length us, event | category | flops | bytes accessed | tf_op | source)
XLA Modules:
  0.0 26.6 jit_solution(15279186620637436854)
XLA Ops:
  0.0 4.0 %collective-permute-start.2 = (bf16[16,4,4,128]{3,2,1,0:T(4,128)(2,1)}, bf16[16,4,4,128]{3,2,1,0:T(4,128)(2,1)S(1)}, u32[]{:S(2)}, u32[]{:S(2)}) collective-permute-start(bf16[16,4,4,128]{3,2,1,0:T(4,128)(2,1)} %param.3), channel_id=1, source_target_pairs={{0,16},{1,17},{2,18},{3,19},{4,20},{5,21},{6,22},{7,23},{8,24},{9,... | collective-permute-start | bytes 196616 | tf_op jit(solution)/shard_map/ppermute | solution.py:183
  4.0 0.1 pad_add_fusion.flags_ref
  4.1 0.8 %copy-done.1 = bf16[16,4,4,128]{3,2,1,0:T(4,128)(2,1)S(1)} copy-done((bf16[16,4,4,128]{3,2,1,0:T(4,128)(2,1)S(1)}, bf16[16,4,4,128]{3,2,1,0:T(4,128)(2,1)}, u32[]{:S(2)}) %copy-start.1) | copy-done | bytes 65560
  5.0 0.7 %shard_map.38 = (bf16[256,128]{1,0:T(8,128)(2,1)S(1)}, bf16[64,128]{1,0:T(8,128)(2,1)S(1)}) custom-call(s32[4]{0:T(128)S(1)} %pad_add_fusion.flags_ref, bf16[256,128]{1,0:T(8,128)(2,1)S(1)} %bitcast.19), custom_call_target="tpu_custom_call" | custom-call | flops 1105 | bytes 256 | tf_op jit(solution)/shard_map/pallas_call | solution.py:204
  5.7 1.6 %collective-permute-start = (bf16[64,128]{1,0:T(8,128)(2,1)S(1)}, bf16[64,128]{1,0:T(8,128)(2,1)S(1)}, u32[]{:S(2)}, u32[]{:S(2)}) collective-permute-start(bf16[64,128]{1,0:T(8,128)(2,1)S(1)} %get-tuple-element.13), channel_id=1, source_target_pairs={{0,1},{1,0},{2,3},{3,2},{4,5},{5,4},{6,7},{7,6},{8,9},{9,8},{10,11... | collective-permute-start | bytes 49160 | tf_op jit(solution)/shard_map/ppermute | solution.py:183
  7.2 0.0 collective-permute-start.1
  7.2 2.2 %collective-permute-done.refs_1_ = bf16[64,128]{1,0:T(8,128)(2,1)S(1)} collective-permute-done((bf16[64,128]{1,0:T(8,128)(2,1)S(1)}, bf16[64,128]{1,0:T(8,128)(2,1)S(1)}, u32[]{:S(2)}, u32[]{:S(2)}) %collective-permute-start) | collective-permute-done | bytes 16416 | tf_op jit(solution)/shard_map/ppermute | solution.py:183
  9.5 3.3 %collective-permute-done.1.refs_2_ = bf16[64,128]{1,0:T(8,128)(2,1)S(1)} collective-permute-done((bf16[64,128]{1,0:T(8,128)(2,1)S(1)}, bf16[64,128]{1,0:T(8,128)(2,1)S(1)}, u32[]{:S(2)}, u32[]{:S(2)}) %collective-permute-start.1) | collective-permute-done | bytes 16416 | tf_op jit(solution)/shard_map/ppermute | solution.py:183
  12.8 0.0 collective-permute-done.2
  12.8 0.2 shard_map.39.refs_1_
  13.0 1.6 %collective-permute-start.6 = (bf16[640,128]{1,0:T(8,128)(2,1)S(1)}, bf16[640,128]{1,0:T(8,128)(2,1)S(1)}, u32[]{:S(2)}, u32[]{:S(2)}) collective-permute-start(bf16[640,128]{1,0:T(8,128)(2,1)S(1)} %shard_map.39.refs_1_), channel_id=1, source_target_pairs={{0,4},{1,5},{2,6},{3,7},{4,0},{5,1},{6,2},{7,3},{8,12},{9,13},{10,... | collective-permute-start | bytes 491528 | tf_op jit(solution)/shard_map/ppermute | solution.py:183
  14.5 1.6 %collective-permute-start.3 = (bf16[640,128]{1,0:T(8,128)(2,1)S(1)}, bf16[640,128]{1,0:T(8,128)(2,1)S(1)}, u32[]{:S(2)}, u32[]{:S(2)}) collective-permute-start(bf16[640,128]{1,0:T(8,128)(2,1)S(1)} %shard_map.39.refs_1_), channel_id=1, source_target_pairs={{0,8},{1,9},{2,10},{3,11},{4,12},{5,13},{6,14},{7,15},{8,0},{9,1},... | collective-permute-start | bytes 491528 | tf_op jit(solution)/shard_map/ppermute | solution.py:183
  16.1 0.4 %collective-permute-start.4 = (bf16[640,128]{1,0:T(8,128)(2,1)S(1)}, bf16[640,128]{1,0:T(8,128)(2,1)S(1)}, u32[]{:S(2)}, u32[]{:S(2)}) collective-permute-start(bf16[640,128]{1,0:T(8,128)(2,1)S(1)} %shard_map.39.refs_1_), channel_id=1, source_target_pairs={{0,12},{1,13},{2,14},{3,15},{4,8},{5,9},{6,10},{7,11},{8,4},{9,5},... | collective-permute-start | bytes 491528 | tf_op jit(solution)/shard_map/ppermute | solution.py:183
  16.5 0.7 %copy-done.2 = bf16[32]{0:T(256)(128)(2,1)S(1)} copy-done((bf16[32]{0:T(256)(128)(2,1)S(1)}, bf16[32]{0:T(256)(128)(2,1)}, u32[]{:S(2)}) %copy-start.2) | copy-done | bytes 88
  17.2 1.0 %copy-done = bf16[32,3,3,3,256]{4,0,3,2,1:T(8,128)(2,1)S(1)} copy-done((bf16[32,3,3,3,256]{4,0,3,2,1:T(8,128)(2,1)S(1)}, bf16[32,3,3,3,256]{4,0,3,2,1:T(8,128)(2,1)}, u32[]{:S(2)}) %copy-start) | copy-done | bytes 442392
  18.2 0.8 %shard_map.37 = (bf16[9,96,128]{2,1,0:T(8,128)(2,1)S(1)}, bf16[9,96,128]{2,1,0:T(8,128)(2,1)S(1)}, f32[32,128]{1,0:T(8,128)S(1)}) custom-call(s32[4]{0:T(128)S(1)} %pad_add_fusion.flags_ref, bf16[864,256]{1,0:T(8,128)(2,1)S(1)} %bitcast.17, bf16[1,32]{1,0:T(2,128)(2,1)S(1)} %bitcast.20), custom_call_target="tpu_custom_call" | custom-call | flops 11059 | bytes 256 | tf_op jit(solution)/shard_map/pallas_call | solution.py:204
  19.0 1.1 %collective-permute-done.6.refs_2_ = bf16[640,128]{1,0:T(8,128)(2,1)S(1)} collective-permute-done((bf16[640,128]{1,0:T(8,128)(2,1)S(1)}, bf16[640,128]{1,0:T(8,128)(2,1)S(1)}, u32[]{:S(2)}, u32[]{:S(2)}) %collective-permute-start.6) | collective-permute-done | bytes 163872 | tf_op jit(solution)/shard_map/ppermute | solution.py:183
  20.1 0.1 collective-permute-start.7
  20.2 0.1 collective-permute-done.3.refs_1_
  20.3 2.2 %collective-permute-done.4.refs_2_ = bf16[640,128]{1,0:T(8,128)(2,1)S(1)} collective-permute-done((bf16[640,128]{1,0:T(8,128)(2,1)S(1)}, bf16[640,128]{1,0:T(8,128)(2,1)S(1)}, u32[]{:S(2)}, u32[]{:S(2)}) %collective-permute-start.4) | collective-permute-done | bytes 163872 | tf_op jit(solution)/shard_map/ppermute | solution.py:183
  22.5 0.1 collective-permute-start.5
  22.6 1.5 %shard_map.42.sum_ref = f32[8,96,256]{2,1,0:T(8,128)S(1)} custom-call(s32[4]{0:T(128)S(1)} %pad_add_fusion.flags_ref, bf16[9,96,128]{2,1,0:T(8,128)(2,1)S(1)} %get-tuple-element.11.refs_0_.w_ref, bf16[80,16,128]{2,1,0:T(8,128)(2,1)S(1)} %bitcast.14, bf16[80,16,128]{2,1,0:T(8,128)(2,1)S(1)} %collective-permute-done.7.theirs_ref), custom_call_target="tpu_custom_call" | custom-call | flops 442368 | bytes 256 | tf_op jit(solution)/shard_map/pallas_call | solution.py:204
  24.0 0.1 collective-permute-done.5.theirs_ref
  24.2 2.5 %shard_map.43 = bf16[128,64]{1,0:T(8,128)(2,1)} custom-call(s32[4]{0:T(128)S(1)} %pad_add_fusion.flags_ref, bf16[9,96,128]{2,1,0:T(8,128)(2,1)S(1)} %get-tuple-element.10.w_ref, bf16[80,16,128]{2,1,0:T(8,128)(2,1)S(1)} %bitcast.16, bf16[80,16,128]{2,1,0:T(8,128)(2,1)S(1)} %collective-permute-done.5.theirs_ref, f32[8,96,256]{2,1,0:T(8,128)S(1)} %shard_map.42.sum_ref, ...), custom_call_target="tpu_custom_call" | custom-call | flops 110592 | bytes 256 | tf_op jit(solution)/shard_map/pallas_call | solution.py:204
  (6 shorter events, 0.1 us)
Async XLA Ops:
  0.0 12.8 %collective-permute-start.2 = (bf16[16,4,4,128]{3,2,1,0:T(4,128)(2,1)}, bf16[16,4,4,128]{3,2,1,0:T(4,128)(2,1)S(1)}, u32[]{:S(2)}, u32[]{:S(2)}) collective-permute-start(bf16[16,4,4,128]{3,2,1,0:T(4,128)(2,1)} %param.3), channel_id=1, source_target_pairs={{0,16},{1,17},{2,18},{3,19},{4,20},{5,21},{6,22},{7,23},{8,24},{9,... | collective-permute-start | bytes 196616 | tf_op jit(solution)/shard_map/ppermute | solution.py:183
  4.1 0.8 %copy-start.1 = (bf16[16,4,4,128]{3,2,1,0:T(4,128)(2,1)S(1)}, bf16[16,4,4,128]{3,2,1,0:T(4,128)(2,1)}, u32[]{:S(2)}) copy-start(bf16[16,4,4,128]{3,2,1,0:T(4,128)(2,1)} %param.3) | copy-start | bytes 196612
  5.7 3.8 %collective-permute-start = (bf16[64,128]{1,0:T(8,128)(2,1)S(1)}, bf16[64,128]{1,0:T(8,128)(2,1)S(1)}, u32[]{:S(2)}, u32[]{:S(2)}) collective-permute-start(bf16[64,128]{1,0:T(8,128)(2,1)S(1)} %get-tuple-element.13), channel_id=1, source_target_pairs={{0,1},{1,0},{2,3},{3,2},{4,5},{5,4},{6,7},{7,6},{8,9},{9,8},{10,11... | collective-permute-start | bytes 49160 | tf_op jit(solution)/shard_map/ppermute | solution.py:183
  7.2 5.5 %collective-permute-start.1 = (bf16[64,128]{1,0:T(8,128)(2,1)S(1)}, bf16[64,128]{1,0:T(8,128)(2,1)S(1)}, u32[]{:S(2)}, u32[]{:S(2)}) collective-permute-start(bf16[64,128]{1,0:T(8,128)(2,1)S(1)} %get-tuple-element.13), channel_id=1, source_target_pairs={{0,17},{1,16},{2,19},{3,18},{4,21},{5,20},{6,23},{7,22},{8,25},{9,... | collective-permute-start | bytes 49160 | tf_op jit(solution)/shard_map/ppermute | solution.py:183
  13.0 7.1 %collective-permute-start.6 = (bf16[640,128]{1,0:T(8,128)(2,1)S(1)}, bf16[640,128]{1,0:T(8,128)(2,1)S(1)}, u32[]{:S(2)}, u32[]{:S(2)}) collective-permute-start(bf16[640,128]{1,0:T(8,128)(2,1)S(1)} %shard_map.39.refs_1_), channel_id=1, source_target_pairs={{0,4},{1,5},{2,6},{3,7},{4,0},{5,1},{6,2},{7,3},{8,12},{9,13},{10,... | collective-permute-start | bytes 491528 | tf_op jit(solution)/shard_map/ppermute | solution.py:183
  14.5 5.7 %collective-permute-start.3 = (bf16[640,128]{1,0:T(8,128)(2,1)S(1)}, bf16[640,128]{1,0:T(8,128)(2,1)S(1)}, u32[]{:S(2)}, u32[]{:S(2)}) collective-permute-start(bf16[640,128]{1,0:T(8,128)(2,1)S(1)} %shard_map.39.refs_1_), channel_id=1, source_target_pairs={{0,8},{1,9},{2,10},{3,11},{4,12},{5,13},{6,14},{7,15},{8,0},{9,1},... | collective-permute-start | bytes 491528 | tf_op jit(solution)/shard_map/ppermute | solution.py:183
  16.1 6.3 %collective-permute-start.4 = (bf16[640,128]{1,0:T(8,128)(2,1)S(1)}, bf16[640,128]{1,0:T(8,128)(2,1)S(1)}, u32[]{:S(2)}, u32[]{:S(2)}) collective-permute-start(bf16[640,128]{1,0:T(8,128)(2,1)S(1)} %shard_map.39.refs_1_), channel_id=1, source_target_pairs={{0,12},{1,13},{2,14},{3,15},{4,8},{5,9},{6,10},{7,11},{8,4},{9,5},... | collective-permute-start | bytes 491528 | tf_op jit(solution)/shard_map/ppermute | solution.py:183
  16.5 0.7 %copy-start.2 = (bf16[32]{0:T(256)(128)(2,1)S(1)}, bf16[32]{0:T(256)(128)(2,1)}, u32[]{:S(2)}) copy-start(bf16[32]{0:T(256)(128)(2,1)} %param.5) | copy-start | bytes 196
  17.2 1.0 %copy-start = (bf16[32,3,3,3,256]{4,0,3,2,1:T(8,128)(2,1)S(1)}, bf16[32,3,3,3,256]{4,0,3,2,1:T(8,128)(2,1)}, u32[]{:S(2)}) copy-start(bf16[32,3,3,3,256]{4,0,3,2,1:T(8,128)(2,1)} %param.4) | copy-start | bytes 1327108
  20.1 2.4 %collective-permute-start.7 = (bf16[80,16,128]{2,1,0:T(8,128)(2,1)S(1)}, bf16[80,16,128]{2,1,0:T(8,128)(2,1)S(1)}, u32[]{:S(2)}, u32[]{:S(2)}) collective-permute-start(bf16[80,16,128]{2,1,0:T(8,128)(2,1)S(1)} %bitcast.13), channel_id=1, source_target_pairs={{0,2},{2,0},{4,6},{6,4},{8,10},{10,8},{12,14},{14,12},{16,18},{18,... | collective-permute-start | bytes 983048 | tf_op jit(solution)/shard_map/ppermute | solution.py:258
  22.5 1.7 %collective-permute-start.5 = (bf16[80,16,128]{2,1,0:T(8,128)(2,1)S(1)}, bf16[80,16,128]{2,1,0:T(8,128)(2,1)S(1)}, u32[]{:S(2)}, u32[]{:S(2)}) collective-permute-start(bf16[80,16,128]{2,1,0:T(8,128)(2,1)S(1)} %bitcast.15), channel_id=1, source_target_pairs={{0,2},{2,0},{4,6},{6,4},{8,10},{10,8},{12,14},{14,12},{16,18},{18,... | collective-permute-start | bytes 983048 | tf_op jit(solution)/shard_map/ppermute | solution.py:258

commit v5 on v4

v5 whole, which is shorter than its diff:
```python
import functools

import jax
import jax.numpy as jnp
from jax import lax
from jax.experimental import pallas as pl
from jax.experimental.pallas import tpu as pltpu
from jax.sharding import PartitionSpec as P

slope = 0.3
f32, bf16 = jnp.float32, jnp.bfloat16


def one_hot(shape, wanted):
    target = lax.broadcasted_iota(jnp.int32, shape, 0)
    source = lax.broadcasted_iota(jnp.int32, shape, 1)
    return jnp.where(source == wanted(target), 1.0, 0.0).astype(bf16)


def sort_rows(x, block):
    rows = x.shape[0]
    cells = rows // block
    pick = one_hot((rows, rows), lambda t: (t & (block - 1)) * cells + t // block)
    return jnp.dot(pick, x, preferred_element_type=f32).astype(bf16)


def begin(flags_ref, vol_ref, kernel_ref, bias_ref, own_ref, *refs, block, depth, count):
    plane_refs, (w_ref, bias_out_ref, raw_ref, done) = refs[:-4], refs[-4:]
    copies = [
        pltpu.make_async_copy(source, target, done.at[k])
        for k, (source, target) in enumerate(
            [(vol_ref, raw_ref), (kernel_ref, w_ref), (bias_ref, bias_out_ref)]
        )
    ]
    for copy in copies:
        copy.start()
    copies[0].wait()
    own_ref[...] = sort_rows(raw_ref[...], block)
    rows = own_ref.shape[0] // depth
    if count == 2:
        at = jnp.where(flags_ref[2] == 0, (depth - 1) * rows, 0)
        plane_refs[0][...] = own_ref[pl.ds(pl.multiple_of(at, rows), rows)]
    else:
        plane_refs[0][...] = own_ref[(depth - 1) * rows :]
        plane_refs[1][...] = own_ref[:rows]
    for copy in copies[1:]:
        copy.wait()


def prepare(flags_ref, kernel_ref, bias_ref, w_mine_ref, w_theirs_ref, bias_out_ref, *, block):
    cin = kernel_ref.shape[-1]
    half = cin // 2
    far = half // block // 2
    shift = block.bit_length() - 1
    core, group = flags_ref[0], flags_ref[1]
    source = lax.broadcasted_iota(jnp.int32, (cin, cin), 0)
    target = lax.broadcasted_iota(jnp.int32, (1, cin), 1)
    part = jnp.where(target < half, core, 1 - core)
    slot = (target & (half - 1)) >> shift
    relative = (slot >> 1) | jnp.where((slot & 1) > 0, far, 0)
    wanted = ((((relative ^ group) << 1) | part) << shift) | (target & (block - 1))
    shuffle = jnp.where(source == wanted, 1.0, 0.0).astype(bf16)
    ordered = jnp.dot(kernel_ref[...], shuffle, preferred_element_type=f32).astype(bf16)
    w_mine_ref[...] = ordered[:, :half].reshape(w_mine_ref.shape)
    w_theirs_ref[...] = ordered[:, half:].reshape(w_theirs_ref.shape)
    filters = bias_ref.shape[1]
    row = lax.broadcasted_iota(jnp.int32, (filters, filters), 0)
    column = lax.broadcasted_iota(jnp.int32, (filters, filters), 1)
    spread = jnp.where(row == column, bias_ref[...].astype(f32), 0.0)
    bias_out_ref[...] = jnp.broadcast_to(
        jnp.sum(spread, axis=1, keepdims=True), bias_out_ref.shape
    )


def assemble(_, own_ref, far_ref, pair_ref, *, block):
    size = own_ref.shape[0]
    pair_ref[:size] = own_ref[...]
    pair_ref[size:] = sort_rows(far_ref[...], block)


def join(*refs):
    in_refs, out_ref = refs[1:-1], refs[-1]
    at = 0
    for ref in in_refs:
        out_ref[at : at + ref.shape[0]] = ref[...]
        at += ref.shape[0]


def channels(refs, per_block, row):
    return jnp.concatenate(
        [ref[k * per_block + row] for ref in refs for k in range(ref.shape[0] // per_block)],
        axis=0,
    )


def windows(rows):
    zero = jnp.zeros_like(rows[0])
    rows = [zero] + rows + [zero]
    return [
        [jnp.concatenate([rows[y + b], rows[y + b + 1]], axis=1) for b in range(3)]
        for y in range(0, len(rows) - 2, 2)
    ]


def products(w_ref, refs, depth, height):
    cells = depth * height
    for z in range(depth):
        taps = [a for a in range(3) if 0 <= z + a - 1 < depth]
        left = jnp.concatenate([w_ref[a * 3 + b] for a in taps for b in range(3)], axis=1)
        views = [
            windows([channels(refs, cells, (z + a - 1) * height + y) for y in range(height)])
            for a in taps
        ]
        for y in range(height // 2):
            right = jnp.concatenate([w for view in views for w in view[y]], axis=0)
            yield z, y, jnp.dot(left, right, preferred_element_type=f32)


def combine(total, k, filters, across):
    part = total[:, k * across : (k + 1) * across]
    lane = lax.broadcasted_iota(jnp.int32, (filters, across), 1)
    left = pltpu.roll(part[:filters], 1, 1)
    right = pltpu.roll(part[2 * filters :], across - 1, 1)
    v = part[filters : 2 * filters]
    v += jnp.where(lane > 0, left, 0.0)
    return v + jnp.where(lane < across - 1, right, 0.0)


def own_parity(w_ref, *refs, depth, height):
    refs, sum_ref = refs[:-1], refs[-1]
    for z, y, total in products(w_ref, refs, depth, height):
        sum_ref[z * (height // 2) + y] = total


def other_parity(w_ref, bias_ref, sum_ref, *refs, depth, height):
    refs, v_ref = refs[:-1], refs[-1]
    filters, across = bias_ref.shape
    for z, y, total in products(w_ref, refs, depth, height):
        total += sum_ref[z * (height // 2) + y]
        for j in range(2):
            v_ref[z * height + 2 * y + j] = combine(total, j, filters, across) + bias_ref[...]


def finish(flags_ref, w_mine_ref, w_theirs_ref, v_ref, *refs, depth, height, count):
    refs, out_ref = refs[:-1], refs[-1]
    filters, across = v_ref.shape[1:]
    extra = 1 if count == 2 else 2
    beside = []
    for which in range(extra):
        tap = 2 * which if extra == 2 else jnp.where(flags_ref[2] > 0, 0, 2)
        left = jnp.concatenate(
            [w[tap * 3 + b] for b in range(3) for w in (w_mine_ref, w_theirs_ref)], axis=1
        )
        rows = [channels(refs, extra * height, which * height + y) for y in range(height)]
        added = []
        for view in windows(rows):
            total = jnp.dot(left, jnp.concatenate(view, axis=0), preferred_element_type=f32)
            added += [combine(total, j, filters, across) for j in range(2)]
        beside.append(added)
    pooled = {}
    for z in range(depth):
        for y in range(height):
            v = v_ref[z * height + y]
            if z == 0:
                v += jnp.where(flags_ref[2] > 0, beside[0][y], 0.0)
            if z == depth - 1:
                v += jnp.where(flags_ref[3] > 0, beside[-1][y], 0.0)
            v = jnp.where(v > 0, v, slope * v)
            key = (z // 2, y // 2)
            pooled[key] = v if key not in pooled else jnp.maximum(pooled[key], v)
    stacked = jnp.concatenate(
        [pooled[z, y] for z in range(depth // 2) for y in range(height // 2)], axis=0
    )
    stacked = jnp.maximum(stacked, pltpu.roll(stacked, across - 1, 1)).astype(bf16)
    cells = (depth // 2) * (height // 2)
    size = cells * filters
    rows_pick = one_hot((size, size), lambda t: (t & (cells - 1)) * filters + t // cells)
    lane_from = lax.broadcasted_iota(jnp.int32, (across, across // 2), 0)
    lane_to = lax.broadcasted_iota(jnp.int32, (across, across // 2), 1)
    lanes_pick = jnp.where(lane_from == 2 * lane_to, 1.0, 0.0).astype(bf16)
    picked = jnp.dot(stacked, lanes_pick, preferred_element_type=f32).astype(bf16)
    out_ref[...] = jnp.dot(rows_pick, picked, preferred_element_type=f32).astype(bf16)


def shifted(x, relative, step, size, count):
    pairs = []
    for f in range(size):
        for s in range(count):
            t = 1 - s if step == "swap" else s + step
            if 0 <= t < count:
                pairs.append((f * count + s, (f ^ (2 * relative)) * count + t))
    return lax.ppermute(x, ("filt", "space"), pairs)


def on_device(volume, kernel, filter_bias):
    block, depth, height, across = volume.shape
    filters, cin = kernel.shape[0], kernel.shape[-1]
    size = lax.axis_size("filt")
    count = lax.axis_size("space")
    here = lax.axis_index("space")
    place = lax.axis_index("filt")
    flags = jnp.stack([place & 1, place >> 1, here, count - 1 - here]).astype(jnp.int32)
    far = size // 4
    pairs = height // 2
    cells = depth * height * block
    beside = height * block
    steps = ["swap"] if count == 2 else [1, -1]
    extra = len(steps)

    vmem = pl.BlockSpec(memory_space=pltpu.VMEM)
    smem = pl.BlockSpec(memory_space=pltpu.SMEM)
    hbm = pl.BlockSpec(memory_space=pltpu.HBM)
    anywhere = pl.BlockSpec(memory_space=pl.ANY)
    shape = jax.ShapeDtypeStruct

    def call(body, outs, ins, args, scratch=(), cost=12):
        return pl.pallas_call(
            body,
            out_shape=outs,
            in_specs=ins,
            out_specs=jax.tree.map(lambda _: vmem, outs),
            scratch_shapes=scratch,
            compiler_params=pltpu.CompilerParams(vmem_limit_bytes=16 << 20),
            cost_estimate=pl.CostEstimate(flops=1 << cost, bytes_accessed=1 << 8, transcendentals=0),
        )(*args)

    far_block = shifted(volume, far, 0, size, count)
    weights = kernel.transpose(1, 2, 3, 0, 4).reshape(-1, cin)
    given = [volume.reshape(cells, across), weights, filter_bias[None]]
    own_block, *edges, weights, bias = call(
        functools.partial(begin, block=block, depth=depth, count=count),
        [shape((cells, across), bf16)]
        + [shape((beside, across), bf16)] * extra
        + [shape(weights.shape, bf16), shape((1, filters), bf16)],
        [smem, hbm, hbm, hbm],
        [flags] + [pltpu.with_memory_space_constraint(x, pltpu.HBM) for x in given],
        [pltpu.VMEM((cells, across), bf16), pltpu.SemaphoreType.DMA((3,))],
    )
    sends = list(zip(edges, steps))
    far_planes = [shifted(x, far, step, size, count) for x, step in sends]
    own_planes = [shifted(x, 0, step, size, count) for x, step in sends]
    ordered = shape((9, 3 * filters, cin // 2), bf16)
    w_mine, w_theirs, bias = call(
        functools.partial(prepare, block=block),
        (ordered, ordered, shape((filters, across), f32)),
        [smem, vmem, vmem],
        (flags, weights, bias),
        cost=31,
    )

    pair = call(
        functools.partial(assemble, block=block),
        shape((2 * cells, across), bf16),
        [anywhere, vmem, vmem],
        (w_mine, own_block, far_block.reshape(cells, across)),
        cost=31,
    )
    planes = call(
        join,
        shape((2 * extra * beside, across), bf16),
        [anywhere] + [vmem] * (2 * extra),
        [pair] + own_planes + far_planes,
        cost=31,
    )

    def near(x):
        parts = [x] + [shifted(x, r, 0, size, count) for r in range(1, far)]
        return [part.reshape(-1, block, across) for part in parts]

    def swapped(x):
        return lax.ppermute(x, "filt", [(i, i ^ 1) for i in range(size)])

    mine = near(pair)
    theirs = [swapped(jnp.concatenate(mine[k : k + far // 2], axis=0)) for k in (0, far // 2)]
    dims = dict(depth=depth, height=height)
    partial = call(
        functools.partial(own_parity, **dims),
        shape((depth * pairs, 3 * filters, 2 * across), f32),
        [vmem] * (1 + far),
        [w_mine] + mine,
        cost=28,
    )
    again = call(join, shape(planes.shape, bf16), [anywhere, vmem], (mine[1], planes), cost=12)
    behind = [shifted(planes, r, 0, size, count) for r in range(2, far)]
    behind = [planes, shifted(again, 1, 0, size, count)] + behind
    planes = call(
        join,
        shape((far * planes.shape[0], across), bf16),
        [anywhere] + [vmem] * far,
        [partial] + behind,
    ).reshape(-1, block, across)
    v = call(
        functools.partial(other_parity, **dims),
        shape((depth * height, filters, across), f32),
        [vmem] * 5,
        [w_theirs, bias, partial] + theirs,
    )
    pooled = call(
        functools.partial(finish, count=count, **dims),
        shape((filters * depth * height // 4, across // 2), bf16),
        [smem] + [vmem] * 5,
        (flags, w_mine, w_theirs, v, planes, swapped(planes)),
    )
    return pooled.reshape(filters, depth // 2, height // 2, across // 2)


def solution(mesh):
    in_specs = (P("filt", "space", None, None), P("filt", None, None, None, None), P("filt"))
    out_specs = P("filt", "space", None, None)
    return jax.shard_map(
        on_device, mesh=mesh, in_specs=in_specs, out_specs=out_specs, check_vma=False
    )
```

time: 26.8 us -> 29.2 us (1.090)
  starting transfers between devices: 9.29 us -> 14.8 us
  local copies, waits for them, and re-layouts: 2.51 us -> 0 us
  waiting for transfers between devices: 9.01 us -> 7.96 us
  Pallas kernels: 5.68 us -> 6.1 us
    ppermute x6 -> x9, starting transfers between devices: 9.15 us -> 14.5 us  [shifted(): return lax.ppermute(x, ('filt', 'space'), pairs)]
    unnamed x6 -> x0, local copies, waits for them, and re-layouts: 2.51 us -> none
    ppermute x6 -> x9, waiting for transfers between devices: 8.86 us -> 7.51 us  [shifted(): return lax.ppermute(x, ('filt', 'space'), pairs)]
    pallas_call x7 -> x9, Pallas kernels: 5.68 us -> 6.1 us  [call(): pl.pallas_call(body, out_shape=outs, in_specs=ins, out_specs=jax.tree.map...]
    ppermute x2 -> x3, waiting for transfers between devices: 0.15 us -> 0.45 us  [swapped(): return lax.ppermute(x, 'filt', [(i, i ^ 1) for i in range(size)])]
  transfers between devices with their start and end apart: 8 -> 12, of which waited for: 6 -> 8; matrix products, arithmetic and copies ran while one was open for 0% -> 0% of each run, Pallas kernels for 11% -> 14%
where the time goes in v5:
time: 29.2 us; the launch traced here: 29 us
  starting transfers between devices  14.8 us (51%)
  waiting for transfers between devices  7.96 us (27%)
  Pallas kernels  6.1 us (21%)
    ppermute x9, starting transfers between devices, shifted(): return lax.ppermute(x, ('filt', 'space'), pairs)  14.5 us
    ppermute x9, waiting for transfers between devices, shifted(): return lax.ppermute(x, ('filt', 'space'), pairs)  7.51 us
    pallas_call x9, Pallas kernels, call(): pl.pallas_call(body, out_shape=outs, in_specs=ins, out_specs=jax.tree.map...  6.1 us
  transfers between devices with their start and end apart: 12, of which 8 were waited for; matrix products, arithmetic and copies ran while one was open for 0% of the time, Pallas kernels for 14%

profile of v5, /device:TPU:0, one launch (start us, length us, event | category | flops | bytes accessed | tf_op | source)
XLA Modules:
  0.0 29.0 jit_solution(16052106769077345473)
XLA Ops:
  0.0 4.0 %collective-permute-start = (bf16[16,4,4,128]{3,2,1,0:T(4,128)(2,1)}, bf16[16,4,4,128]{3,2,1,0:T(4,128)(2,1)S(1)}, u32[]{:S(2)}, u32[]{:S(2)}) collective-permute-start(bf16[16,4,4,128]{3,2,1,0:T(4,128)(2,1)} %param.3), channel_id=1, source_target_pairs={{0,16},{1,17},{2,18},{3,19},{4,20},{5,21},{6,22},{7,23},{8,24},{9,... | collective-permute-start | bytes 196616 | tf_op jit(solution)/shard_map/ppermute | solution.py:192
  4.0 0.1 pad_add_fusion.flags_ref
  4.1 1.6 %shard_map.37 = (bf16[256,128]{1,0:T(8,128)(2,1)S(1)}, bf16[64,128]{1,0:T(8,128)(2,1)S(1)}, bf16[864,256]{1,0:T(8,128)(2,1)S(1)}, bf16[1,32]{1,0:T(2,128)(2,1)S(1)}) custom-call(s32[4]{0:T(128)S(1)} %pad_add_fusion.flags_ref, bf16[256,128]{1,0:T(8,128)(2,1)} %bitcast.29, bf16[864,256]{1,0:T(8,128)(2,1)} %bitcast.28, bf16[1,32]{1,0:T(2,128)(2,1)} %bitcast.30), custom_call_target="tpu_custom_call" | custom-call | flops 4096 | bytes 256 | tf_op jit(solution)/shard_map/pallas_call | solution.py:217
  5.7 0.8 %shard_map.38 = (bf16[9,96,128]{2,1,0:T(8,128)(2,1)S(1)}, bf16[9,96,128]{2,1,0:T(8,128)(2,1)S(1)}, f32[32,128]{1,0:T(8,128)S(1)}) custom-call(s32[4]{0:T(128)S(1)} %pad_add_fusion.flags_ref, bf16[864,256]{1,0:T(8,128)(2,1)S(1)} %get-tuple-element.12.kernel_ref, bf16[1,32]{1,0:T(2,128)(2,1)S(1)} %get-tuple-element.13.bias_ref), custom_call_target="tpu_custom_call" | custom-call | flops 2147483648 | bytes 256 | tf_op jit(solution)/shard_map/pallas_call | solution.py:217
  6.6 1.3 %collective-permute-done = bf16[16,4,4,128]{3,2,1,0:T(4,128)(2,1)S(1)} collective-permute-done((bf16[16,4,4,128]{3,2,1,0:T(4,128)(2,1)}, bf16[16,4,4,128]{3,2,1,0:T(4,128)(2,1)S(1)}, u32[]{:S(2)}, u32[]{:S(2)}) %collective-permute-start) | collective-permute-done | bytes 65568 | tf_op jit(solution)/shard_map/ppermute | solution.py:192
  7.9 0.2 shard_map.39.refs_0_
  8.1 0.7 %collective-permute-start.2 = (bf16[512,128]{1,0:T(8,128)(2,1)S(1)}, bf16[512,128]{1,0:T(8,128)(2,1)S(1)}, u32[]{:S(2)}, u32[]{:S(2)}) collective-permute-start(bf16[512,128]{1,0:T(8,128)(2,1)S(1)} %shard_map.39.refs_0_), channel_id=1, source_target_pairs={{0,8},{1,9},{2,10},{3,11},{4,12},{5,13},{6,14},{7,15},{8,0},{9,1},... | collective-permute-start | bytes 393224 | tf_op jit(solution)/shard_map/ppermute | solution.py:192
  8.8 2.5 %collective-permute-start.3 = (bf16[512,128]{1,0:T(8,128)(2,1)S(1)}, bf16[512,128]{1,0:T(8,128)(2,1)S(1)}, u32[]{:S(2)}, u32[]{:S(2)}) collective-permute-start(bf16[512,128]{1,0:T(8,128)(2,1)S(1)} %shard_map.39.refs_0_), channel_id=1, source_target_pairs={{0,12},{1,13},{2,14},{3,15},{4,8},{5,9},{6,10},{7,11},{8,4},{9,5},... | collective-permute-start | bytes 393224 | tf_op jit(solution)/shard_map/ppermute | solution.py:192
  11.3 0.3 %collective-permute-start.1 = (bf16[512,128]{1,0:T(8,128)(2,1)S(1)}, bf16[512,128]{1,0:T(8,128)(2,1)S(1)}, u32[]{:S(2)}, u32[]{:S(2)}) collective-permute-start(bf16[512,128]{1,0:T(8,128)(2,1)S(1)} %shard_map.39.refs_0_), channel_id=1, source_target_pairs={{0,4},{1,5},{2,6},{3,7},{4,0},{5,1},{6,2},{7,3},{8,12},{9,13},{10,... | collective-permute-start | bytes 393224 | tf_op jit(solution)/shard_map/ppermute | solution.py:192
  11.6 1.7 %collective-permute-start.6 = (bf16[64,128]{1,0:T(8,128)(2,1)S(1)}, bf16[64,128]{1,0:T(8,128)(2,1)S(1)}, u32[]{:S(2)}, u32[]{:S(2)}) collective-permute-start(bf16[64,128]{1,0:T(8,128)(2,1)S(1)} %get-tuple-element.18), channel_id=1, source_target_pairs={{0,1},{1,0},{2,3},{3,2},{4,5},{5,4},{6,7},{7,6},{8,9},{9,8},{10,11... | collective-permute-start | bytes 49160 | tf_op jit(solution)/shard_map/ppermute | solution.py:192
  13.3 1.8 %collective-permute-start.7 = (bf16[64,128]{1,0:T(8,128)(2,1)S(1)}, bf16[64,128]{1,0:T(8,128)(2,1)S(1)}, u32[]{:S(2)}, u32[]{:S(2)}) collective-permute-start(bf16[64,128]{1,0:T(8,128)(2,1)S(1)} %get-tuple-element.18), channel_id=1, source_target_pairs={{0,17},{1,16},{2,19},{3,18},{4,21},{5,20},{6,23},{7,22},{8,25},{9,... | collective-permute-start | bytes 49160 | tf_op jit(solution)/shard_map/ppermute | solution.py:192
  15.1 0.8 %collective-permute-done.3 = bf16[512,128]{1,0:T(8,128)(2,1)S(1)} collective-permute-done((bf16[512,128]{1,0:T(8,128)(2,1)S(1)}, bf16[512,128]{1,0:T(8,128)(2,1)S(1)}, u32[]{:S(2)}, u32[]{:S(2)}) %collective-permute-start.3) | collective-permute-done | bytes 131104 | tf_op jit(solution)/shard_map/ppermute | solution.py:192
  16.0 1.2 %collective-permute-done.1 = bf16[512,128]{1,0:T(8,128)(2,1)S(1)} collective-permute-done((bf16[512,128]{1,0:T(8,128)(2,1)S(1)}, bf16[512,128]{1,0:T(8,128)(2,1)S(1)}, u32[]{:S(2)}, u32[]{:S(2)}) %collective-permute-start.1) | collective-permute-done | bytes 131104 | tf_op jit(solution)/shard_map/ppermute | solution.py:192
  17.3 1.6 %collective-permute-done.7.refs_2_ = bf16[64,128]{1,0:T(8,128)(2,1)S(1)} collective-permute-done((bf16[64,128]{1,0:T(8,128)(2,1)S(1)}, bf16[64,128]{1,0:T(8,128)(2,1)S(1)}, u32[]{:S(2)}, u32[]{:S(2)}) %collective-permute-start.7) | collective-permute-done | bytes 16416 | tf_op jit(solution)/shard_map/ppermute | solution.py:192
  18.9 1.7 %collective-permute-start.10 = (bf16[128,128]{1,0:T(8,128)(2,1)S(1)}, bf16[128,128]{1,0:T(8,128)(2,1)S(1)}, u32[]{:S(2)}, u32[]{:S(2)}) collective-permute-start(bf16[128,128]{1,0:T(8,128)(2,1)S(1)} %shard_map.42.refs_1_), channel_id=1, source_target_pairs={{0,12},{1,13},{2,14},{3,15},{4,8},{5,9},{6,10},{7,11},{8,4},{9,5},... | collective-permute-start | bytes 98312 | tf_op jit(solution)/shard_map/ppermute | solution.py:192
  20.6 1.3 %collective-permute-start.9 = (bf16[128,128]{1,0:T(8,128)(2,1)S(1)}, bf16[128,128]{1,0:T(8,128)(2,1)S(1)}, u32[]{:S(2)}, u32[]{:S(2)}) collective-permute-start(bf16[128,128]{1,0:T(8,128)(2,1)S(1)} %shard_map.42.refs_1_), channel_id=1, source_target_pairs={{0,8},{1,9},{2,10},{3,11},{4,12},{5,13},{6,14},{7,15},{8,0},{9,1},... | collective-permute-start | bytes 98312 | tf_op jit(solution)/shard_map/ppermute | solution.py:192
  21.9 0.5 %collective-permute-start.8 = (bf16[128,128]{1,0:T(8,128)(2,1)S(1)}, bf16[128,128]{1,0:T(8,128)(2,1)S(1)}, u32[]{:S(2)}, u32[]{:S(2)}) collective-permute-start(bf16[128,128]{1,0:T(8,128)(2,1)S(1)} %shard_map.43), channel_id=1, source_target_pairs={{0,4},{1,5},{2,6},{3,7},{4,0},{5,1},{6,2},{7,3},{8,12},{9,13},{10,... | collective-permute-start | bytes 98312 | tf_op jit(solution)/shard_map/ppermute | solution.py:192
  22.4 0.8 %shard_map.40.sum_ref.refs_0_ = f32[8,96,256]{2,1,0:T(8,128)S(1)} custom-call(bf16[9,96,128]{2,1,0:T(8,128)(2,1)S(1)} %get-tuple-element.14._.w_ref.w_mine_ref, bf16[32,16,128]{2,1,0:T(8,128)(2,1)S(1)} %bitcast.20, bf16[32,16,128]{2,1,0:T(8,128)(2,1)S(1)} %bitcast.18, bf16[32,16,128]{2,1,0:T(8,128)(2,1)S(1)} %bitcast.22, bf16[32,16,128]{2,1,0:T(8,128)(2,1)S(1)} %bitcast.24), custom_call_target="tpu_custom_call" | custom-call | flops 268435456 | bytes 256 | tf_op jit(solution)/shard_map/pallas_call | solution.py:217
  23.2 0.5 %collective-permute-done.10.refs_4_ = bf16[128,128]{1,0:T(8,128)(2,1)S(1)} collective-permute-done((bf16[128,128]{1,0:T(8,128)(2,1)S(1)}, bf16[128,128]{1,0:T(8,128)(2,1)S(1)}, u32[]{:S(2)}, u32[]{:S(2)}) %collective-permute-start.10) | collective-permute-done | bytes 32800 | tf_op jit(solution)/shard_map/ppermute | solution.py:192
  23.7 0.8 %collective-permute-done.9.refs_3_ = bf16[128,128]{1,0:T(8,128)(2,1)S(1)} collective-permute-done((bf16[128,128]{1,0:T(8,128)(2,1)S(1)}, bf16[128,128]{1,0:T(8,128)(2,1)S(1)}, u32[]{:S(2)}, u32[]{:S(2)}) %collective-permute-start.9) | collective-permute-done | bytes 32800 | tf_op jit(solution)/shard_map/ppermute | solution.py:192
  24.5 1.3 %collective-permute-done.8.refs_2_ = bf16[128,128]{1,0:T(8,128)(2,1)S(1)} collective-permute-done((bf16[128,128]{1,0:T(8,128)(2,1)S(1)}, bf16[128,128]{1,0:T(8,128)(2,1)S(1)}, u32[]{:S(2)}, u32[]{:S(2)}) %collective-permute-start.8) | collective-permute-done | bytes 32800 | tf_op jit(solution)/shard_map/ppermute | solution.py:192
  25.9 0.9 %shard_map.41.v_ref = f32[16,32,128]{2,1,0:T(8,128)S(1)} custom-call(bf16[9,96,128]{2,1,0:T(8,128)(2,1)S(1)} %get-tuple-element.15.w_ref.w_theirs_ref, f32[32,128]{1,0:T(8,128)S(1)} %get-tuple-element.16.bias_ref, f32[8,96,256]{2,1,0:T(8,128)S(1)} %shard_map.40.sum_ref.refs_0_, bf16[64,16,128]{2,1,0:T(8,128)(2,1)S(1)} %collective-permute-done.4.refs_0_, ...), custom_call_target="tpu_custom_call" | custom-call | flops 4096 | bytes 256 | tf_op jit(solution)/shard_map/pallas_call | solution.py:217
  26.8 0.4 %collective-permute-done.11.refs_1_ = bf16[32,16,128]{2,1,0:T(8,128)(2,1)S(1)} collective-permute-done((bf16[32,16,128]{2,1,0:T(8,128)(2,1)S(1)}, bf16[32,16,128]{2,1,0:T(8,128)(2,1)S(1)}, u32[]{:S(2)}, u32[]{:S(2)}) %collective-permute-start.11) | collective-permute-done | bytes 131104 | tf_op jit(solution)/shard_map/ppermute | solution.py:271
  27.2 1.8 %shard_map.45 = bf16[128,64]{1,0:T(8,128)(2,1)} custom-call(s32[4]{0:T(128)S(1)} %pad_add_fusion.flags_ref, bf16[9,96,128]{2,1,0:T(8,128)(2,1)S(1)} %get-tuple-element.14._.w_ref.w_mine_ref, bf16[9,96,128]{2,1,0:T(8,128)(2,1)S(1)} %get-tuple-element.15.w_ref.w_theirs_ref, f32[16,32,128]{2,1,0:T(8,128)S(1)} %shard_map.41.v_ref, ...), custom_call_target="tpu_custom_call" | custom-call | flops 4096 | bytes 256 | tf_op jit(solution)/shard_map/pallas_call | solution.py:217
  (12 shorter events, 0.3 us)
Async XLA Ops:
  0.0 7.9 %collective-permute-start = (bf16[16,4,4,128]{3,2,1,0:T(4,128)(2,1)}, bf16[16,4,4,128]{3,2,1,0:T(4,128)(2,1)S(1)}, u32[]{:S(2)}, u32[]{:S(2)}) collective-permute-start(bf16[16,4,4,128]{3,2,1,0:T(4,128)(2,1)} %param.3), channel_id=1, source_target_pairs={{0,16},{1,17},{2,18},{3,19},{4,20},{5,21},{6,22},{7,23},{8,24},{9,... | collective-permute-start | bytes 196616 | tf_op jit(solution)/shard_map/ppermute | solution.py:192
  8.1 7.0 %collective-permute-start.2 = (bf16[512,128]{1,0:T(8,128)(2,1)S(1)}, bf16[512,128]{1,0:T(8,128)(2,1)S(1)}, u32[]{:S(2)}, u32[]{:S(2)}) collective-permute-start(bf16[512,128]{1,0:T(8,128)(2,1)S(1)} %shard_map.39.refs_0_), channel_id=1, source_target_pairs={{0,8},{1,9},{2,10},{3,11},{4,12},{5,13},{6,14},{7,15},{8,0},{9,1},... | collective-permute-start | bytes 393224 | tf_op jit(solution)/shard_map/ppermute | solution.py:192
  8.8 7.0 %collective-permute-start.3 = (bf16[512,128]{1,0:T(8,128)(2,1)S(1)}, bf16[512,128]{1,0:T(8,128)(2,1)S(1)}, u32[]{:S(2)}, u32[]{:S(2)}) collective-permute-start(bf16[512,128]{1,0:T(8,128)(2,1)S(1)} %shard_map.39.refs_0_), channel_id=1, source_target_pairs={{0,12},{1,13},{2,14},{3,15},{4,8},{5,9},{6,10},{7,11},{8,4},{9,5},... | collective-permute-start | bytes 393224 | tf_op jit(solution)/shard_map/ppermute | solution.py:192
  11.3 5.8 %collective-permute-start.1 = (bf16[512,128]{1,0:T(8,128)(2,1)S(1)}, bf16[512,128]{1,0:T(8,128)(2,1)S(1)}, u32[]{:S(2)}, u32[]{:S(2)}) collective-permute-start(bf16[512,128]{1,0:T(8,128)(2,1)S(1)} %shard_map.39.refs_0_), channel_id=1, source_target_pairs={{0,4},{1,5},{2,6},{3,7},{4,0},{5,1},{6,2},{7,3},{8,12},{9,13},{10,... | collective-permute-start | bytes 393224 | tf_op jit(solution)/shard_map/ppermute | solution.py:192
  11.6 5.7 %collective-permute-start.6 = (bf16[64,128]{1,0:T(8,128)(2,1)S(1)}, bf16[64,128]{1,0:T(8,128)(2,1)S(1)}, u32[]{:S(2)}, u32[]{:S(2)}) collective-permute-start(bf16[64,128]{1,0:T(8,128)(2,1)S(1)} %get-tuple-element.18), channel_id=1, source_target_pairs={{0,1},{1,0},{2,3},{3,2},{4,5},{5,4},{6,7},{7,6},{8,9},{9,8},{10,11... | collective-permute-start | bytes 49160 | tf_op jit(solution)/shard_map/ppermute | solution.py:192
  13.3 5.5 %collective-permute-start.7 = (bf16[64,128]{1,0:T(8,128)(2,1)S(1)}, bf16[64,128]{1,0:T(8,128)(2,1)S(1)}, u32[]{:S(2)}, u32[]{:S(2)}) collective-permute-start(bf16[64,128]{1,0:T(8,128)(2,1)S(1)} %get-tuple-element.18), channel_id=1, source_target_pairs={{0,17},{1,16},{2,19},{3,18},{4,21},{5,20},{6,23},{7,22},{8,25},{9,... | collective-permute-start | bytes 49160 | tf_op jit(solution)/shard_map/ppermute | solution.py:192
  15.9 10.0 %collective-permute-start.5 = (bf16[64,16,128]{2,1,0:T(8,128)(2,1)S(1)}, bf16[64,16,128]{2,1,0:T(8,128)(2,1)S(1)}, u32[]{:S(2)}, u32[]{:S(2)}) collective-permute-start(bf16[64,16,128]{2,1,0:T(8,128)(2,1)S(1)} %pad_maximum_fusion.1), channel_id=1, source_target_pairs={{0,2},{2,0},{4,6},{6,4},{8,10},{10,8},{12,14},{14,12},{16,18},{18,... | collective-permute-start | bytes 786440 | tf_op jit(solution)/shard_map/ppermute | solution.py:271
  17.2 8.7 %collective-permute-start.4 = (bf16[64,16,128]{2,1,0:T(8,128)(2,1)S(1)}, bf16[64,16,128]{2,1,0:T(8,128)(2,1)S(1)}, u32[]{:S(2)}, u32[]{:S(2)}) collective-permute-start(bf16[64,16,128]{2,1,0:T(8,128)(2,1)S(1)} %pad_maximum_fusion), channel_id=1, source_target_pairs={{0,2},{2,0},{4,6},{6,4},{8,10},{10,8},{12,14},{14,12},{16,18},{18,... | collective-permute-start | bytes 786440 | tf_op jit(solution)/shard_map/ppermute | solution.py:271
  18.9 4.8 %collective-permute-start.10 = (bf16[128,128]{1,0:T(8,128)(2,1)S(1)}, bf16[128,128]{1,0:T(8,128)(2,1)S(1)}, u32[]{:S(2)}, u32[]{:S(2)}) collective-permute-start(bf16[128,128]{1,0:T(8,128)(2,1)S(1)} %shard_map.42.refs_1_), channel_id=1, source_target_pairs={{0,12},{1,13},{2,14},{3,15},{4,8},{5,9},{6,10},{7,11},{8,4},{9,5},... | collective-permute-start | bytes 98312 | tf_op jit(solution)/shard_map/ppermute | solution.py:192
  20.6 3.9 %collective-permute-start.9 = (bf16[128,128]{1,0:T(8,128)(2,1)S(1)}, bf16[128,128]{1,0:T(8,128)(2,1)S(1)}, u32[]{:S(2)}, u32[]{:S(2)}) collective-permute-start(bf16[128,128]{1,0:T(8,128)(2,1)S(1)} %shard_map.42.refs_1_), channel_id=1, source_target_pairs={{0,8},{1,9},{2,10},{3,11},{4,12},{5,13},{6,14},{7,15},{8,0},{9,1},... | collective-permute-start | bytes 98312 | tf_op jit(solution)/shard_map/ppermute | solution.py:192
  21.9 3.9 %collective-permute-start.8 = (bf16[128,128]{1,0:T(8,128)(2,1)S(1)}, bf16[128,128]{1,0:T(8,128)(2,1)S(1)}, u32[]{:S(2)}, u32[]{:S(2)}) collective-permute-start(bf16[128,128]{1,0:T(8,128)(2,1)S(1)} %shard_map.43), channel_id=1, source_target_pairs={{0,4},{1,5},{2,6},{3,7},{4,0},{5,1},{6,2},{7,3},{8,12},{9,13},{10,... | collective-permute-start | bytes 98312 | tf_op jit(solution)/shard_map/ppermute | solution.py:192
  25.8 1.4 %collective-permute-start.11 = (bf16[32,16,128]{2,1,0:T(8,128)(2,1)S(1)}, bf16[32,16,128]{2,1,0:T(8,128)(2,1)S(1)}, u32[]{:S(2)}, u32[]{:S(2)}) collective-permute-start(bf16[32,16,128]{2,1,0:T(8,128)(2,1)S(1)} %bitcast.25), channel_id=1, source_target_pairs={{0,2},{2,0},{4,6},{6,4},{8,10},{10,8},{12,14},{14,12},{16,18},{18,... | collective-permute-start | bytes 393224 | tf_op jit(solution)/shard_map/ppermute | solution.py:271

commit v6 on v5

--- a/solution.py
+++ b/solution.py
@@ -271,7 +271,7 @@
         return lax.ppermute(x, "filt", [(i, i ^ 1) for i in range(size)])
 
     mine = near(pair)
-    theirs = [swapped(jnp.concatenate(mine[k : k + far // 2], axis=0)) for k in (0, far // 2)]
+    theirs = [swapped(x) for x in mine]
     dims = dict(depth=depth, height=height)
     partial = call(
         functools.partial(own_parity, **dims),
@@ -292,7 +292,7 @@
     v = call(
         functools.partial(other_parity, **dims),
         shape((depth * height, filters, across), f32),
-        [vmem] * 5,
+        [vmem] * (3 + far),
         [w_theirs, bias, partial] + theirs,
     )
     pooled = call(

time: 29.2 us -> 23.9 us (0.82)
  waiting for transfers between devices: 7.96 us -> 3.69 us
  starting transfers between devices: 14.8 us -> 13.8 us
    ppermute x9, waiting for transfers between devices: 7.51 us -> 2.93 us  [shifted(): return lax.ppermute(x, ('filt', 'space'), pairs)]
    ppermute x9, starting transfers between devices: 14.5 us -> 12.7 us  [shifted(): return lax.ppermute(x, ('filt', 'space'), pairs)]
    ppermute x3 -> x5, starting transfers between devices: 0.21 us -> 1.11 us  [swapped(): return lax.ppermute(x, 'filt', [(i, i ^ 1) for i in range(size)])]
    ppermute x3 -> x5, waiting for transfers between devices: 0.45 us -> 0.76 us  [swapped(): return lax.ppermute(x, 'filt', [(i, i ^ 1) for i in range(size)])]
  transfers between devices with their start and end apart: 12 -> 14, of which waited for: 8 -> 6; matrix products, arithmetic and copies ran while one was open for 0% -> 0% of each run, Pallas kernels for 14% -> 18%
where the time goes in v6:
time: 23.9 us; the launch traced here: 23.8 us
  starting transfers between devices  13.8 us (58%)
  Pallas kernels  6.1 us (26%)
  waiting for transfers between devices  3.69 us (15%)
    ppermute x9, starting transfers between devices, shifted(): return lax.ppermute(x, ('filt', 'space'), pairs)  12.7 us
    pallas_call x9, Pallas kernels, call(): pl.pallas_call(body, out_shape=outs, in_specs=ins, out_specs=jax.tree.map...  6.1 us
    ppermute x9, waiting for transfers between devices, shifted(): return lax.ppermute(x, ('filt', 'space'), pairs)  2.93 us
    ppermute x5, starting transfers between devices, swapped(): return lax.ppermute(x, 'filt', [(i, i ^ 1) for i in range(size)])  1.11 us
    ppermute x5, waiting for transfers between devices, swapped(): return lax.ppermute(x, 'filt', [(i, i ^ 1) for i in range(size)])  0.76 us
  transfers between devices with their start and end apart: 14, of which 6 were waited for; matrix products, arithmetic and copies ran while one was open for 0% of the time, Pallas kernels for 18%

profile of v6, /device:TPU:0, one launch (start us, length us, event | category | flops | bytes accessed | tf_op | source)
XLA Modules:
  0.0 23.8 jit_solution(7536693636388450282)
XLA Ops:
  0.0 4.0 %collective-permute-start = (bf16[16,4,4,128]{3,2,1,0:T(4,128)(2,1)}, bf16[16,4,4,128]{3,2,1,0:T(4,128)(2,1)S(1)}, u32[]{:S(2)}, u32[]{:S(2)}) collective-permute-start(bf16[16,4,4,128]{3,2,1,0:T(4,128)(2,1)} %param.3), channel_id=1, source_target_pairs={{0,16},{1,17},{2,18},{3,19},{4,20},{5,21},{6,22},{7,23},{8,24},{9,... | collective-permute-start | bytes 196616 | tf_op jit(solution)/shard_map/ppermute | solution.py:192
  4.0 0.1 pad_add_fusion.flags_ref
  4.1 1.6 %shard_map.37 = (bf16[256,128]{1,0:T(8,128)(2,1)S(1)}, bf16[64,128]{1,0:T(8,128)(2,1)S(1)}, bf16[864,256]{1,0:T(8,128)(2,1)S(1)}, bf16[1,32]{1,0:T(2,128)(2,1)S(1)}) custom-call(s32[4]{0:T(128)S(1)} %pad_add_fusion.flags_ref, bf16[256,128]{1,0:T(8,128)(2,1)} %bitcast.29, bf16[864,256]{1,0:T(8,128)(2,1)} %bitcast.28, bf16[1,32]{1,0:T(2,128)(2,1)} %bitcast.30), custom_call_target="tpu_custom_call" | custom-call | flops 4096 | bytes 256 | tf_op jit(solution)/shard_map/pallas_call | solution.py:217
  5.7 1.6 %collective-permute-start.8 = (bf16[64,128]{1,0:T(8,128)(2,1)S(1)}, bf16[64,128]{1,0:T(8,128)(2,1)S(1)}, u32[]{:S(2)}, u32[]{:S(2)}) collective-permute-start(bf16[64,128]{1,0:T(8,128)(2,1)S(1)} %get-tuple-element.18), channel_id=1, source_target_pairs={{0,1},{1,0},{2,3},{3,2},{4,5},{5,4},{6,7},{7,6},{8,9},{9,8},{10,11... | collective-permute-start | bytes 49160 | tf_op jit(solution)/shard_map/ppermute | solution.py:192
  7.3 0.8 %shard_map.38 = (bf16[9,96,128]{2,1,0:T(8,128)(2,1)S(1)}, bf16[9,96,128]{2,1,0:T(8,128)(2,1)S(1)}, f32[32,128]{1,0:T(8,128)S(1)}) custom-call(s32[4]{0:T(128)S(1)} %pad_add_fusion.flags_ref, bf16[864,256]{1,0:T(8,128)(2,1)S(1)} %get-tuple-element.12.kernel_ref, bf16[1,32]{1,0:T(2,128)(2,1)S(1)} %get-tuple-element.13.bias_ref), custom_call_target="tpu_custom_call" | custom-call | flops 2147483648 | bytes 256 | tf_op jit(solution)/shard_map/pallas_call | solution.py:217
  8.1 0.2 shard_map.39.refs_0_
  8.3 1.9 %collective-permute-start.1 = (bf16[512,128]{1,0:T(8,128)(2,1)S(1)}, bf16[512,128]{1,0:T(8,128)(2,1)S(1)}, u32[]{:S(2)}, u32[]{:S(2)}) collective-permute-start(bf16[512,128]{1,0:T(8,128)(2,1)S(1)} %shard_map.39.refs_0_), channel_id=1, source_target_pairs={{0,4},{1,5},{2,6},{3,7},{4,0},{5,1},{6,2},{7,3},{8,12},{9,13},{10,... | collective-permute-start | bytes 393224 | tf_op jit(solution)/shard_map/ppermute | solution.py:192
  10.2 1.6 %collective-permute-start.2 = (bf16[512,128]{1,0:T(8,128)(2,1)S(1)}, bf16[512,128]{1,0:T(8,128)(2,1)S(1)}, u32[]{:S(2)}, u32[]{:S(2)}) collective-permute-start(bf16[512,128]{1,0:T(8,128)(2,1)S(1)} %shard_map.39.refs_0_), channel_id=1, source_target_pairs={{0,8},{1,9},{2,10},{3,11},{4,12},{5,13},{6,14},{7,15},{8,0},{9,1},... | collective-permute-start | bytes 393224 | tf_op jit(solution)/shard_map/ppermute | solution.py:192
  11.8 0.1 collective-permute-start.3
  11.9 1.1 %collective-permute-done.9.refs_2_ = bf16[64,128]{1,0:T(8,128)(2,1)S(1)} collective-permute-done((bf16[64,128]{1,0:T(8,128)(2,1)S(1)}, bf16[64,128]{1,0:T(8,128)(2,1)S(1)}, u32[]{:S(2)}, u32[]{:S(2)}) %collective-permute-start.9) | collective-permute-done | bytes 16416 | tf_op jit(solution)/shard_map/ppermute | solution.py:192
  12.9 1.5 %collective-permute-start.11 = (bf16[128,128]{1,0:T(8,128)(2,1)S(1)}, bf16[128,128]{1,0:T(8,128)(2,1)S(1)}, u32[]{:S(2)}, u32[]{:S(2)}) collective-permute-start(bf16[128,128]{1,0:T(8,128)(2,1)S(1)} %shard_map.42.refs_1_), channel_id=1, source_target_pairs={{0,8},{1,9},{2,10},{3,11},{4,12},{5,13},{6,14},{7,15},{8,0},{9,1},... | collective-permute-start | bytes 98312 | tf_op jit(solution)/shard_map/ppermute | solution.py:192
  14.4 1.5 %collective-permute-start.12 = (bf16[128,128]{1,0:T(8,128)(2,1)S(1)}, bf16[128,128]{1,0:T(8,128)(2,1)S(1)}, u32[]{:S(2)}, u32[]{:S(2)}) collective-permute-start(bf16[128,128]{1,0:T(8,128)(2,1)S(1)} %shard_map.42.refs_1_), channel_id=1, source_target_pairs={{0,12},{1,13},{2,14},{3,15},{4,8},{5,9},{6,10},{7,11},{8,4},{9,5},... | collective-permute-start | bytes 98312 | tf_op jit(solution)/shard_map/ppermute | solution.py:192
  15.9 0.6 %collective-permute-start.10 = (bf16[128,128]{1,0:T(8,128)(2,1)S(1)}, bf16[128,128]{1,0:T(8,128)(2,1)S(1)}, u32[]{:S(2)}, u32[]{:S(2)}) collective-permute-start(bf16[128,128]{1,0:T(8,128)(2,1)S(1)} %shard_map.43), channel_id=1, source_target_pairs={{0,4},{1,5},{2,6},{3,7},{4,0},{5,1},{6,2},{7,3},{8,12},{9,13},{10,... | collective-permute-start | bytes 98312 | tf_op jit(solution)/shard_map/ppermute | solution.py:192
  16.5 0.1 collective-permute-done.2
  16.6 1.7 %collective-permute-done.3 = bf16[512,128]{1,0:T(8,128)(2,1)S(1)} collective-permute-done((bf16[512,128]{1,0:T(8,128)(2,1)S(1)}, bf16[512,128]{1,0:T(8,128)(2,1)S(1)}, u32[]{:S(2)}, u32[]{:S(2)}) %collective-permute-start.3) | collective-permute-done | bytes 131104 | tf_op jit(solution)/shard_map/ppermute | solution.py:192
  18.3 0.8 %shard_map.40.sum_ref.refs_0_ = f32[8,96,256]{2,1,0:T(8,128)S(1)} custom-call(bf16[9,96,128]{2,1,0:T(8,128)(2,1)S(1)} %get-tuple-element.14._.w_ref.w_mine_ref, bf16[32,16,128]{2,1,0:T(8,128)(2,1)S(1)} %bitcast.22, bf16[32,16,128]{2,1,0:T(8,128)(2,1)S(1)} %bitcast.18, bf16[32,16,128]{2,1,0:T(8,128)(2,1)S(1)} %bitcast.23, bf16[32,16,128]{2,1,0:T(8,128)(2,1)S(1)} %bitcast.25), custom_call_target="tpu_custom_call" | custom-call | flops 268435456 | bytes 256 | tf_op jit(solution)/shard_map/pallas_call | solution.py:217
  19.1 0.6 %collective-permute-start.6 = (bf16[32,16,128]{2,1,0:T(8,128)(2,1)S(1)}, bf16[32,16,128]{2,1,0:T(8,128)(2,1)S(1)}, u32[]{:S(2)}, u32[]{:S(2)}) collective-permute-start(bf16[32,16,128]{2,1,0:T(8,128)(2,1)S(1)} %bitcast.24), channel_id=1, source_target_pairs={{0,2},{2,0},{4,6},{6,4},{8,10},{10,8},{12,14},{14,12},{16,18},{18,... | collective-permute-start | bytes 393224 | tf_op jit(solution)/shard_map/ppermute | solution.py:271
  19.7 0.1 collective-permute-start.7
  19.8 0.1 collective-permute-done.10.refs_2_
  19.9 0.4 %collective-permute-start.13 = (bf16[32,16,128]{2,1,0:T(8,128)(2,1)S(1)}, bf16[32,16,128]{2,1,0:T(8,128)(2,1)S(1)}, u32[]{:S(2)}, u32[]{:S(2)}) collective-permute-start(bf16[32,16,128]{2,1,0:T(8,128)(2,1)S(1)} %bitcast.19), channel_id=1, source_target_pairs={{0,2},{2,0},{4,6},{6,4},{8,10},{10,8},{12,14},{14,12},{16,18},{18,... | collective-permute-start | bytes 393224 | tf_op jit(solution)/shard_map/ppermute | solution.py:271
  20.3 0.4 %collective-permute-done.6.refs_2_ = bf16[32,16,128]{2,1,0:T(8,128)(2,1)S(1)} collective-permute-done((bf16[32,16,128]{2,1,0:T(8,128)(2,1)S(1)}, bf16[32,16,128]{2,1,0:T(8,128)(2,1)S(1)}, u32[]{:S(2)}, u32[]{:S(2)}) %collective-permute-start.6) | collective-permute-done | bytes 131104 | tf_op jit(solution)/shard_map/ppermute | solution.py:271
  20.7 0.4 %collective-permute-done.7.refs_3_ = bf16[32,16,128]{2,1,0:T(8,128)(2,1)S(1)} collective-permute-done((bf16[32,16,128]{2,1,0:T(8,128)(2,1)S(1)}, bf16[32,16,128]{2,1,0:T(8,128)(2,1)S(1)}, u32[]{:S(2)}, u32[]{:S(2)}) %collective-permute-start.7) | collective-permute-done | bytes 131104 | tf_op jit(solution)/shard_map/ppermute | solution.py:271
  21.1 0.9 %shard_map.41.v_ref = f32[16,32,128]{2,1,0:T(8,128)S(1)} custom-call(bf16[9,96,128]{2,1,0:T(8,128)(2,1)S(1)} %get-tuple-element.15.w_ref.w_theirs_ref, f32[32,128]{1,0:T(8,128)S(1)} %get-tuple-element.16.bias_ref, f32[8,96,256]{2,1,0:T(8,128)S(1)} %shard_map.40.sum_ref.refs_0_, bf16[32,16,128]{2,1,0:T(8,128)(2,1)S(1)} %collective-permute-done.4.refs_0_, ...), custom_call_target="tpu_custom_call" | custom-call | flops 4096 | bytes 256 | tf_op jit(solution)/shard_map/pallas_call | solution.py:217
  21.9 1.8 %shard_map.45 = bf16[128,64]{1,0:T(8,128)(2,1)} custom-call(s32[4]{0:T(128)S(1)} %pad_add_fusion.flags_ref, bf16[9,96,128]{2,1,0:T(8,128)(2,1)S(1)} %get-tuple-element.14._.w_ref.w_mine_ref, bf16[9,96,128]{2,1,0:T(8,128)(2,1)S(1)} %get-tuple-element.15.w_ref.w_theirs_ref, f32[16,32,128]{2,1,0:T(8,128)S(1)} %shard_map.41.v_ref, ...), custom_call_target="tpu_custom_call" | custom-call | flops 4096 | bytes 256 | tf_op jit(solution)/shard_map/pallas_call | solution.py:217
  (14 shorter events, 0.0 us)
Async XLA Ops:
  0.0 8.1 %collective-permute-start = (bf16[16,4,4,128]{3,2,1,0:T(4,128)(2,1)}, bf16[16,4,4,128]{3,2,1,0:T(4,128)(2,1)S(1)}, u32[]{:S(2)}, u32[]{:S(2)}) collective-permute-start(bf16[16,4,4,128]{3,2,1,0:T(4,128)(2,1)} %param.3), channel_id=1, source_target_pairs={{0,16},{1,17},{2,18},{3,19},{4,20},{5,21},{6,22},{7,23},{8,24},{9,... | collective-permute-start | bytes 196616 | tf_op jit(solution)/shard_map/ppermute | solution.py:192
  5.7 6.1 %collective-permute-start.8 = (bf16[64,128]{1,0:T(8,128)(2,1)S(1)}, bf16[64,128]{1,0:T(8,128)(2,1)S(1)}, u32[]{:S(2)}, u32[]{:S(2)}) collective-permute-start(bf16[64,128]{1,0:T(8,128)(2,1)S(1)} %get-tuple-element.18), channel_id=1, source_target_pairs={{0,1},{1,0},{2,3},{3,2},{4,5},{5,4},{6,7},{7,6},{8,9},{9,8},{10,11... | collective-permute-start | bytes 49160 | tf_op jit(solution)/shard_map/ppermute | solution.py:192
  7.3 5.6 %collective-permute-start.9 = (bf16[64,128]{1,0:T(8,128)(2,1)S(1)}, bf16[64,128]{1,0:T(8,128)(2,1)S(1)}, u32[]{:S(2)}, u32[]{:S(2)}) collective-permute-start(bf16[64,128]{1,0:T(8,128)(2,1)S(1)} %get-tuple-element.18), channel_id=1, source_target_pairs={{0,17},{1,16},{2,19},{3,18},{4,21},{5,20},{6,23},{7,22},{8,25},{9,... | collective-permute-start | bytes 49160 | tf_op jit(solution)/shard_map/ppermute | solution.py:192
  8.3 7.6 %collective-permute-start.1 = (bf16[512,128]{1,0:T(8,128)(2,1)S(1)}, bf16[512,128]{1,0:T(8,128)(2,1)S(1)}, u32[]{:S(2)}, u32[]{:S(2)}) collective-permute-start(bf16[512,128]{1,0:T(8,128)(2,1)S(1)} %shard_map.39.refs_0_), channel_id=1, source_target_pairs={{0,4},{1,5},{2,6},{3,7},{4,0},{5,1},{6,2},{7,3},{8,12},{9,13},{10,... | collective-permute-start | bytes 393224 | tf_op jit(solution)/shard_map/ppermute | solution.py:192
  10.2 6.4 %collective-permute-start.2 = (bf16[512,128]{1,0:T(8,128)(2,1)S(1)}, bf16[512,128]{1,0:T(8,128)(2,1)S(1)}, u32[]{:S(2)}, u32[]{:S(2)}) collective-permute-start(bf16[512,128]{1,0:T(8,128)(2,1)S(1)} %shard_map.39.refs_0_), channel_id=1, source_target_pairs={{0,8},{1,9},{2,10},{3,11},{4,12},{5,13},{6,14},{7,15},{8,0},{9,1},... | collective-permute-start | bytes 393224 | tf_op jit(solution)/shard_map/ppermute | solution.py:192
  11.8 6.5 %collective-permute-start.3 = (bf16[512,128]{1,0:T(8,128)(2,1)S(1)}, bf16[512,128]{1,0:T(8,128)(2,1)S(1)}, u32[]{:S(2)}, u32[]{:S(2)}) collective-permute-start(bf16[512,128]{1,0:T(8,128)(2,1)S(1)} %shard_map.39.refs_0_), channel_id=1, source_target_pairs={{0,12},{1,13},{2,14},{3,15},{4,8},{5,9},{6,10},{7,11},{8,4},{9,5},... | collective-permute-start | bytes 393224 | tf_op jit(solution)/shard_map/ppermute | solution.py:192
  12.9 6.2 %collective-permute-start.11 = (bf16[128,128]{1,0:T(8,128)(2,1)S(1)}, bf16[128,128]{1,0:T(8,128)(2,1)S(1)}, u32[]{:S(2)}, u32[]{:S(2)}) collective-permute-start(bf16[128,128]{1,0:T(8,128)(2,1)S(1)} %shard_map.42.refs_1_), channel_id=1, source_target_pairs={{0,8},{1,9},{2,10},{3,11},{4,12},{5,13},{6,14},{7,15},{8,0},{9,1},... | collective-permute-start | bytes 98312 | tf_op jit(solution)/shard_map/ppermute | solution.py:192
  14.4 5.3 %collective-permute-start.12 = (bf16[128,128]{1,0:T(8,128)(2,1)S(1)}, bf16[128,128]{1,0:T(8,128)(2,1)S(1)}, u32[]{:S(2)}, u32[]{:S(2)}) collective-permute-start(bf16[128,128]{1,0:T(8,128)(2,1)S(1)} %shard_map.42.refs_1_), channel_id=1, source_target_pairs={{0,12},{1,13},{2,14},{3,15},{4,8},{5,9},{6,10},{7,11},{8,4},{9,5},... | collective-permute-start | bytes 98312 | tf_op jit(solution)/shard_map/ppermute | solution.py:192
  15.9 3.9 %collective-permute-start.10 = (bf16[128,128]{1,0:T(8,128)(2,1)S(1)}, bf16[128,128]{1,0:T(8,128)(2,1)S(1)}, u32[]{:S(2)}, u32[]{:S(2)}) collective-permute-start(bf16[128,128]{1,0:T(8,128)(2,1)S(1)} %shard_map.43), channel_id=1, source_target_pairs={{0,4},{1,5},{2,6},{3,7},{4,0},{5,1},{6,2},{7,3},{8,12},{9,13},{10,... | collective-permute-start | bytes 98312 | tf_op jit(solution)/shard_map/ppermute | solution.py:192
  16.6 3.7 %collective-permute-start.4 = (bf16[32,16,128]{2,1,0:T(8,128)(2,1)S(1)}, bf16[32,16,128]{2,1,0:T(8,128)(2,1)S(1)}, u32[]{:S(2)}, u32[]{:S(2)}) collective-permute-start(bf16[32,16,128]{2,1,0:T(8,128)(2,1)S(1)} %bitcast.21), channel_id=1, source_target_pairs={{0,2},{2,0},{4,6},{6,4},{8,10},{10,8},{12,14},{14,12},{16,18},{18,... | collective-permute-start | bytes 393224 | tf_op jit(solution)/shard_map/ppermute | solution.py:271
  18.3 2.0 %collective-permute-start.5 = (bf16[32,16,128]{2,1,0:T(8,128)(2,1)S(1)}, bf16[32,16,128]{2,1,0:T(8,128)(2,1)S(1)}, u32[]{:S(2)}, u32[]{:S(2)}) collective-permute-start(bf16[32,16,128]{2,1,0:T(8,128)(2,1)S(1)} %bitcast.17), channel_id=1, source_target_pairs={{0,2},{2,0},{4,6},{6,4},{8,10},{10,8},{12,14},{14,12},{16,18},{18,... | collective-permute-start | bytes 393224 | tf_op jit(solution)/shard_map/ppermute | solution.py:271
  19.1 1.6 %collective-permute-start.6 = (bf16[32,16,128]{2,1,0:T(8,128)(2,1)S(1)}, bf16[32,16,128]{2,1,0:T(8,128)(2,1)S(1)}, u32[]{:S(2)}, u32[]{:S(2)}) collective-permute-start(bf16[32,16,128]{2,1,0:T(8,128)(2,1)S(1)} %bitcast.24), channel_id=1, source_target_pairs={{0,2},{2,0},{4,6},{6,4},{8,10},{10,8},{12,14},{14,12},{16,18},{18,... | collective-permute-start | bytes 393224 | tf_op jit(solution)/shard_map/ppermute | solution.py:271
  19.7 1.3 %collective-permute-start.7 = (bf16[32,16,128]{2,1,0:T(8,128)(2,1)S(1)}, bf16[32,16,128]{2,1,0:T(8,128)(2,1)S(1)}, u32[]{:S(2)}, u32[]{:S(2)}) collective-permute-start(bf16[32,16,128]{2,1,0:T(8,128)(2,1)S(1)} %bitcast.26), channel_id=1, source_target_pairs={{0,2},{2,0},{4,6},{6,4},{8,10},{10,8},{12,14},{14,12},{16,18},{18,... | collective-permute-start | bytes 393224 | tf_op jit(solution)/shard_map/ppermute | solution.py:271
  19.9 2.1 %collective-permute-start.13 = (bf16[32,16,128]{2,1,0:T(8,128)(2,1)S(1)}, bf16[32,16,128]{2,1,0:T(8,128)(2,1)S(1)}, u32[]{:S(2)}, u32[]{:S(2)}) collective-permute-start(bf16[32,16,128]{2,1,0:T(8,128)(2,1)S(1)} %bitcast.19), channel_id=1, source_target_pairs={{0,2},{2,0},{4,6},{6,4},{8,10},{10,8},{12,14},{14,12},{16,18},{18,... | collective-permute-start | bytes 393224 | tf_op jit(solution)/shard_map/ppermute | solution.py:271

commit v7 on v6

--- a/solution.py
+++ b/solution.py
@@ -12,42 +12,45 @@
 
 
 def one_hot(shape, wanted):
-    target = lax.broadcasted_iota(jnp.int32, shape, 0)
+    target = lax.broadcasted_iota(jnp.int32, (shape[0], 1), 0)
     source = lax.broadcasted_iota(jnp.int32, shape, 1)
     return jnp.where(source == wanted(target), 1.0, 0.0).astype(bf16)
 
 
-def sort_rows(x, block):
+def pick_rows(x, block, count, first):
     rows = x.shape[0]
     cells = rows // block
-    pick = one_hot((rows, rows), lambda t: (t & (block - 1)) * cells + t // block)
+    shift = block.bit_length() - 1
+    pick = one_hot(
+        (count * block, rows), lambda t: (t & (block - 1)) * cells + (t >> shift) + first
+    )
     return jnp.dot(pick, x, preferred_element_type=f32).astype(bf16)
 
 
 def begin(flags_ref, vol_ref, kernel_ref, bias_ref, own_ref, *refs, block, depth, count):
-    plane_refs, (w_ref, bias_out_ref, raw_ref, done) = refs[:-4], refs[-4:]
+    plane_refs, (w_ref, bias_out_ref, done) = refs[:-3], refs[-3:]
     copies = [
         pltpu.make_async_copy(source, target, done.at[k])
         for k, (source, target) in enumerate(
-            [(vol_ref, raw_ref), (kernel_ref, w_ref), (bias_ref, bias_out_ref)]
+            [(vol_ref, own_ref), (kernel_ref, w_ref), (bias_ref, bias_out_ref)]
         )
     ]
     for copy in copies:
         copy.start()
+    height = own_ref.shape[0] // block // depth
+    last = (depth - 1) * height
     copies[0].wait()
-    own_ref[...] = sort_rows(raw_ref[...], block)
-    rows = own_ref.shape[0] // depth
     if count == 2:
-        at = jnp.where(flags_ref[2] == 0, (depth - 1) * rows, 0)
-        plane_refs[0][...] = own_ref[pl.ds(pl.multiple_of(at, rows), rows)]
+        firsts = [jnp.where(flags_ref[2] == 0, last, 0)]
     else:
-        plane_refs[0][...] = own_ref[(depth - 1) * rows :]
-        plane_refs[1][...] = own_ref[:rows]
+        firsts = [last, 0]
+    for ref, first in zip(plane_refs, firsts):
+        ref[...] = pick_rows(own_ref[...], block, height, first)
     for copy in copies[1:]:
         copy.wait()
 
 
-def prepare(flags_ref, kernel_ref, bias_ref, w_mine_ref, w_theirs_ref, bias_out_ref, *, block):
+def prepare(flags_ref, _, kernel_ref, bias_ref, w_mine_ref, w_theirs_ref, bias_out_ref, *, block):
     cin = kernel_ref.shape[-1]
     half = cin // 2
     far = half // block // 2
@@ -72,10 +75,12 @@
     )
 
 
-def assemble(_, own_ref, far_ref, pair_ref, *, block):
-    size = own_ref.shape[0]
-    pair_ref[:size] = own_ref[...]
-    pair_ref[size:] = sort_rows(far_ref[...], block)
+def assemble(own_ref, far_ref, pair_ref, *, block):
+    size, across = own_ref.shape
+    both = jnp.concatenate([own_ref[...], far_ref[...]], axis=1)
+    moved = pick_rows(both, block, size // block, 0)
+    pair_ref[:size] = moved[:, :across]
+    pair_ref[size:] = moved[:, across:]
 
 
 def join(*refs):
@@ -126,8 +131,8 @@
     return v + jnp.where(lane < across - 1, right, 0.0)
 
 
-def own_parity(w_ref, *refs, depth, height):
-    refs, sum_ref = refs[:-1], refs[-1]
+def own_parity(w_ref, *refs, depth, height, blocks):
+    refs, sum_ref = (*refs[1:blocks], refs[0]), refs[-1]
     for z, y, total in products(w_ref, refs, depth, height):
         sum_ref[z * (height // 2) + y] = total
 
@@ -174,7 +179,8 @@
     stacked = jnp.maximum(stacked, pltpu.roll(stacked, across - 1, 1)).astype(bf16)
     cells = (depth // 2) * (height // 2)
     size = cells * filters
-    rows_pick = one_hot((size, size), lambda t: (t & (cells - 1)) * filters + t // cells)
+    shift = cells.bit_length() - 1
+    rows_pick = one_hot((size, size), lambda t: (t & (cells - 1)) * filters + (t >> shift))
     lane_from = lax.broadcasted_iota(jnp.int32, (across, across // 2), 0)
     lane_to = lax.broadcasted_iota(jnp.int32, (across, across // 2), 1)
     lanes_pick = jnp.where(lane_from == 2 * lane_to, 1.0, 0.0).astype(bf16)
@@ -234,38 +240,39 @@
         + [shape(weights.shape, bf16), shape((1, filters), bf16)],
         [smem, hbm, hbm, hbm],
         [flags] + [pltpu.with_memory_space_constraint(x, pltpu.HBM) for x in given],
-        [pltpu.VMEM((cells, across), bf16), pltpu.SemaphoreType.DMA((3,))],
+        [pltpu.SemaphoreType.DMA((3,))],
     )
     sends = list(zip(edges, steps))
     far_planes = [shifted(x, far, step, size, count) for x, step in sends]
     own_planes = [shifted(x, 0, step, size, count) for x, step in sends]
+    pair = call(
+        functools.partial(assemble, block=block),
+        shape((2 * cells, across), bf16),
+        [vmem, vmem],
+        (own_block, far_block.reshape(cells, across)),
+        cost=31,
+    )
     ordered = shape((9, 3 * filters, cin // 2), bf16)
     w_mine, w_theirs, bias = call(
         functools.partial(prepare, block=block),
         (ordered, ordered, shape((filters, across), f32)),
-        [smem, vmem, vmem],
-        (flags, weights, bias),
-        cost=31,
-    )
-
-    pair = call(
-        functools.partial(assemble, block=block),
-        shape((2 * cells, across), bf16),
-        [anywhere, vmem, vmem],
-        (w_mine, own_block, far_block.reshape(cells, across)),
+        [smem, anywhere, vmem, vmem],
+        (flags, pair, weights, bias),
         cost=31,
     )
     planes = call(
         join,
         shape((2 * extra * beside, across), bf16),
         [anywhere] + [vmem] * (2 * extra),
-        [pair] + own_planes + far_planes,
+        [w_mine] + own_planes + far_planes,
         cost=31,
     )
 
     def near(x):
-        parts = [x] + [shifted(x, r, 0, size, count) for r in range(1, far)]
-        return [part.reshape(-1, block, across) for part in parts]
+        parts = {r: shifted(x, r, 0, size, count) for r in [far - 1, *range(1, far - 1)]}
+        return [x.reshape(-1, block, across)] + [
+            parts[r].reshape(-1, block, across) for r in range(1, far)
+        ]
 
     def swapped(x):
         return lax.ppermute(x, "filt", [(i, i ^ 1) for i in range(size)])
@@ -273,16 +280,16 @@
     mine = near(pair)
     theirs = [swapped(x) for x in mine]
     dims = dict(depth=depth, height=height)
-    partial = call(
-        functools.partial(own_parity, **dims),
-        shape((depth * pairs, 3 * filters, 2 * across), f32),
-        [vmem] * (1 + far),
-        [w_mine] + mine,
-        cost=28,
-    )
-    again = call(join, shape(planes.shape, bf16), [anywhere, vmem], (mine[1], planes), cost=12)
+    again = call(join, shape(planes.shape, bf16), [anywhere, vmem], (mine[-1], planes), cost=12)
     behind = [shifted(planes, r, 0, size, count) for r in range(2, far)]
     behind = [planes, shifted(again, 1, 0, size, count)] + behind
+    partial = call(
+        functools.partial(own_parity, blocks=far, **dims),
+        shape((depth * pairs, 3 * filters, 2 * across), f32),
+        [vmem] * (1 + far) + [anywhere] * (far - 2),
+        [w_mine, mine[-1]] + mine[:-1] + behind[2:],
+        cost=28,
+    )
     planes = call(
         join,
         shape((far * planes.shape[0], across), bf16),

time: 23.9 us -> 24.3 us (1.017)
    ppermute x9, waiting for transfers between devices: 2.93 us -> 3.77 us  [shifted(): return lax.ppermute(x, ('filt', 'space'), pairs)]
    ppermute x5, waiting for transfers between devices: 0.76 us -> 0.1 us  [swapped(): return lax.ppermute(x, 'filt', [(i, i ^ 1) for i in range(size)])]
  transfers between devices with their start and end apart: 14 -> 14, of which waited for: 6 -> 5; matrix products, arithmetic and copies ran while one was open for 0% -> 0% of each run, Pallas kernels for 18% -> 18%
where the time goes in v7:
time: 24.3 us; the launch traced here: 24.1 us
  starting transfers between devices  14 us (58%)
  Pallas kernels  6.13 us (25%)
  waiting for transfers between devices  3.87 us (16%)
    ppermute x9, starting transfers between devices, shifted(): return lax.ppermute(x, ('filt', 'space'), pairs)  12.9 us
    pallas_call x9, Pallas kernels, call(): pl.pallas_call(body, out_shape=outs, in_specs=ins, out_specs=jax.tree.map...  6.13 us
    ppermute x9, waiting for transfers between devices, shifted(): return lax.ppermute(x, ('filt', 'space'), pairs)  3.77 us
    ppermute x5, starting transfers between devices, swapped(): return lax.ppermute(x, 'filt', [(i, i ^ 1) for i in range(size)])  1.09 us
  transfers between devices with their start and end apart: 14, of which 5 were waited for; matrix products, arithmetic and copies ran while one was open for 0% of the time, Pallas kernels for 18%

profile of v7, /device:TPU:0, one launch (start us, length us, event | category | flops | bytes accessed | tf_op | source)
XLA Modules:
  0.0 24.1 jit_solution(12743238029278734873)
XLA Ops:
  0.0 4.0 %collective-permute-start = (bf16[16,4,4,128]{3,2,1,0:T(4,128)(2,1)}, bf16[16,4,4,128]{3,2,1,0:T(4,128)(2,1)S(1)}, u32[]{:S(2)}, u32[]{:S(2)}) collective-permute-start(bf16[16,4,4,128]{3,2,1,0:T(4,128)(2,1)} %param.3), channel_id=1, source_target_pairs={{0,16},{1,17},{2,18},{3,19},{4,20},{5,21},{6,22},{7,23},{8,24},{9,... | collective-permute-start | bytes 196616 | tf_op jit(solution)/shard_map/ppermute | solution.py:198
  4.0 0.1 pad_add_fusion.flags_ref
  4.1 1.6 %shard_map.37 = (bf16[256,128]{1,0:T(8,128)(2,1)S(1)}, bf16[64,128]{1,0:T(8,128)(2,1)S(1)}, bf16[864,256]{1,0:T(8,128)(2,1)S(1)}, bf16[1,32]{1,0:T(2,128)(2,1)S(1)}) custom-call(s32[4]{0:T(128)S(1)} %pad_add_fusion.flags_ref, bf16[256,128]{1,0:T(8,128)(2,1)} %bitcast.29, bf16[864,256]{1,0:T(8,128)(2,1)} %bitcast.28, bf16[1,32]{1,0:T(2,128)(2,1)} %bitcast.30), custom_call_target="tpu_custom_call" | custom-call | flops 4096 | bytes 256 | tf_op jit(solution)/shard_map/pallas_call | solution.py:223
  5.7 1.6 %collective-permute-start.4 = (bf16[64,128]{1,0:T(8,128)(2,1)S(1)}, bf16[64,128]{1,0:T(8,128)(2,1)S(1)}, u32[]{:S(2)}, u32[]{:S(2)}) collective-permute-start(bf16[64,128]{1,0:T(8,128)(2,1)S(1)} %get-tuple-element.18), channel_id=1, source_target_pairs={{0,1},{1,0},{2,3},{3,2},{4,5},{5,4},{6,7},{7,6},{8,9},{9,8},{10,11... | collective-permute-start | bytes 49160 | tf_op jit(solution)/shard_map/ppermute | solution.py:198
  7.3 0.0 collective-permute-start.5
  7.3 0.6 %collective-permute-done = bf16[16,4,4,128]{3,2,1,0:T(4,128)(2,1)S(1)} collective-permute-done((bf16[16,4,4,128]{3,2,1,0:T(4,128)(2,1)}, bf16[16,4,4,128]{3,2,1,0:T(4,128)(2,1)S(1)}, u32[]{:S(2)}, u32[]{:S(2)}) %collective-permute-start) | collective-permute-done | bytes 65568 | tf_op jit(solution)/shard_map/ppermute | solution.py:198
  7.9 0.2 shard_map.38._
  8.1 2.3 %collective-permute-start.1 = (bf16[512,128]{1,0:T(8,128)(2,1)S(1)}, bf16[512,128]{1,0:T(8,128)(2,1)S(1)}, u32[]{:S(2)}, u32[]{:S(2)}) collective-permute-start(bf16[512,128]{1,0:T(8,128)(2,1)S(1)} %shard_map.38._), channel_id=1, source_target_pairs={{0,12},{1,13},{2,14},{3,15},{4,8},{5,9},{6,10},{7,11},{8,4},{9,5},... | collective-permute-start | bytes 393224 | tf_op jit(solution)/shard_map/ppermute | solution.py:198
  10.4 0.5 %collective-permute-start.2 = (bf16[512,128]{1,0:T(8,128)(2,1)S(1)}, bf16[512,128]{1,0:T(8,128)(2,1)S(1)}, u32[]{:S(2)}, u32[]{:S(2)}) collective-permute-start(bf16[512,128]{1,0:T(8,128)(2,1)S(1)} %shard_map.38._), channel_id=1, source_target_pairs={{0,4},{1,5},{2,6},{3,7},{4,0},{5,1},{6,2},{7,3},{8,12},{9,13},{10,... | collective-permute-start | bytes 393224 | tf_op jit(solution)/shard_map/ppermute | solution.py:198
  10.9 0.7 %collective-permute-start.3 = (bf16[512,128]{1,0:T(8,128)(2,1)S(1)}, bf16[512,128]{1,0:T(8,128)(2,1)S(1)}, u32[]{:S(2)}, u32[]{:S(2)}) collective-permute-start(bf16[512,128]{1,0:T(8,128)(2,1)S(1)} %shard_map.38._), channel_id=1, source_target_pairs={{0,8},{1,9},{2,10},{3,11},{4,12},{5,13},{6,14},{7,15},{8,0},{9,1},... | collective-permute-start | bytes 393224 | tf_op jit(solution)/shard_map/ppermute | solution.py:198
  11.6 0.8 %shard_map.39 = (bf16[9,96,128]{2,1,0:T(8,128)(2,1)S(1)}, bf16[9,96,128]{2,1,0:T(8,128)(2,1)S(1)}, f32[32,128]{1,0:T(8,128)S(1)}) custom-call(s32[4]{0:T(128)S(1)} %pad_add_fusion.flags_ref, bf16[512,128]{1,0:T(8,128)(2,1)S(1)} %shard_map.38._, bf16[864,256]{1,0:T(8,128)(2,1)S(1)} %get-tuple-element.13.kernel_ref, bf16[1,32]{1,0:T(2,128)(2,1)S(1)} %get-tuple-element.14.bias_ref), custom_call_target="tpu_custom_call" | custom-call | flops 2147483648 | bytes 256 | tf_op jit(solution)/shard_map/pallas_call | solution.py:223
  12.5 0.4 %collective-permute-done.5.refs_2_ = bf16[64,128]{1,0:T(8,128)(2,1)S(1)} collective-permute-done((bf16[64,128]{1,0:T(8,128)(2,1)S(1)}, bf16[64,128]{1,0:T(8,128)(2,1)S(1)}, u32[]{:S(2)}, u32[]{:S(2)}) %collective-permute-start.5) | collective-permute-done | bytes 16416 | tf_op jit(solution)/shard_map/ppermute | solution.py:198
  12.9 1.7 %collective-permute-start.6 = (bf16[128,128]{1,0:T(8,128)(2,1)S(1)}, bf16[128,128]{1,0:T(8,128)(2,1)S(1)}, u32[]{:S(2)}, u32[]{:S(2)}) collective-permute-start(bf16[128,128]{1,0:T(8,128)(2,1)S(1)} %shard_map.40.refs_1_), channel_id=1, source_target_pairs={{0,8},{1,9},{2,10},{3,11},{4,12},{5,13},{6,14},{7,15},{8,0},{9,1},... | collective-permute-start | bytes 98312 | tf_op jit(solution)/shard_map/ppermute | solution.py:198
  14.6 1.2 %collective-permute-start.7 = (bf16[128,128]{1,0:T(8,128)(2,1)S(1)}, bf16[128,128]{1,0:T(8,128)(2,1)S(1)}, u32[]{:S(2)}, u32[]{:S(2)}) collective-permute-start(bf16[128,128]{1,0:T(8,128)(2,1)S(1)} %shard_map.40.refs_1_), channel_id=1, source_target_pairs={{0,12},{1,13},{2,14},{3,15},{4,8},{5,9},{6,10},{7,11},{8,4},{9,5},... | collective-permute-start | bytes 98312 | tf_op jit(solution)/shard_map/ppermute | solution.py:198
  15.8 0.8 %collective-permute-start.12 = (bf16[128,128]{1,0:T(8,128)(2,1)S(1)}, bf16[128,128]{1,0:T(8,128)(2,1)S(1)}, u32[]{:S(2)}, u32[]{:S(2)}) collective-permute-start(bf16[128,128]{1,0:T(8,128)(2,1)S(1)} %shard_map.43), channel_id=1, source_target_pairs={{0,4},{1,5},{2,6},{3,7},{4,0},{5,1},{6,2},{7,3},{8,12},{9,13},{10,... | collective-permute-start | bytes 98312 | tf_op jit(solution)/shard_map/ppermute | solution.py:198
  16.7 0.6 %collective-permute-done.6.refs_4_.refs_3_ = bf16[128,128]{1,0:T(8,128)(2,1)S(1)} collective-permute-done((bf16[128,128]{1,0:T(8,128)(2,1)S(1)}, bf16[128,128]{1,0:T(8,128)(2,1)S(1)}, u32[]{:S(2)}, u32[]{:S(2)}) %collective-permute-start.6) | collective-permute-done | bytes 32800 | tf_op jit(solution)/shard_map/ppermute | solution.py:198
  17.3 2.1 %collective-permute-done.7.refs_5_.refs_4_ = bf16[128,128]{1,0:T(8,128)(2,1)S(1)} collective-permute-done((bf16[128,128]{1,0:T(8,128)(2,1)S(1)}, bf16[128,128]{1,0:T(8,128)(2,1)S(1)}, u32[]{:S(2)}, u32[]{:S(2)}) %collective-permute-start.7) | collective-permute-done | bytes 32800 | tf_op jit(solution)/shard_map/ppermute | solution.py:198
  19.4 0.5 %collective-permute-start.9 = (bf16[32,16,128]{2,1,0:T(8,128)(2,1)S(1)}, bf16[32,16,128]{2,1,0:T(8,128)(2,1)S(1)}, u32[]{:S(2)}, u32[]{:S(2)}) collective-permute-start(bf16[32,16,128]{2,1,0:T(8,128)(2,1)S(1)} %bitcast.23), channel_id=1, source_target_pairs={{0,2},{2,0},{4,6},{6,4},{8,10},{10,8},{12,14},{14,12},{16,18},{18,... | collective-permute-start | bytes 393224 | tf_op jit(solution)/shard_map/ppermute | solution.py:278
  19.9 0.1 collective-permute-start.10
  20.0 0.8 %shard_map.41.sum_ref.refs_0_ = f32[8,96,256]{2,1,0:T(8,128)S(1)} custom-call(bf16[9,96,128]{2,1,0:T(8,128)(2,1)S(1)} %get-tuple-element.15.refs_0_.w_ref.w_mine_ref, bf16[32,16,128]{2,1,0:T(8,128)(2,1)S(1)} %bitcast.18, bf16[32,16,128]{2,1,0:T(8,128)(2,1)S(1)} %bitcast.22, bf16[32,16,128]{2,1,0:T(8,128)(2,1)S(1)} %bitcast.24, ...), custom_call_target="tpu_custom_call" | custom-call | flops 268435456 | bytes 256 | tf_op jit(solution)/shard_map/pallas_call | solution.py:223
  20.8 0.5 %collective-permute-start.13 = (bf16[32,16,128]{2,1,0:T(8,128)(2,1)S(1)}, bf16[32,16,128]{2,1,0:T(8,128)(2,1)S(1)}, u32[]{:S(2)}, u32[]{:S(2)}) collective-permute-start(bf16[32,16,128]{2,1,0:T(8,128)(2,1)S(1)} %bitcast.19), channel_id=1, source_target_pairs={{0,2},{2,0},{4,6},{6,4},{8,10},{10,8},{12,14},{14,12},{16,18},{18,... | collective-permute-start | bytes 393224 | tf_op jit(solution)/shard_map/ppermute | solution.py:278
  21.3 0.9 %shard_map.42.v_ref = f32[16,32,128]{2,1,0:T(8,128)S(1)} custom-call(bf16[9,96,128]{2,1,0:T(8,128)(2,1)S(1)} %get-tuple-element.16.w_ref.w_theirs_ref, f32[32,128]{1,0:T(8,128)S(1)} %get-tuple-element.17.bias_ref, f32[8,96,256]{2,1,0:T(8,128)S(1)} %shard_map.41.sum_ref.refs_0_, bf16[32,16,128]{2,1,0:T(8,128)(2,1)S(1)} %collective-permute-done.8.refs_0_, ...), custom_call_target="tpu_custom_call" | custom-call | flops 4096 | bytes 256 | tf_op jit(solution)/shard_map/pallas_call | solution.py:223
  22.2 0.1 collective-permute-done.13.refs_1_
  22.3 1.8 %shard_map.45 = bf16[128,64]{1,0:T(8,128)(2,1)} custom-call(s32[4]{0:T(128)S(1)} %pad_add_fusion.flags_ref, bf16[9,96,128]{2,1,0:T(8,128)(2,1)S(1)} %get-tuple-element.15.refs_0_.w_ref.w_mine_ref, bf16[9,96,128]{2,1,0:T(8,128)(2,1)S(1)} %get-tuple-element.16.w_ref.w_theirs_ref, f32[16,32,128]{2,1,0:T(8,128)S(1)} %shard_map.42.v_ref, ...), custom_call_target="tpu_custom_call" | custom-call | flops 4096 | bytes 256 | tf_op jit(solution)/shard_map/pallas_call | solution.py:223
  (14 shorter events, 0.0 us)
Async XLA Ops:
  0.0 7.9 %collective-permute-start = (bf16[16,4,4,128]{3,2,1,0:T(4,128)(2,1)}, bf16[16,4,4,128]{3,2,1,0:T(4,128)(2,1)S(1)}, u32[]{:S(2)}, u32[]{:S(2)}) collective-permute-start(bf16[16,4,4,128]{3,2,1,0:T(4,128)(2,1)} %param.3), channel_id=1, source_target_pairs={{0,16},{1,17},{2,18},{3,19},{4,20},{5,21},{6,22},{7,23},{8,24},{9,... | collective-permute-start | bytes 196616 | tf_op jit(solution)/shard_map/ppermute | solution.py:198
  5.7 6.7 %collective-permute-start.4 = (bf16[64,128]{1,0:T(8,128)(2,1)S(1)}, bf16[64,128]{1,0:T(8,128)(2,1)S(1)}, u32[]{:S(2)}, u32[]{:S(2)}) collective-permute-start(bf16[64,128]{1,0:T(8,128)(2,1)S(1)} %get-tuple-element.18), channel_id=1, source_target_pairs={{0,1},{1,0},{2,3},{3,2},{4,5},{5,4},{6,7},{7,6},{8,9},{9,8},{10,11... | collective-permute-start | bytes 49160 | tf_op jit(solution)/shard_map/ppermute | solution.py:198
  7.3 5.6 %collective-permute-start.5 = (bf16[64,128]{1,0:T(8,128)(2,1)S(1)}, bf16[64,128]{1,0:T(8,128)(2,1)S(1)}, u32[]{:S(2)}, u32[]{:S(2)}) collective-permute-start(bf16[64,128]{1,0:T(8,128)(2,1)S(1)} %get-tuple-element.18), channel_id=1, source_target_pairs={{0,17},{1,16},{2,19},{3,18},{4,21},{5,20},{6,23},{7,22},{8,25},{9,... | collective-permute-start | bytes 49160 | tf_op jit(solution)/shard_map/ppermute | solution.py:198
  8.1 7.7 %collective-permute-start.1 = (bf16[512,128]{1,0:T(8,128)(2,1)S(1)}, bf16[512,128]{1,0:T(8,128)(2,1)S(1)}, u32[]{:S(2)}, u32[]{:S(2)}) collective-permute-start(bf16[512,128]{1,0:T(8,128)(2,1)S(1)} %shard_map.38._), channel_id=1, source_target_pairs={{0,12},{1,13},{2,14},{3,15},{4,8},{5,9},{6,10},{7,11},{8,4},{9,5},... | collective-permute-start | bytes 393224 | tf_op jit(solution)/shard_map/ppermute | solution.py:198
  10.4 9.0 %collective-permute-start.2 = (bf16[512,128]{1,0:T(8,128)(2,1)S(1)}, bf16[512,128]{1,0:T(8,128)(2,1)S(1)}, u32[]{:S(2)}, u32[]{:S(2)}) collective-permute-start(bf16[512,128]{1,0:T(8,128)(2,1)S(1)} %shard_map.38._), channel_id=1, source_target_pairs={{0,4},{1,5},{2,6},{3,7},{4,0},{5,1},{6,2},{7,3},{8,12},{9,13},{10,... | collective-permute-start | bytes 393224 | tf_op jit(solution)/shard_map/ppermute | solution.py:198
  10.9 9.0 %collective-permute-start.3 = (bf16[512,128]{1,0:T(8,128)(2,1)S(1)}, bf16[512,128]{1,0:T(8,128)(2,1)S(1)}, u32[]{:S(2)}, u32[]{:S(2)}) collective-permute-start(bf16[512,128]{1,0:T(8,128)(2,1)S(1)} %shard_map.38._), channel_id=1, source_target_pairs={{0,8},{1,9},{2,10},{3,11},{4,12},{5,13},{6,14},{7,15},{8,0},{9,1},... | collective-permute-start | bytes 393224 | tf_op jit(solution)/shard_map/ppermute | solution.py:198
  12.9 4.3 %collective-permute-start.6 = (bf16[128,128]{1,0:T(8,128)(2,1)S(1)}, bf16[128,128]{1,0:T(8,128)(2,1)S(1)}, u32[]{:S(2)}, u32[]{:S(2)}) collective-permute-start(bf16[128,128]{1,0:T(8,128)(2,1)S(1)} %shard_map.40.refs_1_), channel_id=1, source_target_pairs={{0,8},{1,9},{2,10},{3,11},{4,12},{5,13},{6,14},{7,15},{8,0},{9,1},... | collective-permute-start | bytes 98312 | tf_op jit(solution)/shard_map/ppermute | solution.py:198
  14.6 4.8 %collective-permute-start.7 = (bf16[128,128]{1,0:T(8,128)(2,1)S(1)}, bf16[128,128]{1,0:T(8,128)(2,1)S(1)}, u32[]{:S(2)}, u32[]{:S(2)}) collective-permute-start(bf16[128,128]{1,0:T(8,128)(2,1)S(1)} %shard_map.40.refs_1_), channel_id=1, source_target_pairs={{0,12},{1,13},{2,14},{3,15},{4,8},{5,9},{6,10},{7,11},{8,4},{9,5},... | collective-permute-start | bytes 98312 | tf_op jit(solution)/shard_map/ppermute | solution.py:198
  15.8 4.9 %collective-permute-start.12 = (bf16[128,128]{1,0:T(8,128)(2,1)S(1)}, bf16[128,128]{1,0:T(8,128)(2,1)S(1)}, u32[]{:S(2)}, u32[]{:S(2)}) collective-permute-start(bf16[128,128]{1,0:T(8,128)(2,1)S(1)} %shard_map.43), channel_id=1, source_target_pairs={{0,4},{1,5},{2,6},{3,7},{4,0},{5,1},{6,2},{7,3},{8,12},{9,13},{10,... | collective-permute-start | bytes 98312 | tf_op jit(solution)/shard_map/ppermute | solution.py:198
  17.3 4.0 %collective-permute-start.8 = (bf16[32,16,128]{2,1,0:T(8,128)(2,1)S(1)}, bf16[32,16,128]{2,1,0:T(8,128)(2,1)S(1)}, u32[]{:S(2)}, u32[]{:S(2)}) collective-permute-start(bf16[32,16,128]{2,1,0:T(8,128)(2,1)S(1)} %bitcast.21), channel_id=1, source_target_pairs={{0,2},{2,0},{4,6},{6,4},{8,10},{10,8},{12,14},{14,12},{16,18},{18,... | collective-permute-start | bytes 393224 | tf_op jit(solution)/shard_map/ppermute | solution.py:278
  19.4 1.9 %collective-permute-start.11 = (bf16[32,16,128]{2,1,0:T(8,128)(2,1)S(1)}, bf16[32,16,128]{2,1,0:T(8,128)(2,1)S(1)}, u32[]{:S(2)}, u32[]{:S(2)}) collective-permute-start(bf16[32,16,128]{2,1,0:T(8,128)(2,1)S(1)} %bitcast.17), channel_id=1, source_target_pairs={{0,2},{2,0},{4,6},{6,4},{8,10},{10,8},{12,14},{14,12},{16,18},{18,... | collective-permute-start | bytes 393224 | tf_op jit(solution)/shard_map/ppermute | solution.py:278
  19.4 1.9 %collective-permute-start.9 = (bf16[32,16,128]{2,1,0:T(8,128)(2,1)S(1)}, bf16[32,16,128]{2,1,0:T(8,128)(2,1)S(1)}, u32[]{:S(2)}, u32[]{:S(2)}) collective-permute-start(bf16[32,16,128]{2,1,0:T(8,128)(2,1)S(1)} %bitcast.23), channel_id=1, source_target_pairs={{0,2},{2,0},{4,6},{6,4},{8,10},{10,8},{12,14},{14,12},{16,18},{18,... | collective-permute-start | bytes 393224 | tf_op jit(solution)/shard_map/ppermute | solution.py:278
  19.9 1.4 %collective-permute-start.10 = (bf16[32,16,128]{2,1,0:T(8,128)(2,1)S(1)}, bf16[32,16,128]{2,1,0:T(8,128)(2,1)S(1)}, u32[]{:S(2)}, u32[]{:S(2)}) collective-permute-start(bf16[32,16,128]{2,1,0:T(8,128)(2,1)S(1)} %bitcast.25), channel_id=1, source_target_pairs={{0,2},{2,0},{4,6},{6,4},{8,10},{10,8},{12,14},{14,12},{16,18},{18,... | collective-permute-start | bytes 393224 | tf_op jit(solution)/shard_map/ppermute | solution.py:278
  20.8 1.5 %collective-permute-start.13 = (bf16[32,16,128]{2,1,0:T(8,128)(2,1)S(1)}, bf16[32,16,128]{2,1,0:T(8,128)(2,1)S(1)}, u32[]{:S(2)}, u32[]{:S(2)}) collective-permute-start(bf16[32,16,128]{2,1,0:T(8,128)(2,1)S(1)} %bitcast.19), channel_id=1, source_target_pairs={{0,2},{2,0},{4,6},{6,4},{8,10},{10,8},{12,14},{14,12},{16,18},{18,... | collective-permute-start | bytes 393224 | tf_op jit(solution)/shard_map/ppermute | solution.py:278

commit v8 on v7

--- a/solution.py
+++ b/solution.py
@@ -27,12 +27,12 @@
     return jnp.dot(pick, x, preferred_element_type=f32).astype(bf16)
 
 
-def begin(flags_ref, vol_ref, kernel_ref, bias_ref, own_ref, *refs, block, depth, count):
-    plane_refs, (w_ref, bias_out_ref, done) = refs[:-3], refs[-3:]
+def begin(vol_ref, bias_ref, own_ref, *refs, block, depth, count):
+    plane_refs, (bias_out_ref, done) = refs[:-2], refs[-2:]
     copies = [
         pltpu.make_async_copy(source, target, done.at[k])
         for k, (source, target) in enumerate(
-            [(vol_ref, own_ref), (kernel_ref, w_ref), (bias_ref, bias_out_ref)]
+            [(vol_ref, own_ref), (bias_ref, bias_out_ref)]
         )
     ]
     for copy in copies:
@@ -41,7 +41,7 @@
     last = (depth - 1) * height
     copies[0].wait()
     if count == 2:
-        firsts = [jnp.where(flags_ref[2] == 0, last, 0)]
+        firsts = [jnp.where(lax.axis_index("space") == 0, last, 0)]
     else:
         firsts = [last, 0]
     for ref, first in zip(plane_refs, firsts):
@@ -50,12 +50,17 @@
         copy.wait()
 
 
-def prepare(flags_ref, _, kernel_ref, bias_ref, w_mine_ref, w_theirs_ref, bias_out_ref, *, block):
+def prepare(
+    _, w_ref, bias_ref, w_mine_ref, w_theirs_ref, bias_out_ref, kernel_ref, done, *, block
+):
+    fetch = pltpu.make_async_copy(w_ref, kernel_ref, done)
+    fetch.start()
     cin = kernel_ref.shape[-1]
     half = cin // 2
     far = half // block // 2
     shift = block.bit_length() - 1
-    core, group = flags_ref[0], flags_ref[1]
+    place = lax.axis_index("filt")
+    core, group = place & 1, place >> 1
     source = lax.broadcasted_iota(jnp.int32, (cin, cin), 0)
     target = lax.broadcasted_iota(jnp.int32, (1, cin), 1)
     part = jnp.where(target < half, core, 1 - core)
@@ -63,9 +68,6 @@
     relative = (slot >> 1) | jnp.where((slot & 1) > 0, far, 0)
     wanted = ((((relative ^ group) << 1) | part) << shift) | (target & (block - 1))
     shuffle = jnp.where(source == wanted, 1.0, 0.0).astype(bf16)
-    ordered = jnp.dot(kernel_ref[...], shuffle, preferred_element_type=f32).astype(bf16)
-    w_mine_ref[...] = ordered[:, :half].reshape(w_mine_ref.shape)
-    w_theirs_ref[...] = ordered[:, half:].reshape(w_theirs_ref.shape)
     filters = bias_ref.shape[1]
     row = lax.broadcasted_iota(jnp.int32, (filters, filters), 0)
     column = lax.broadcasted_iota(jnp.int32, (filters, filters), 1)
@@ -73,6 +75,10 @@
     bias_out_ref[...] = jnp.broadcast_to(
         jnp.sum(spread, axis=1, keepdims=True), bias_out_ref.shape
     )
+    fetch.wait()
+    ordered = jnp.dot(kernel_ref[...], shuffle, preferred_element_type=f32).astype(bf16)
+    w_mine_ref[...] = ordered[:, :half].reshape(w_mine_ref.shape)
+    w_theirs_ref[...] = ordered[:, half:].reshape(w_theirs_ref.shape)
 
 
 def assemble(own_ref, far_ref, pair_ref, *, block):
@@ -146,13 +152,14 @@
             v_ref[z * height + 2 * y + j] = combine(total, j, filters, across) + bias_ref[...]
 
 
-def finish(flags_ref, w_mine_ref, w_theirs_ref, v_ref, *refs, depth, height, count):
+def finish(w_mine_ref, w_theirs_ref, v_ref, *refs, depth, height, count):
     refs, out_ref = refs[:-1], refs[-1]
     filters, across = v_ref.shape[1:]
+    here = lax.axis_index("space")
     extra = 1 if count == 2 else 2
     beside = []
     for which in range(extra):
-        tap = 2 * which if extra == 2 else jnp.where(flags_ref[2] > 0, 0, 2)
+        tap = 2 * which if extra == 2 else jnp.where(here > 0, 0, 2)
         left = jnp.concatenate(
             [w[tap * 3 + b] for b in range(3) for w in (w_mine_ref, w_theirs_ref)], axis=1
         )
@@ -167,9 +174,9 @@
         for y in range(height):
             v = v_ref[z * height + y]
             if z == 0:
-                v += jnp.where(flags_ref[2] > 0, beside[0][y], 0.0)
+                v += jnp.where(here > 0, beside[0][y], 0.0)
             if z == depth - 1:
-                v += jnp.where(flags_ref[3] > 0, beside[-1][y], 0.0)
+                v += jnp.where(here < count - 1, beside[-1][y], 0.0)
             v = jnp.where(v > 0, v, slope * v)
             key = (z // 2, y // 2)
             pooled[key] = v if key not in pooled else jnp.maximum(pooled[key], v)
@@ -203,9 +210,6 @@
     filters, cin = kernel.shape[0], kernel.shape[-1]
     size = lax.axis_size("filt")
     count = lax.axis_size("space")
-    here = lax.axis_index("space")
-    place = lax.axis_index("filt")
-    flags = jnp.stack([place & 1, place >> 1, here, count - 1 - here]).astype(jnp.int32)
     far = size // 4
     pairs = height // 2
     cells = depth * height * block
@@ -214,7 +218,6 @@
     extra = len(steps)
 
     vmem = pl.BlockSpec(memory_space=pltpu.VMEM)
-    smem = pl.BlockSpec(memory_space=pltpu.SMEM)
     hbm = pl.BlockSpec(memory_space=pltpu.HBM)
     anywhere = pl.BlockSpec(memory_space=pl.ANY)
     shape = jax.ShapeDtypeStruct
@@ -230,17 +233,19 @@
             cost_estimate=pl.CostEstimate(flops=1 << cost, bytes_accessed=1 << 8, transcendentals=0),
         )(*args)
 
+    def pinned(x):
+        return pltpu.with_memory_space_constraint(x, pltpu.HBM)
+
     far_block = shifted(volume, far, 0, size, count)
     weights = kernel.transpose(1, 2, 3, 0, 4).reshape(-1, cin)
-    given = [volume.reshape(cells, across), weights, filter_bias[None]]
-    own_block, *edges, weights, bias = call(
+    own_block, *edges, bias = call(
         functools.partial(begin, block=block, depth=depth, count=count),
         [shape((cells, across), bf16)]
         + [shape((beside, across), bf16)] * extra
-        + [shape(weights.shape, bf16), shape((1, filters), bf16)],
-        [smem, hbm, hbm, hbm],
-        [flags] + [pltpu.with_memory_space_constraint(x, pltpu.HBM) for x in given],
-        [pltpu.SemaphoreType.DMA((3,))],
+        + [shape((1, filters), bf16)],
+        [hbm, hbm],
+        (pinned(volume.reshape(cells, across)), pinned(filter_bias[None])),
+        [pltpu.SemaphoreType.DMA((2,))],
     )
     sends = list(zip(edges, steps))
     far_planes = [shifted(x, far, step, size, count) for x, step in sends]
@@ -256,8 +261,9 @@
     w_mine, w_theirs, bias = call(
         functools.partial(prepare, block=block),
         (ordered, ordered, shape((filters, across), f32)),
-        [smem, anywhere, vmem, vmem],
-        (flags, pair, weights, bias),
+        [anywhere, hbm, vmem],
+        (pair, pinned(weights), bias),
+        [pltpu.VMEM(weights.shape, bf16), pltpu.SemaphoreType.DMA(())],
         cost=31,
     )
     planes = call(
@@ -286,8 +292,8 @@
     partial = call(
         functools.partial(own_parity, blocks=far, **dims),
         shape((depth * pairs, 3 * filters, 2 * across), f32),
-        [vmem] * (1 + far) + [anywhere] * (far - 2),
-        [w_mine, mine[-1]] + mine[:-1] + behind[2:],
+        [vmem] * (1 + far),
+        [w_mine, mine[-1]] + mine[:-1],
         cost=28,
     )
     planes = call(
@@ -305,8 +311,8 @@
     pooled = call(
         functools.partial(finish, count=count, **dims),
         shape((filters * depth * height // 4, across // 2), bf16),
-        [smem] + [vmem] * 5,
-        (flags, w_mine, w_theirs, v, planes, swapped(planes)),
+        [vmem] * 5,
+        (w_mine, w_theirs, v, planes, swapped(planes)),
     )
     return pooled.reshape(filters, depth // 2, height // 2, across // 2)
 

time: 24.3 us -> 23.1 us (0.951)
  Pallas kernels: 6.13 us -> 5.45 us
  starting transfers between devices: 14 us -> 13.4 us
    pallas_call x9, Pallas kernels: 6.13 us -> 5.45 us  [call(): pl.pallas_call(body, out_shape=outs, in_specs=ins, out_specs=jax.tree.map...]
    ppermute x5, starting transfers between devices: 1.09 us -> 0.65 us  [swapped(): return lax.ppermute(x, 'filt', [(i, i ^ 1) for i in range(size)])]
    ppermute x5, waiting for transfers between devices: 0.1 us -> 0.43 us  [swapped(): return lax.ppermute(x, 'filt', [(i, i ^ 1) for i in range(size)])]
    ppermute x9, waiting for transfers between devices: 3.77 us -> 3.45 us  [shifted(): return lax.ppermute(x, ('filt', 'space'), pairs)]
where the time goes in v8:
time: 23.1 us; the launch traced here: 22.9 us
  starting transfers between devices  13.4 us (58%)
  Pallas kernels  5.45 us (24%)
  waiting for transfers between devices  3.88 us (17%)
    ppermute x9, starting transfers between devices, shifted(): return lax.ppermute(x, ('filt', 'space'), pairs)  12.8 us
    pallas_call x9, Pallas kernels, call(): pl.pallas_call(body, out_shape=outs, in_specs=ins, out_specs=jax.tree.map...  5.45 us
    ppermute x9, waiting for transfers between devices, shifted(): return lax.ppermute(x, ('filt', 'space'), pairs)  3.45 us
    ppermute x5, starting transfers between devices, swapped(): return lax.ppermute(x, 'filt', [(i, i ^ 1) for i in range(size)])  0.65 us
  transfers between devices with their start and end apart: 14, of which 5 were waited for; matrix products, arithmetic and copies ran while one was open for 0% of the time, Pallas kernels for 18%

profile of v8, /device:TPU:0, one launch (start us, length us, event | category | flops | bytes accessed | tf_op | source)
XLA Modules:
  0.0 22.9 jit_solution(15952600026698918293)
XLA Ops:
  0.0 4.0 %collective-permute-start = (bf16[16,4,4,128]{3,2,1,0:T(4,128)(2,1)}, bf16[16,4,4,128]{3,2,1,0:T(4,128)(2,1)S(1)}, u32[]{:S(2)}, u32[]{:S(2)}) collective-permute-start(bf16[16,4,4,128]{3,2,1,0:T(4,128)(2,1)} %param.3), channel_id=1, source_target_pairs={{0,16},{1,17},{2,18},{3,19},{4,20},{5,21},{6,22},{7,23},{8,24},{9,... | collective-permute-start | bytes 196616 | tf_op jit(solution)/shard_map/ppermute | solution.py:205
  4.0 1.0 %shard_map.37 = (bf16[256,128]{1,0:T(8,128)(2,1)S(1)}, bf16[64,128]{1,0:T(8,128)(2,1)S(1)}, bf16[1,32]{1,0:T(2,128)(2,1)S(1)}) custom-call(bf16[256,128]{1,0:T(8,128)(2,1)} %bitcast.24, bf16[1,32]{1,0:T(2,128)(2,1)} %bitcast.25), custom_call_target="tpu_custom_call" | custom-call | flops 4096 | bytes 256 | tf_op jit(solution)/shard_map/pallas_call | solution.py:226
  5.1 1.6 %collective-permute-start.8 = (bf16[64,128]{1,0:T(8,128)(2,1)S(1)}, bf16[64,128]{1,0:T(8,128)(2,1)S(1)}, u32[]{:S(2)}, u32[]{:S(2)}) collective-permute-start(bf16[64,128]{1,0:T(8,128)(2,1)S(1)} %get-tuple-element.16), channel_id=1, source_target_pairs={{0,1},{1,0},{2,3},{3,2},{4,5},{5,4},{6,7},{7,6},{8,9},{9,8},{10,11... | collective-permute-start | bytes 49160 | tf_op jit(solution)/shard_map/ppermute | solution.py:205
  6.6 0.0 collective-permute-start.9
  6.6 1.3 %collective-permute-done = bf16[16,4,4,128]{3,2,1,0:T(4,128)(2,1)S(1)} collective-permute-done((bf16[16,4,4,128]{3,2,1,0:T(4,128)(2,1)}, bf16[16,4,4,128]{3,2,1,0:T(4,128)(2,1)S(1)}, u32[]{:S(2)}, u32[]{:S(2)}) %collective-permute-start) | collective-permute-done | bytes 65568 | tf_op jit(solution)/shard_map/ppermute | solution.py:205
  7.9 0.2 shard_map.38._
  8.1 2.0 %collective-permute-start.1 = (bf16[512,128]{1,0:T(8,128)(2,1)S(1)}, bf16[512,128]{1,0:T(8,128)(2,1)S(1)}, u32[]{:S(2)}, u32[]{:S(2)}) collective-permute-start(bf16[512,128]{1,0:T(8,128)(2,1)S(1)} %shard_map.38._), channel_id=1, source_target_pairs={{0,12},{1,13},{2,14},{3,15},{4,8},{5,9},{6,10},{7,11},{8,4},{9,5},... | collective-permute-start | bytes 393224 | tf_op jit(solution)/shard_map/ppermute | solution.py:205
  10.1 0.5 %collective-permute-start.2 = (bf16[512,128]{1,0:T(8,128)(2,1)S(1)}, bf16[512,128]{1,0:T(8,128)(2,1)S(1)}, u32[]{:S(2)}, u32[]{:S(2)}) collective-permute-start(bf16[512,128]{1,0:T(8,128)(2,1)S(1)} %shard_map.38._), channel_id=1, source_target_pairs={{0,4},{1,5},{2,6},{3,7},{4,0},{5,1},{6,2},{7,3},{8,12},{9,13},{10,... | collective-permute-start | bytes 393224 | tf_op jit(solution)/shard_map/ppermute | solution.py:205
  10.6 1.0 %collective-permute-start.3 = (bf16[512,128]{1,0:T(8,128)(2,1)S(1)}, bf16[512,128]{1,0:T(8,128)(2,1)S(1)}, u32[]{:S(2)}, u32[]{:S(2)}) collective-permute-start(bf16[512,128]{1,0:T(8,128)(2,1)S(1)} %shard_map.38._), channel_id=1, source_target_pairs={{0,8},{1,9},{2,10},{3,11},{4,12},{5,13},{6,14},{7,15},{8,0},{9,1},... | collective-permute-start | bytes 393224 | tf_op jit(solution)/shard_map/ppermute | solution.py:205
  11.6 1.3 %shard_map.39 = (bf16[9,96,128]{2,1,0:T(8,128)(2,1)S(1)}, bf16[9,96,128]{2,1,0:T(8,128)(2,1)S(1)}, f32[32,128]{1,0:T(8,128)S(1)}) custom-call(bf16[512,128]{1,0:T(8,128)(2,1)S(1)} %shard_map.38._, bf16[864,256]{1,0:T(8,128)(2,1)} %bitcast.26, bf16[1,32]{1,0:T(2,128)(2,1)S(1)} %get-tuple-element.12.bias_ref), custom_call_target="tpu_custom_call" | custom-call | flops 2147483648 | bytes 256 | tf_op jit(solution)/shard_map/pallas_call | solution.py:226
  12.9 0.0 collective-permute-done.8.refs_1_
  13.0 1.1 %collective-permute-start.11 = (bf16[128,128]{1,0:T(8,128)(2,1)S(1)}, bf16[128,128]{1,0:T(8,128)(2,1)S(1)}, u32[]{:S(2)}, u32[]{:S(2)}) collective-permute-start(bf16[128,128]{1,0:T(8,128)(2,1)S(1)} %shard_map.42.refs_1_), channel_id=1, source_target_pairs={{0,8},{1,9},{2,10},{3,11},{4,12},{5,13},{6,14},{7,15},{8,0},{9,1},... | collective-permute-start | bytes 98312 | tf_op jit(solution)/shard_map/ppermute | solution.py:205
  14.1 2.2 %collective-permute-start.12 = (bf16[128,128]{1,0:T(8,128)(2,1)S(1)}, bf16[128,128]{1,0:T(8,128)(2,1)S(1)}, u32[]{:S(2)}, u32[]{:S(2)}) collective-permute-start(bf16[128,128]{1,0:T(8,128)(2,1)S(1)} %shard_map.42.refs_1_), channel_id=1, source_target_pairs={{0,12},{1,13},{2,14},{3,15},{4,8},{5,9},{6,10},{7,11},{8,4},{9,5},... | collective-permute-start | bytes 98312 | tf_op jit(solution)/shard_map/ppermute | solution.py:205
  16.2 0.4 %collective-permute-start.10 = (bf16[128,128]{1,0:T(8,128)(2,1)S(1)}, bf16[128,128]{1,0:T(8,128)(2,1)S(1)}, u32[]{:S(2)}, u32[]{:S(2)}) collective-permute-start(bf16[128,128]{1,0:T(8,128)(2,1)S(1)} %shard_map.43), channel_id=1, source_target_pairs={{0,4},{1,5},{2,6},{3,7},{4,0},{5,1},{6,2},{7,3},{8,12},{9,13},{10,... | collective-permute-start | bytes 98312 | tf_op jit(solution)/shard_map/ppermute | solution.py:205
  16.6 0.2 collective-permute-done.3
  16.8 0.3 %collective-permute-start.5 = (bf16[32,16,128]{2,1,0:T(8,128)(2,1)S(1)}, bf16[32,16,128]{2,1,0:T(8,128)(2,1)S(1)}, u32[]{:S(2)}, u32[]{:S(2)}) collective-permute-start(bf16[32,16,128]{2,1,0:T(8,128)(2,1)S(1)} %bitcast.19), channel_id=1, source_target_pairs={{0,2},{2,0},{4,6},{6,4},{8,10},{10,8},{12,14},{14,12},{16,18},{18,... | collective-permute-start | bytes 393224 | tf_op jit(solution)/shard_map/ppermute | solution.py:284
  17.1 0.8 %shard_map.40.sum_ref.refs_0_ = f32[8,96,256]{2,1,0:T(8,128)S(1)} custom-call(bf16[9,96,128]{2,1,0:T(8,128)(2,1)S(1)} %get-tuple-element.13.w_ref.refs_0_.w_mine_ref, bf16[32,16,128]{2,1,0:T(8,128)(2,1)S(1)} %bitcast.13, bf16[32,16,128]{2,1,0:T(8,128)(2,1)S(1)} %bitcast.18, bf16[32,16,128]{2,1,0:T(8,128)(2,1)S(1)} %bitcast.20, bf16[32,16,128]{2,1,0:T(8,128)(2,1)S(1)} %bitcast.21), custom_call_target="tpu_custom_call" | custom-call | flops 268435456 | bytes 256 | tf_op jit(solution)/shard_map/pallas_call | solution.py:226
  17.9 0.2 %collective-permute-start.6 = (bf16[32,16,128]{2,1,0:T(8,128)(2,1)S(1)}, bf16[32,16,128]{2,1,0:T(8,128)(2,1)S(1)}, u32[]{:S(2)}, u32[]{:S(2)}) collective-permute-start(bf16[32,16,128]{2,1,0:T(8,128)(2,1)S(1)} %bitcast.22), channel_id=1, source_target_pairs={{0,2},{2,0},{4,6},{6,4},{8,10},{10,8},{12,14},{14,12},{16,18},{18,... | collective-permute-start | bytes 393224 | tf_op jit(solution)/shard_map/ppermute | solution.py:284
  18.1 0.7 %collective-permute-done.12.refs_4_ = bf16[128,128]{1,0:T(8,128)(2,1)S(1)} collective-permute-done((bf16[128,128]{1,0:T(8,128)(2,1)S(1)}, bf16[128,128]{1,0:T(8,128)(2,1)S(1)}, u32[]{:S(2)}, u32[]{:S(2)}) %collective-permute-start.12) | collective-permute-done | bytes 32800 | tf_op jit(solution)/shard_map/ppermute | solution.py:205
  18.9 1.3 %collective-permute-done.10.refs_2_ = bf16[128,128]{1,0:T(8,128)(2,1)S(1)} collective-permute-done((bf16[128,128]{1,0:T(8,128)(2,1)S(1)}, bf16[128,128]{1,0:T(8,128)(2,1)S(1)}, u32[]{:S(2)}, u32[]{:S(2)}) %collective-permute-start.10) | collective-permute-done | bytes 32800 | tf_op jit(solution)/shard_map/ppermute | solution.py:205
  20.2 0.1 collective-permute-start.13
  20.3 0.9 %shard_map.41.v_ref = f32[16,32,128]{2,1,0:T(8,128)S(1)} custom-call(bf16[9,96,128]{2,1,0:T(8,128)(2,1)S(1)} %get-tuple-element.14.w_ref.w_theirs_ref, f32[32,128]{1,0:T(8,128)S(1)} %get-tuple-element.15.bias_ref, f32[8,96,256]{2,1,0:T(8,128)S(1)} %shard_map.40.sum_ref.refs_0_, bf16[32,16,128]{2,1,0:T(8,128)(2,1)S(1)} %collective-permute-done.4.refs_0_, ...), custom_call_target="tpu_custom_call" | custom-call | flops 4096 | bytes 256 | tf_op jit(solution)/shard_map/pallas_call | solution.py:226
  21.1 0.4 %collective-permute-done.13.refs_1_ = bf16[32,16,128]{2,1,0:T(8,128)(2,1)S(1)} collective-permute-done((bf16[32,16,128]{2,1,0:T(8,128)(2,1)S(1)}, bf16[32,16,128]{2,1,0:T(8,128)(2,1)S(1)}, u32[]{:S(2)}, u32[]{:S(2)}) %collective-permute-start.13) | collective-permute-done | bytes 131104 | tf_op jit(solution)/shard_map/ppermute | solution.py:284
  21.6 1.3 %shard_map.45 = bf16[128,64]{1,0:T(8,128)(2,1)} custom-call(bf16[9,96,128]{2,1,0:T(8,128)(2,1)S(1)} %get-tuple-element.13.w_ref.refs_0_.w_mine_ref, bf16[9,96,128]{2,1,0:T(8,128)(2,1)S(1)} %get-tuple-element.14.w_ref.w_theirs_ref, f32[16,32,128]{2,1,0:T(8,128)S(1)} %shard_map.41.v_ref, bf16[32,16,128]{2,1,0:T(8,128)(2,1)S(1)} %bitcast.16, ...), custom_call_target="tpu_custom_call" | custom-call | flops 4096 | bytes 256 | tf_op jit(solution)/shard_map/pallas_call | solution.py:226
  (13 shorter events, 0.0 us)
Async XLA Ops:
  0.0 7.9 %collective-permute-start = (bf16[16,4,4,128]{3,2,1,0:T(4,128)(2,1)}, bf16[16,4,4,128]{3,2,1,0:T(4,128)(2,1)S(1)}, u32[]{:S(2)}, u32[]{:S(2)}) collective-permute-start(bf16[16,4,4,128]{3,2,1,0:T(4,128)(2,1)} %param.3), channel_id=1, source_target_pairs={{0,16},{1,17},{2,18},{3,19},{4,20},{5,21},{6,22},{7,23},{8,24},{9,... | collective-permute-start | bytes 196616 | tf_op jit(solution)/shard_map/ppermute | solution.py:205
  5.1 7.9 %collective-permute-start.8 = (bf16[64,128]{1,0:T(8,128)(2,1)S(1)}, bf16[64,128]{1,0:T(8,128)(2,1)S(1)}, u32[]{:S(2)}, u32[]{:S(2)}) collective-permute-start(bf16[64,128]{1,0:T(8,128)(2,1)S(1)} %get-tuple-element.16), channel_id=1, source_target_pairs={{0,1},{1,0},{2,3},{3,2},{4,5},{5,4},{6,7},{7,6},{8,9},{9,8},{10,11... | collective-permute-start | bytes 49160 | tf_op jit(solution)/shard_map/ppermute | solution.py:205
  6.6 6.3 %collective-permute-start.9 = (bf16[64,128]{1,0:T(8,128)(2,1)S(1)}, bf16[64,128]{1,0:T(8,128)(2,1)S(1)}, u32[]{:S(2)}, u32[]{:S(2)}) collective-permute-start(bf16[64,128]{1,0:T(8,128)(2,1)S(1)} %get-tuple-element.16), channel_id=1, source_target_pairs={{0,17},{1,16},{2,19},{3,18},{4,21},{5,20},{6,23},{7,22},{8,25},{9,... | collective-permute-start | bytes 49160 | tf_op jit(solution)/shard_map/ppermute | solution.py:205
  8.1 8.1 %collective-permute-start.1 = (bf16[512,128]{1,0:T(8,128)(2,1)S(1)}, bf16[512,128]{1,0:T(8,128)(2,1)S(1)}, u32[]{:S(2)}, u32[]{:S(2)}) collective-permute-start(bf16[512,128]{1,0:T(8,128)(2,1)S(1)} %shard_map.38._), channel_id=1, source_target_pairs={{0,12},{1,13},{2,14},{3,15},{4,8},{5,9},{6,10},{7,11},{8,4},{9,5},... | collective-permute-start | bytes 393224 | tf_op jit(solution)/shard_map/ppermute | solution.py:205
  10.1 6.4 %collective-permute-start.2 = (bf16[512,128]{1,0:T(8,128)(2,1)S(1)}, bf16[512,128]{1,0:T(8,128)(2,1)S(1)}, u32[]{:S(2)}, u32[]{:S(2)}) collective-permute-start(bf16[512,128]{1,0:T(8,128)(2,1)S(1)} %shard_map.38._), channel_id=1, source_target_pairs={{0,4},{1,5},{2,6},{3,7},{4,0},{5,1},{6,2},{7,3},{8,12},{9,13},{10,... | collective-permute-start | bytes 393224 | tf_op jit(solution)/shard_map/ppermute | solution.py:205
  10.6 6.1 %collective-permute-start.3 = (bf16[512,128]{1,0:T(8,128)(2,1)S(1)}, bf16[512,128]{1,0:T(8,128)(2,1)S(1)}, u32[]{:S(2)}, u32[]{:S(2)}) collective-permute-start(bf16[512,128]{1,0:T(8,128)(2,1)S(1)} %shard_map.38._), channel_id=1, source_target_pairs={{0,8},{1,9},{2,10},{3,11},{4,12},{5,13},{6,14},{7,15},{8,0},{9,1},... | collective-permute-start | bytes 393224 | tf_op jit(solution)/shard_map/ppermute | solution.py:205
  13.0 4.9 %collective-permute-start.11 = (bf16[128,128]{1,0:T(8,128)(2,1)S(1)}, bf16[128,128]{1,0:T(8,128)(2,1)S(1)}, u32[]{:S(2)}, u32[]{:S(2)}) collective-permute-start(bf16[128,128]{1,0:T(8,128)(2,1)S(1)} %shard_map.42.refs_1_), channel_id=1, source_target_pairs={{0,8},{1,9},{2,10},{3,11},{4,12},{5,13},{6,14},{7,15},{8,0},{9,1},... | collective-permute-start | bytes 98312 | tf_op jit(solution)/shard_map/ppermute | solution.py:205
  14.1 4.8 %collective-permute-start.12 = (bf16[128,128]{1,0:T(8,128)(2,1)S(1)}, bf16[128,128]{1,0:T(8,128)(2,1)S(1)}, u32[]{:S(2)}, u32[]{:S(2)}) collective-permute-start(bf16[128,128]{1,0:T(8,128)(2,1)S(1)} %shard_map.42.refs_1_), channel_id=1, source_target_pairs={{0,12},{1,13},{2,14},{3,15},{4,8},{5,9},{6,10},{7,11},{8,4},{9,5},... | collective-permute-start | bytes 98312 | tf_op jit(solution)/shard_map/ppermute | solution.py:205
  16.2 3.9 %collective-permute-start.10 = (bf16[128,128]{1,0:T(8,128)(2,1)S(1)}, bf16[128,128]{1,0:T(8,128)(2,1)S(1)}, u32[]{:S(2)}, u32[]{:S(2)}) collective-permute-start(bf16[128,128]{1,0:T(8,128)(2,1)S(1)} %shard_map.43), channel_id=1, source_target_pairs={{0,4},{1,5},{2,6},{3,7},{4,0},{5,1},{6,2},{7,3},{8,12},{9,13},{10,... | collective-permute-start | bytes 98312 | tf_op jit(solution)/shard_map/ppermute | solution.py:205
  16.6 3.6 %collective-permute-start.4 = (bf16[32,16,128]{2,1,0:T(8,128)(2,1)S(1)}, bf16[32,16,128]{2,1,0:T(8,128)(2,1)S(1)}, u32[]{:S(2)}, u32[]{:S(2)}) collective-permute-start(bf16[32,16,128]{2,1,0:T(8,128)(2,1)S(1)} %bitcast.17), channel_id=1, source_target_pairs={{0,2},{2,0},{4,6},{6,4},{8,10},{10,8},{12,14},{14,12},{16,18},{18,... | collective-permute-start | bytes 393224 | tf_op jit(solution)/shard_map/ppermute | solution.py:284
  16.8 3.5 %collective-permute-start.5 = (bf16[32,16,128]{2,1,0:T(8,128)(2,1)S(1)}, bf16[32,16,128]{2,1,0:T(8,128)(2,1)S(1)}, u32[]{:S(2)}, u32[]{:S(2)}) collective-permute-start(bf16[32,16,128]{2,1,0:T(8,128)(2,1)S(1)} %bitcast.19), channel_id=1, source_target_pairs={{0,2},{2,0},{4,6},{6,4},{8,10},{10,8},{12,14},{14,12},{16,18},{18,... | collective-permute-start | bytes 393224 | tf_op jit(solution)/shard_map/ppermute | solution.py:284
  17.9 2.4 %collective-permute-start.6 = (bf16[32,16,128]{2,1,0:T(8,128)(2,1)S(1)}, bf16[32,16,128]{2,1,0:T(8,128)(2,1)S(1)}, u32[]{:S(2)}, u32[]{:S(2)}) collective-permute-start(bf16[32,16,128]{2,1,0:T(8,128)(2,1)S(1)} %bitcast.22), channel_id=1, source_target_pairs={{0,2},{2,0},{4,6},{6,4},{8,10},{10,8},{12,14},{14,12},{16,18},{18,... | collective-permute-start | bytes 393224 | tf_op jit(solution)/shard_map/ppermute | solution.py:284
  18.9 1.4 %collective-permute-start.7 = (bf16[32,16,128]{2,1,0:T(8,128)(2,1)S(1)}, bf16[32,16,128]{2,1,0:T(8,128)(2,1)S(1)}, u32[]{:S(2)}, u32[]{:S(2)}) collective-permute-start(bf16[32,16,128]{2,1,0:T(8,128)(2,1)S(1)} %bitcast.14), channel_id=1, source_target_pairs={{0,2},{2,0},{4,6},{6,4},{8,10},{10,8},{12,14},{14,12},{16,18},{18,... | collective-permute-start | bytes 393224 | tf_op jit(solution)/shard_map/ppermute | solution.py:284
  20.2 1.4 %collective-permute-start.13 = (bf16[32,16,128]{2,1,0:T(8,128)(2,1)S(1)}, bf16[32,16,128]{2,1,0:T(8,128)(2,1)S(1)}, u32[]{:S(2)}, u32[]{:S(2)}) collective-permute-start(bf16[32,16,128]{2,1,0:T(8,128)(2,1)S(1)} %bitcast.15), channel_id=1, source_target_pairs={{0,2},{2,0},{4,6},{6,4},{8,10},{10,8},{12,14},{14,12},{16,18},{18,... | collective-permute-start | bytes 393224 | tf_op jit(solution)/shard_map/ppermute | solution.py:284

commit v9 on v8

--- a/solution.py
+++ b/solution.py
@@ -257,20 +257,21 @@
         (own_block, far_block.reshape(cells, across)),
         cost=31,
     )
+    planes = call(
+        join,
+        shape((2 * extra * beside, across), bf16),
+        [anywhere] + [vmem] * (2 * extra),
+        [pair] + own_planes + far_planes,
+        cost=31,
+    )
+
     ordered = shape((9, 3 * filters, cin // 2), bf16)
     w_mine, w_theirs, bias = call(
         functools.partial(prepare, block=block),
         (ordered, ordered, shape((filters, across), f32)),
         [anywhere, hbm, vmem],
-        (pair, pinned(weights), bias),
+        (planes, pinned(weights), bias),
         [pltpu.VMEM(weights.shape, bf16), pltpu.SemaphoreType.DMA(())],
-        cost=31,
-    )
-    planes = call(
-        join,
-        shape((2 * extra * beside, across), bf16),
-        [anywhere] + [vmem] * (2 * extra),
-        [w_mine] + own_planes + far_planes,
         cost=31,
     )
 
@@ -284,7 +285,8 @@
         return lax.ppermute(x, "filt", [(i, i ^ 1) for i in range(size)])
 
     mine = near(pair)
-    theirs = [swapped(x) for x in mine]
+    first = call(join, shape(pair.shape, bf16), [anywhere, vmem], (w_mine, pair))
+    theirs = [swapped(x) for x in [first.reshape(-1, block, across)] + mine[1:]]
     dims = dict(depth=depth, height=height)
     again = call(join, shape(planes.shape, bf16), [anywhere, vmem], (mine[-1], planes), cost=12)
     behind = [shifted(planes, r, 0, size, count) for r in range(2, far)]

time: 23.1 us -> 23.2 us (level)
  starting transfers between devices: 13.4 us -> 14.7 us
  waiting for transfers between devices: 3.88 us -> 2.82 us
    ppermute x9, waiting for transfers between devices: 3.45 us -> 1.96 us  [shifted(): return lax.ppermute(x, ('filt', 'space'), pairs)]
    ppermute x5, starting transfers between devices: 0.65 us -> 1.29 us  [swapped(): return lax.ppermute(x, 'filt', [(i, i ^ 1) for i in range(size)])]
    ppermute x9, starting transfers between devices: 12.8 us -> 13.4 us  [shifted(): return lax.ppermute(x, ('filt', 'space'), pairs)]
    ppermute x5, waiting for transfers between devices: 0.43 us -> 0.85 us  [swapped(): return lax.ppermute(x, 'filt', [(i, i ^ 1) for i in range(size)])]
    pallas_call x9 -> x10, Pallas kernels: 5.45 us -> 5.46 us  [call(): pl.pallas_call(body, out_shape=outs, in_specs=ins, out_specs=jax.tree.map...]
where the time goes in v9:
time: 23.2 us; the launch traced here: 23 us
  starting transfers between devices  14.7 us (63%)
  Pallas kernels  5.46 us (24%)
  waiting for transfers between devices  2.82 us (12%)
    ppermute x9, starting transfers between devices, shifted(): return lax.ppermute(x, ('filt', 'space'), pairs)  13.4 us
    pallas_call x10, Pallas kernels, call(): pl.pallas_call(body, out_shape=outs, in_specs=ins, out_specs=jax.tree.map...  5.46 us
    ppermute x9, waiting for transfers between devices, shifted(): return lax.ppermute(x, ('filt', 'space'), pairs)  1.96 us
    ppermute x5, starting transfers between devices, swapped(): return lax.ppermute(x, 'filt', [(i, i ^ 1) for i in range(size)])  1.29 us
    ppermute x5, waiting for transfers between devices, swapped(): return lax.ppermute(x, 'filt', [(i, i ^ 1) for i in range(size)])  0.85 us
  transfers between devices with their start and end apart: 14, of which 5 were waited for; matrix products, arithmetic and copies ran while one was open for 0% of the time, Pallas kernels for 18%

profile of v9, /device:TPU:0, one launch (start us, length us, event | category | flops | bytes accessed | tf_op | source)
XLA Modules:
  0.0 23.0 jit_solution(2707305510872882513)
XLA Ops:
  0.0 4.0 %collective-permute-start = (bf16[16,4,4,128]{3,2,1,0:T(4,128)(2,1)}, bf16[16,4,4,128]{3,2,1,0:T(4,128)(2,1)S(1)}, u32[]{:S(2)}, u32[]{:S(2)}) collective-permute-start(bf16[16,4,4,128]{3,2,1,0:T(4,128)(2,1)} %param.3), channel_id=1, source_target_pairs={{0,16},{1,17},{2,18},{3,19},{4,20},{5,21},{6,22},{7,23},{8,24},{9,... | collective-permute-start | bytes 196616 | tf_op jit(solution)/shard_map/ppermute | solution.py:205
  4.0 1.0 %shard_map.37 = (bf16[256,128]{1,0:T(8,128)(2,1)S(1)}, bf16[64,128]{1,0:T(8,128)(2,1)S(1)}, bf16[1,32]{1,0:T(2,128)(2,1)S(1)}) custom-call(bf16[256,128]{1,0:T(8,128)(2,1)} %bitcast.25, bf16[1,32]{1,0:T(2,128)(2,1)} %bitcast.26), custom_call_target="tpu_custom_call" | custom-call | flops 4096 | bytes 256 | tf_op jit(solution)/shard_map/pallas_call | solution.py:226
  5.1 1.6 %collective-permute-start.1 = (bf16[64,128]{1,0:T(8,128)(2,1)S(1)}, bf16[64,128]{1,0:T(8,128)(2,1)S(1)}, u32[]{:S(2)}, u32[]{:S(2)}) collective-permute-start(bf16[64,128]{1,0:T(8,128)(2,1)S(1)} %get-tuple-element.12), channel_id=1, source_target_pairs={{0,1},{1,0},{2,3},{3,2},{4,5},{5,4},{6,7},{7,6},{8,9},{9,8},{10,11... | collective-permute-start | bytes 49160 | tf_op jit(solution)/shard_map/ppermute | solution.py:205
  6.6 1.3 %collective-permute-done = bf16[16,4,4,128]{3,2,1,0:T(4,128)(2,1)S(1)} collective-permute-done((bf16[16,4,4,128]{3,2,1,0:T(4,128)(2,1)}, bf16[16,4,4,128]{3,2,1,0:T(4,128)(2,1)S(1)}, u32[]{:S(2)}, u32[]{:S(2)}) %collective-permute-start) | collective-permute-done | bytes 65568 | tf_op jit(solution)/shard_map/ppermute | solution.py:205
  7.9 0.2 shard_map.38.refs_0_.refs_1_
  8.1 2.0 %collective-permute-start.3 = (bf16[512,128]{1,0:T(8,128)(2,1)S(1)}, bf16[512,128]{1,0:T(8,128)(2,1)S(1)}, u32[]{:S(2)}, u32[]{:S(2)}) collective-permute-start(bf16[512,128]{1,0:T(8,128)(2,1)S(1)} %shard_map.38.refs_0_.refs_1_), channel_id=1, source_target_pairs={{0,12},{1,13},{2,14},{3,15},{4,8},{5,9},{6,10},{7,11},{8,4},{9,5},... | collective-permute-start | bytes 393224 | tf_op jit(solution)/shard_map/ppermute | solution.py:205
  10.1 0.5 %collective-permute-start.4 = (bf16[512,128]{1,0:T(8,128)(2,1)S(1)}, bf16[512,128]{1,0:T(8,128)(2,1)S(1)}, u32[]{:S(2)}, u32[]{:S(2)}) collective-permute-start(bf16[512,128]{1,0:T(8,128)(2,1)S(1)} %shard_map.38.refs_0_.refs_1_), channel_id=1, source_target_pairs={{0,4},{1,5},{2,6},{3,7},{4,0},{5,1},{6,2},{7,3},{8,12},{9,13},{10,... | collective-permute-start | bytes 393224 | tf_op jit(solution)/shard_map/ppermute | solution.py:205
  10.6 1.0 %collective-permute-start.5 = (bf16[512,128]{1,0:T(8,128)(2,1)S(1)}, bf16[512,128]{1,0:T(8,128)(2,1)S(1)}, u32[]{:S(2)}, u32[]{:S(2)}) collective-permute-start(bf16[512,128]{1,0:T(8,128)(2,1)S(1)} %shard_map.38.refs_0_.refs_1_), channel_id=1, source_target_pairs={{0,8},{1,9},{2,10},{3,11},{4,12},{5,13},{6,14},{7,15},{8,0},{9,1},... | collective-permute-start | bytes 393224 | tf_op jit(solution)/shard_map/ppermute | solution.py:205
  11.6 0.6 %collective-permute-done.2.refs_2_ = bf16[64,128]{1,0:T(8,128)(2,1)S(1)} collective-permute-done((bf16[64,128]{1,0:T(8,128)(2,1)S(1)}, bf16[64,128]{1,0:T(8,128)(2,1)S(1)}, u32[]{:S(2)}, u32[]{:S(2)}) %collective-permute-start.2) | collective-permute-done | bytes 16416 | tf_op jit(solution)/shard_map/ppermute | solution.py:205
  12.3 1.5 %collective-permute-start.11 = (bf16[128,128]{1,0:T(8,128)(2,1)S(1)}, bf16[128,128]{1,0:T(8,128)(2,1)S(1)}, u32[]{:S(2)}, u32[]{:S(2)}) collective-permute-start(bf16[128,128]{1,0:T(8,128)(2,1)S(1)} %shard_map.39._.refs_1_), channel_id=1, source_target_pairs={{0,8},{1,9},{2,10},{3,11},{4,12},{5,13},{6,14},{7,15},{8,0},{9,1},... | collective-permute-start | bytes 98312 | tf_op jit(solution)/shard_map/ppermute | solution.py:205
  13.8 1.4 %collective-permute-start.12 = (bf16[128,128]{1,0:T(8,128)(2,1)S(1)}, bf16[128,128]{1,0:T(8,128)(2,1)S(1)}, u32[]{:S(2)}, u32[]{:S(2)}) collective-permute-start(bf16[128,128]{1,0:T(8,128)(2,1)S(1)} %shard_map.39._.refs_1_), channel_id=1, source_target_pairs={{0,12},{1,13},{2,14},{3,15},{4,8},{5,9},{6,10},{7,11},{8,4},{9,5},... | collective-permute-start | bytes 98312 | tf_op jit(solution)/shard_map/ppermute | solution.py:205
  15.2 0.1 collective-permute-done.3
  15.2 1.3 %collective-permute-start.10 = (bf16[128,128]{1,0:T(8,128)(2,1)S(1)}, bf16[128,128]{1,0:T(8,128)(2,1)S(1)}, u32[]{:S(2)}, u32[]{:S(2)}) collective-permute-start(bf16[128,128]{1,0:T(8,128)(2,1)S(1)} %shard_map.44), channel_id=1, source_target_pairs={{0,4},{1,5},{2,6},{3,7},{4,0},{5,1},{6,2},{7,3},{8,12},{9,13},{10,... | collective-permute-start | bytes 98312 | tf_op jit(solution)/shard_map/ppermute | solution.py:205
  16.6 1.3 %shard_map.40 = (bf16[9,96,128]{2,1,0:T(8,128)(2,1)S(1)}, bf16[9,96,128]{2,1,0:T(8,128)(2,1)S(1)}, f32[32,128]{1,0:T(8,128)S(1)}) custom-call(bf16[128,128]{1,0:T(8,128)(2,1)S(1)} %shard_map.39._.refs_1_, bf16[864,256]{1,0:T(8,128)(2,1)} %bitcast.27, bf16[1,32]{1,0:T(2,128)(2,1)S(1)} %get-tuple-element.13.bias_ref), custom_call_target="tpu_custom_call" | custom-call | flops 2147483648 | bytes 256 | tf_op jit(solution)/shard_map/pallas_call | solution.py:226
  17.9 0.1 collective-permute-start.6
  18.0 0.5 %collective-permute-start.7 = (bf16[32,16,128]{2,1,0:T(8,128)(2,1)S(1)}, bf16[32,16,128]{2,1,0:T(8,128)(2,1)S(1)}, u32[]{:S(2)}, u32[]{:S(2)}) collective-permute-start(bf16[32,16,128]{2,1,0:T(8,128)(2,1)S(1)} %bitcast.19), channel_id=1, source_target_pairs={{0,2},{2,0},{4,6},{6,4},{8,10},{10,8},{12,14},{14,12},{16,18},{18,... | collective-permute-start | bytes 393224 | tf_op jit(solution)/shard_map/ppermute | solution.py:285
  18.5 0.8 %shard_map.41.sum_ref.refs_0_ = f32[8,96,256]{2,1,0:T(8,128)S(1)} custom-call(bf16[9,96,128]{2,1,0:T(8,128)(2,1)S(1)} %get-tuple-element.14.w_ref.refs_0_.w_mine_ref, bf16[32,16,128]{2,1,0:T(8,128)(2,1)S(1)} %bitcast.14, bf16[32,16,128]{2,1,0:T(8,128)(2,1)S(1)} %bitcast.16, bf16[32,16,128]{2,1,0:T(8,128)(2,1)S(1)} %bitcast.20, bf16[32,16,128]{2,1,0:T(8,128)(2,1)S(1)} %bitcast.21), custom_call_target="tpu_custom_call" | custom-call | flops 268435456 | bytes 256 | tf_op jit(solution)/shard_map/pallas_call | solution.py:226
  19.3 0.2 collective-permute-start.8
  19.4 0.4 %collective-permute-start.9 = (bf16[32,16,128]{2,1,0:T(8,128)(2,1)S(1)}, bf16[32,16,128]{2,1,0:T(8,128)(2,1)S(1)}, u32[]{:S(2)}, u32[]{:S(2)}) collective-permute-start(bf16[32,16,128]{2,1,0:T(8,128)(2,1)S(1)} %bitcast.15), channel_id=1, source_target_pairs={{0,2},{2,0},{4,6},{6,4},{8,10},{10,8},{12,14},{14,12},{16,18},{18,... | collective-permute-start | bytes 393224 | tf_op jit(solution)/shard_map/ppermute | solution.py:285
  19.9 0.2 collective-permute-start.13
  20.0 0.7 %collective-permute-done.8.refs_2_ = bf16[32,16,128]{2,1,0:T(8,128)(2,1)S(1)} collective-permute-done((bf16[32,16,128]{2,1,0:T(8,128)(2,1)S(1)}, bf16[32,16,128]{2,1,0:T(8,128)(2,1)S(1)}, u32[]{:S(2)}, u32[]{:S(2)}) %collective-permute-start.8) | collective-permute-done | bytes 131104 | tf_op jit(solution)/shard_map/ppermute | solution.py:285
  20.7 0.2 collective-permute-done.9.refs_3_
  20.9 0.9 %shard_map.43.v_ref = f32[16,32,128]{2,1,0:T(8,128)S(1)} custom-call(bf16[9,96,128]{2,1,0:T(8,128)(2,1)S(1)} %get-tuple-element.15.w_ref.w_theirs_ref, f32[32,128]{1,0:T(8,128)S(1)} %get-tuple-element.16.bias_ref, f32[8,96,256]{2,1,0:T(8,128)S(1)} %shard_map.41.sum_ref.refs_0_, bf16[32,16,128]{2,1,0:T(8,128)(2,1)S(1)} %collective-permute-done.6.refs_0_, ...), custom_call_target="tpu_custom_call" | custom-call | flops 4096 | bytes 256 | tf_op jit(solution)/shard_map/pallas_call | solution.py:226
  21.8 1.3 %shard_map.46 = bf16[128,64]{1,0:T(8,128)(2,1)} custom-call(bf16[9,96,128]{2,1,0:T(8,128)(2,1)S(1)} %get-tuple-element.14.w_ref.refs_0_.w_mine_ref, bf16[9,96,128]{2,1,0:T(8,128)(2,1)S(1)} %get-tuple-element.15.w_ref.w_theirs_ref, f32[16,32,128]{2,1,0:T(8,128)S(1)} %shard_map.43.v_ref, bf16[32,16,128]{2,1,0:T(8,128)(2,1)S(1)} %bitcast.18, ...), custom_call_target="tpu_custom_call" | custom-call | flops 4096 | bytes 256 | tf_op jit(solution)/shard_map/pallas_call | solution.py:226
  (14 shorter events, 0.1 us)
Async XLA Ops:
  0.0 7.9 %collective-permute-start = (bf16[16,4,4,128]{3,2,1,0:T(4,128)(2,1)}, bf16[16,4,4,128]{3,2,1,0:T(4,128)(2,1)S(1)}, u32[]{:S(2)}, u32[]{:S(2)}) collective-permute-start(bf16[16,4,4,128]{3,2,1,0:T(4,128)(2,1)} %param.3), channel_id=1, source_target_pairs={{0,16},{1,17},{2,18},{3,19},{4,20},{5,21},{6,22},{7,23},{8,24},{9,... | collective-permute-start | bytes 196616 | tf_op jit(solution)/shard_map/ppermute | solution.py:205
  5.1 6.6 %collective-permute-start.1 = (bf16[64,128]{1,0:T(8,128)(2,1)S(1)}, bf16[64,128]{1,0:T(8,128)(2,1)S(1)}, u32[]{:S(2)}, u32[]{:S(2)}) collective-permute-start(bf16[64,128]{1,0:T(8,128)(2,1)S(1)} %get-tuple-element.12), channel_id=1, source_target_pairs={{0,1},{1,0},{2,3},{3,2},{4,5},{5,4},{6,7},{7,6},{8,9},{9,8},{10,11... | collective-permute-start | bytes 49160 | tf_op jit(solution)/shard_map/ppermute | solution.py:205
  6.6 5.6 %collective-permute-start.2 = (bf16[64,128]{1,0:T(8,128)(2,1)S(1)}, bf16[64,128]{1,0:T(8,128)(2,1)S(1)}, u32[]{:S(2)}, u32[]{:S(2)}) collective-permute-start(bf16[64,128]{1,0:T(8,128)(2,1)S(1)} %get-tuple-element.12), channel_id=1, source_target_pairs={{0,17},{1,16},{2,19},{3,18},{4,21},{5,20},{6,23},{7,22},{8,25},{9,... | collective-permute-start | bytes 49160 | tf_op jit(solution)/shard_map/ppermute | solution.py:205
  8.1 7.1 %collective-permute-start.3 = (bf16[512,128]{1,0:T(8,128)(2,1)S(1)}, bf16[512,128]{1,0:T(8,128)(2,1)S(1)}, u32[]{:S(2)}, u32[]{:S(2)}) collective-permute-start(bf16[512,128]{1,0:T(8,128)(2,1)S(1)} %shard_map.38.refs_0_.refs_1_), channel_id=1, source_target_pairs={{0,12},{1,13},{2,14},{3,15},{4,8},{5,9},{6,10},{7,11},{8,4},{9,5},... | collective-permute-start | bytes 393224 | tf_op jit(solution)/shard_map/ppermute | solution.py:205
  10.1 7.8 %collective-permute-start.4 = (bf16[512,128]{1,0:T(8,128)(2,1)S(1)}, bf16[512,128]{1,0:T(8,128)(2,1)S(1)}, u32[]{:S(2)}, u32[]{:S(2)}) collective-permute-start(bf16[512,128]{1,0:T(8,128)(2,1)S(1)} %shard_map.38.refs_0_.refs_1_), channel_id=1, source_target_pairs={{0,4},{1,5},{2,6},{3,7},{4,0},{5,1},{6,2},{7,3},{8,12},{9,13},{10,... | collective-permute-start | bytes 393224 | tf_op jit(solution)/shard_map/ppermute | solution.py:205
  10.6 7.3 %collective-permute-start.5 = (bf16[512,128]{1,0:T(8,128)(2,1)S(1)}, bf16[512,128]{1,0:T(8,128)(2,1)S(1)}, u32[]{:S(2)}, u32[]{:S(2)}) collective-permute-start(bf16[512,128]{1,0:T(8,128)(2,1)S(1)} %shard_map.38.refs_0_.refs_1_), channel_id=1, source_target_pairs={{0,8},{1,9},{2,10},{3,11},{4,12},{5,13},{6,14},{7,15},{8,0},{9,1},... | collective-permute-start | bytes 393224 | tf_op jit(solution)/shard_map/ppermute | solution.py:205
  12.3 7.0 %collective-permute-start.11 = (bf16[128,128]{1,0:T(8,128)(2,1)S(1)}, bf16[128,128]{1,0:T(8,128)(2,1)S(1)}, u32[]{:S(2)}, u32[]{:S(2)}) collective-permute-start(bf16[128,128]{1,0:T(8,128)(2,1)S(1)} %shard_map.39._.refs_1_), channel_id=1, source_target_pairs={{0,8},{1,9},{2,10},{3,11},{4,12},{5,13},{6,14},{7,15},{8,0},{9,1},... | collective-permute-start | bytes 98312 | tf_op jit(solution)/shard_map/ppermute | solution.py:205
  13.8 5.7 %collective-permute-start.12 = (bf16[128,128]{1,0:T(8,128)(2,1)S(1)}, bf16[128,128]{1,0:T(8,128)(2,1)S(1)}, u32[]{:S(2)}, u32[]{:S(2)}) collective-permute-start(bf16[128,128]{1,0:T(8,128)(2,1)S(1)} %shard_map.39._.refs_1_), channel_id=1, source_target_pairs={{0,12},{1,13},{2,14},{3,15},{4,8},{5,9},{6,10},{7,11},{8,4},{9,5},... | collective-permute-start | bytes 98312 | tf_op jit(solution)/shard_map/ppermute | solution.py:205
  15.2 4.6 %collective-permute-start.10 = (bf16[128,128]{1,0:T(8,128)(2,1)S(1)}, bf16[128,128]{1,0:T(8,128)(2,1)S(1)}, u32[]{:S(2)}, u32[]{:S(2)}) collective-permute-start(bf16[128,128]{1,0:T(8,128)(2,1)S(1)} %shard_map.44), channel_id=1, source_target_pairs={{0,4},{1,5},{2,6},{3,7},{4,0},{5,1},{6,2},{7,3},{8,12},{9,13},{10,... | collective-permute-start | bytes 98312 | tf_op jit(solution)/shard_map/ppermute | solution.py:205
  17.9 2.1 %collective-permute-start.6 = (bf16[32,16,128]{2,1,0:T(8,128)(2,1)S(1)}, bf16[32,16,128]{2,1,0:T(8,128)(2,1)S(1)}, u32[]{:S(2)}, u32[]{:S(2)}) collective-permute-start(bf16[32,16,128]{2,1,0:T(8,128)(2,1)S(1)} %bitcast.23), channel_id=1, source_target_pairs={{0,2},{2,0},{4,6},{6,4},{8,10},{10,8},{12,14},{14,12},{16,18},{18,... | collective-permute-start | bytes 393224 | tf_op jit(solution)/shard_map/ppermute | solution.py:285
  18.0 2.0 %collective-permute-start.7 = (bf16[32,16,128]{2,1,0:T(8,128)(2,1)S(1)}, bf16[32,16,128]{2,1,0:T(8,128)(2,1)S(1)}, u32[]{:S(2)}, u32[]{:S(2)}) collective-permute-start(bf16[32,16,128]{2,1,0:T(8,128)(2,1)S(1)} %bitcast.19), channel_id=1, source_target_pairs={{0,2},{2,0},{4,6},{6,4},{8,10},{10,8},{12,14},{14,12},{16,18},{18,... | collective-permute-start | bytes 393224 | tf_op jit(solution)/shard_map/ppermute | solution.py:285
  19.3 1.4 %collective-permute-start.8 = (bf16[32,16,128]{2,1,0:T(8,128)(2,1)S(1)}, bf16[32,16,128]{2,1,0:T(8,128)(2,1)S(1)}, u32[]{:S(2)}, u32[]{:S(2)}) collective-permute-start(bf16[32,16,128]{2,1,0:T(8,128)(2,1)S(1)} %bitcast.22), channel_id=1, source_target_pairs={{0,2},{2,0},{4,6},{6,4},{8,10},{10,8},{12,14},{14,12},{16,18},{18,... | collective-permute-start | bytes 393224 | tf_op jit(solution)/shard_map/ppermute | solution.py:285
  19.4 1.4 %collective-permute-start.9 = (bf16[32,16,128]{2,1,0:T(8,128)(2,1)S(1)}, bf16[32,16,128]{2,1,0:T(8,128)(2,1)S(1)}, u32[]{:S(2)}, u32[]{:S(2)}) collective-permute-start(bf16[32,16,128]{2,1,0:T(8,128)(2,1)S(1)} %bitcast.15), channel_id=1, source_target_pairs={{0,2},{2,0},{4,6},{6,4},{8,10},{10,8},{12,14},{14,12},{16,18},{18,... | collective-permute-start | bytes 393224 | tf_op jit(solution)/shard_map/ppermute | solution.py:285
  19.9 1.9 %collective-permute-start.13 = (bf16[32,16,128]{2,1,0:T(8,128)(2,1)S(1)}, bf16[32,16,128]{2,1,0:T(8,128)(2,1)S(1)}, u32[]{:S(2)}, u32[]{:S(2)}) collective-permute-start(bf16[32,16,128]{2,1,0:T(8,128)(2,1)S(1)} %bitcast.17), channel_id=1, source_target_pairs={{0,2},{2,0},{4,6},{6,4},{8,10},{10,8},{12,14},{14,12},{16,18},{18,... | collective-permute-start | bytes 393224 | tf_op jit(solution)/shard_map/ppermute | solution.py:285

commit v10 on v8

--- a/solution.py
+++ b/solution.py
@@ -51,10 +51,17 @@
 
 
 def prepare(
-    _, w_ref, bias_ref, w_mine_ref, w_theirs_ref, bias_out_ref, kernel_ref, done, *, block
+    w_ref, bias_ref, w_mine_ref, w_theirs_ref, bias_out_ref, kernel_ref, done, *, block
 ):
-    fetch = pltpu.make_async_copy(w_ref, kernel_ref, done)
-    fetch.start()
+    rows = w_ref.shape[0] // 9
+    fetches = [
+        pltpu.make_async_copy(
+            w_ref.at[pl.ds(k * rows, rows)], kernel_ref.at[pl.ds(k * rows, rows)], done.at[k]
+        )
+        for k in range(9)
+    ]
+    for fetch in fetches:
+        fetch.start()
     cin = kernel_ref.shape[-1]
     half = cin // 2
     far = half // block // 2
@@ -75,13 +82,14 @@
     bias_out_ref[...] = jnp.broadcast_to(
         jnp.sum(spread, axis=1, keepdims=True), bias_out_ref.shape
     )
-    fetch.wait()
+    for fetch in fetches:
+        fetch.wait()
     ordered = jnp.dot(kernel_ref[...], shuffle, preferred_element_type=f32).astype(bf16)
     w_mine_ref[...] = ordered[:, :half].reshape(w_mine_ref.shape)
     w_theirs_ref[...] = ordered[:, half:].reshape(w_theirs_ref.shape)
 
 
-def assemble(own_ref, far_ref, pair_ref, *, block):
+def assemble(_, own_ref, far_ref, pair_ref, *, block):
     size, across = own_ref.shape
     both = jnp.concatenate([own_ref[...], far_ref[...]], axis=1)
     moved = pick_rows(both, block, size // block, 0)
@@ -250,27 +258,28 @@
     sends = list(zip(edges, steps))
     far_planes = [shifted(x, far, step, size, count) for x, step in sends]
     own_planes = [shifted(x, 0, step, size, count) for x, step in sends]
-    pair = call(
-        functools.partial(assemble, block=block),
-        shape((2 * cells, across), bf16),
-        [vmem, vmem],
-        (own_block, far_block.reshape(cells, across)),
-        cost=31,
-    )
     ordered = shape((9, 3 * filters, cin // 2), bf16)
     w_mine, w_theirs, bias = call(
         functools.partial(prepare, block=block),
         (ordered, ordered, shape((filters, across), f32)),
-        [anywhere, hbm, vmem],
-        (pair, pinned(weights), bias),
-        [pltpu.VMEM(weights.shape, bf16), pltpu.SemaphoreType.DMA(())],
+        [hbm, vmem],
+        (pinned(weights), bias),
+        [pltpu.VMEM(weights.shape, bf16), pltpu.SemaphoreType.DMA((9,))],
+        cost=31,
+    )
+
+    pair = call(
+        functools.partial(assemble, block=block),
+        shape((2 * cells, across), bf16),
+        [anywhere, vmem, vmem],
+        (w_mine, own_block, far_block.reshape(cells, across)),
         cost=31,
     )
     planes = call(
         join,
         shape((2 * extra * beside, across), bf16),
         [anywhere] + [vmem] * (2 * extra),
-        [w_mine] + own_planes + far_planes,
+        [pair] + own_planes + far_planes,
         cost=31,
     )
 

time: 23.1 us -> 22.8 us (0.987)
  waiting for transfers between devices: 3.88 us -> 1.43 us
  starting transfers between devices: 13.4 us -> 15.6 us
    ppermute x9, waiting for transfers between devices: 3.45 us -> 0.57 us  [shifted(): return lax.ppermute(x, ('filt', 'space'), pairs)]
    ppermute x9, starting transfers between devices: 12.8 us -> 14.4 us  [shifted(): return lax.ppermute(x, ('filt', 'space'), pairs)]
    ppermute x5, starting transfers between devices: 0.65 us -> 1.19 us  [swapped(): return lax.ppermute(x, 'filt', [(i, i ^ 1) for i in range(size)])]
    ppermute x5, waiting for transfers between devices: 0.43 us -> 0.85 us  [swapped(): return lax.ppermute(x, 'filt', [(i, i ^ 1) for i in range(size)])]
  transfers between devices with their start and end apart: 14 -> 14, of which waited for: 5 -> 4; matrix products, arithmetic and copies ran while one was open for 0% -> 0% of each run, Pallas kernels for 18% -> 19%
where the time goes in v10:
time: 22.8 us; the launch traced here: 22.6 us
  starting transfers between devices  15.6 us (68%)
  Pallas kernels  5.49 us (24%)
  waiting for transfers between devices  1.43 us (6%)
    ppermute x9, starting transfers between devices, shifted(): return lax.ppermute(x, ('filt', 'space'), pairs)  14.4 us
    pallas_call x9, Pallas kernels, call(): pl.pallas_call(body, out_shape=outs, in_specs=ins, out_specs=jax.tree.map...  5.49 us
    ppermute x5, starting transfers between devices, swapped(): return lax.ppermute(x, 'filt', [(i, i ^ 1) for i in range(size)])  1.19 us
    ppermute x5, waiting for transfers between devices, swapped(): return lax.ppermute(x, 'filt', [(i, i ^ 1) for i in range(size)])  0.85 us
    ppermute x9, waiting for transfers between devices, shifted(): return lax.ppermute(x, ('filt', 'space'), pairs)  0.57 us
  transfers between devices with their start and end apart: 14, of which 4 were waited for; matrix products, arithmetic and copies ran while one was open for 0% of the time, Pallas kernels for 19%

profile of v10, /device:TPU:0, one launch (start us, length us, event | category | flops | bytes accessed | tf_op | source)
XLA Modules:
  0.0 22.6 jit_solution(298933376256386963)
XLA Ops:
  0.0 4.0 %collective-permute-start = (bf16[16,4,4,128]{3,2,1,0:T(4,128)(2,1)}, bf16[16,4,4,128]{3,2,1,0:T(4,128)(2,1)S(1)}, u32[]{:S(2)}, u32[]{:S(2)}) collective-permute-start(bf16[16,4,4,128]{3,2,1,0:T(4,128)(2,1)} %param.3), channel_id=1, source_target_pairs={{0,16},{1,17},{2,18},{3,19},{4,20},{5,21},{6,22},{7,23},{8,24},{9,... | collective-permute-start | bytes 196616 | tf_op jit(solution)/shard_map/ppermute | solution.py:213
  4.0 1.0 %shard_map.37 = (bf16[256,128]{1,0:T(8,128)(2,1)S(1)}, bf16[64,128]{1,0:T(8,128)(2,1)S(1)}, bf16[1,32]{1,0:T(2,128)(2,1)S(1)}) custom-call(bf16[256,128]{1,0:T(8,128)(2,1)} %bitcast.24, bf16[1,32]{1,0:T(2,128)(2,1)} %bitcast.25), custom_call_target="tpu_custom_call" | custom-call | flops 4096 | bytes 256 | tf_op jit(solution)/shard_map/pallas_call | solution.py:234
  5.1 1.6 %collective-permute-start.8 = (bf16[64,128]{1,0:T(8,128)(2,1)S(1)}, bf16[64,128]{1,0:T(8,128)(2,1)S(1)}, u32[]{:S(2)}, u32[]{:S(2)}) collective-permute-start(bf16[64,128]{1,0:T(8,128)(2,1)S(1)} %get-tuple-element.16), channel_id=1, source_target_pairs={{0,1},{1,0},{2,3},{3,2},{4,5},{5,4},{6,7},{7,6},{8,9},{9,8},{10,11... | collective-permute-start | bytes 49160 | tf_op jit(solution)/shard_map/ppermute | solution.py:213
  6.6 0.0 collective-permute-start.9
  6.6 1.3 %shard_map.38 = (bf16[9,96,128]{2,1,0:T(8,128)(2,1)S(1)}, bf16[9,96,128]{2,1,0:T(8,128)(2,1)S(1)}, f32[32,128]{1,0:T(8,128)S(1)}) custom-call(bf16[864,256]{1,0:T(8,128)(2,1)} %bitcast.26, bf16[1,32]{1,0:T(2,128)(2,1)S(1)} %get-tuple-element.11.bias_ref), custom_call_target="tpu_custom_call" | custom-call | flops 2147483648 | bytes 256 | tf_op jit(solution)/shard_map/pallas_call | solution.py:234
  8.0 0.2 shard_map.39.refs_0_
  8.2 2.9 %collective-permute-start.1 = (bf16[512,128]{1,0:T(8,128)(2,1)S(1)}, bf16[512,128]{1,0:T(8,128)(2,1)S(1)}, u32[]{:S(2)}, u32[]{:S(2)}) collective-permute-start(bf16[512,128]{1,0:T(8,128)(2,1)S(1)} %shard_map.39.refs_0_), channel_id=1, source_target_pairs={{0,12},{1,13},{2,14},{3,15},{4,8},{5,9},{6,10},{7,11},{8,4},{9,5},... | collective-permute-start | bytes 393224 | tf_op jit(solution)/shard_map/ppermute | solution.py:213
  11.1 0.5 %collective-permute-start.2 = (bf16[512,128]{1,0:T(8,128)(2,1)S(1)}, bf16[512,128]{1,0:T(8,128)(2,1)S(1)}, u32[]{:S(2)}, u32[]{:S(2)}) collective-permute-start(bf16[512,128]{1,0:T(8,128)(2,1)S(1)} %shard_map.39.refs_0_), channel_id=1, source_target_pairs={{0,4},{1,5},{2,6},{3,7},{4,0},{5,1},{6,2},{7,3},{8,12},{9,13},{10,... | collective-permute-start | bytes 393224 | tf_op jit(solution)/shard_map/ppermute | solution.py:213
  11.6 0.2 collective-permute-start.3
  11.7 0.4 %collective-permute-done.9.refs_2_ = bf16[64,128]{1,0:T(8,128)(2,1)S(1)} collective-permute-done((bf16[64,128]{1,0:T(8,128)(2,1)S(1)}, bf16[64,128]{1,0:T(8,128)(2,1)S(1)}, u32[]{:S(2)}, u32[]{:S(2)}) %collective-permute-start.9) | collective-permute-done | bytes 16416 | tf_op jit(solution)/shard_map/ppermute | solution.py:213
  12.2 1.6 %collective-permute-start.11 = (bf16[128,128]{1,0:T(8,128)(2,1)S(1)}, bf16[128,128]{1,0:T(8,128)(2,1)S(1)}, u32[]{:S(2)}, u32[]{:S(2)}) collective-permute-start(bf16[128,128]{1,0:T(8,128)(2,1)S(1)} %shard_map.42.refs_1_), channel_id=1, source_target_pairs={{0,8},{1,9},{2,10},{3,11},{4,12},{5,13},{6,14},{7,15},{8,0},{9,1},... | collective-permute-start | bytes 98312 | tf_op jit(solution)/shard_map/ppermute | solution.py:213
  13.8 1.5 %collective-permute-start.12 = (bf16[128,128]{1,0:T(8,128)(2,1)S(1)}, bf16[128,128]{1,0:T(8,128)(2,1)S(1)}, u32[]{:S(2)}, u32[]{:S(2)}) collective-permute-start(bf16[128,128]{1,0:T(8,128)(2,1)S(1)} %shard_map.42.refs_1_), channel_id=1, source_target_pairs={{0,12},{1,13},{2,14},{3,15},{4,8},{5,9},{6,10},{7,11},{8,4},{9,5},... | collective-permute-start | bytes 98312 | tf_op jit(solution)/shard_map/ppermute | solution.py:213
  15.3 2.2 %collective-permute-start.10 = (bf16[128,128]{1,0:T(8,128)(2,1)S(1)}, bf16[128,128]{1,0:T(8,128)(2,1)S(1)}, u32[]{:S(2)}, u32[]{:S(2)}) collective-permute-start(bf16[128,128]{1,0:T(8,128)(2,1)S(1)} %shard_map.43), channel_id=1, source_target_pairs={{0,4},{1,5},{2,6},{3,7},{4,0},{5,1},{6,2},{7,3},{8,12},{9,13},{10,... | collective-permute-start | bytes 98312 | tf_op jit(solution)/shard_map/ppermute | solution.py:213
  17.4 0.1 collective-permute-done.2
  17.5 0.0 collective-permute-done.3
  17.6 0.5 %collective-permute-start.7 = (bf16[32,16,128]{2,1,0:T(8,128)(2,1)S(1)}, bf16[32,16,128]{2,1,0:T(8,128)(2,1)S(1)}, u32[]{:S(2)}, u32[]{:S(2)}) collective-permute-start(bf16[32,16,128]{2,1,0:T(8,128)(2,1)S(1)} %bitcast.13), channel_id=1, source_target_pairs={{0,2},{2,0},{4,6},{6,4},{8,10},{10,8},{12,14},{14,12},{16,18},{18,... | collective-permute-start | bytes 393224 | tf_op jit(solution)/shard_map/ppermute | solution.py:293
  18.0 0.8 %shard_map.40.sum_ref.refs_0_ = f32[8,96,256]{2,1,0:T(8,128)S(1)} custom-call(bf16[9,96,128]{2,1,0:T(8,128)(2,1)S(1)} %get-tuple-element.12._.w_ref.w_mine_ref, bf16[32,16,128]{2,1,0:T(8,128)(2,1)S(1)} %bitcast.14, bf16[32,16,128]{2,1,0:T(8,128)(2,1)S(1)} %bitcast.18, bf16[32,16,128]{2,1,0:T(8,128)(2,1)S(1)} %bitcast.19, bf16[32,16,128]{2,1,0:T(8,128)(2,1)S(1)} %bitcast.21), custom_call_target="tpu_custom_call" | custom-call | flops 268435456 | bytes 256 | tf_op jit(solution)/shard_map/pallas_call | solution.py:234
  18.8 0.1 collective-permute-start.5
  18.9 0.5 %collective-permute-start.6 = (bf16[32,16,128]{2,1,0:T(8,128)(2,1)S(1)}, bf16[32,16,128]{2,1,0:T(8,128)(2,1)S(1)}, u32[]{:S(2)}, u32[]{:S(2)}) collective-permute-start(bf16[32,16,128]{2,1,0:T(8,128)(2,1)S(1)} %bitcast.22), channel_id=1, source_target_pairs={{0,2},{2,0},{4,6},{6,4},{8,10},{10,8},{12,14},{14,12},{16,18},{18,... | collective-permute-start | bytes 393224 | tf_op jit(solution)/shard_map/ppermute | solution.py:293
  19.4 0.2 collective-permute-start.13
  19.6 0.7 %collective-permute-done.5.refs_1_ = bf16[32,16,128]{2,1,0:T(8,128)(2,1)S(1)} collective-permute-done((bf16[32,16,128]{2,1,0:T(8,128)(2,1)S(1)}, bf16[32,16,128]{2,1,0:T(8,128)(2,1)S(1)}, u32[]{:S(2)}, u32[]{:S(2)}) %collective-permute-start.5) | collective-permute-done | bytes 131104 | tf_op jit(solution)/shard_map/ppermute | solution.py:293
  20.2 0.2 collective-permute-done.6.refs_2_
  20.4 0.9 %shard_map.41.v_ref = f32[16,32,128]{2,1,0:T(8,128)S(1)} custom-call(bf16[9,96,128]{2,1,0:T(8,128)(2,1)S(1)} %get-tuple-element.13.w_ref.w_theirs_ref, f32[32,128]{1,0:T(8,128)S(1)} %get-tuple-element.14.bias_ref, f32[8,96,256]{2,1,0:T(8,128)S(1)} %shard_map.40.sum_ref.refs_0_, bf16[32,16,128]{2,1,0:T(8,128)(2,1)S(1)} %collective-permute-done.4.refs_0_, ...), custom_call_target="tpu_custom_call" | custom-call | flops 4096 | bytes 256 | tf_op jit(solution)/shard_map/pallas_call | solution.py:234
  21.3 1.3 %shard_map.45 = bf16[128,64]{1,0:T(8,128)(2,1)} custom-call(bf16[9,96,128]{2,1,0:T(8,128)(2,1)S(1)} %get-tuple-element.12._.w_ref.w_mine_ref, bf16[9,96,128]{2,1,0:T(8,128)(2,1)S(1)} %get-tuple-element.13.w_ref.w_theirs_ref, f32[16,32,128]{2,1,0:T(8,128)S(1)} %shard_map.41.v_ref, bf16[32,16,128]{2,1,0:T(8,128)(2,1)S(1)} %bitcast.16, ...), custom_call_target="tpu_custom_call" | custom-call | flops 4096 | bytes 256 | tf_op jit(solution)/shard_map/pallas_call | solution.py:234
  (13 shorter events, 0.0 us)
Async XLA Ops:
  0.0 8.0 %collective-permute-start = (bf16[16,4,4,128]{3,2,1,0:T(4,128)(2,1)}, bf16[16,4,4,128]{3,2,1,0:T(4,128)(2,1)S(1)}, u32[]{:S(2)}, u32[]{:S(2)}) collective-permute-start(bf16[16,4,4,128]{3,2,1,0:T(4,128)(2,1)} %param.3), channel_id=1, source_target_pairs={{0,16},{1,17},{2,18},{3,19},{4,20},{5,21},{6,22},{7,23},{8,24},{9,... | collective-permute-start | bytes 196616 | tf_op jit(solution)/shard_map/ppermute | solution.py:213
  5.1 6.7 %collective-permute-start.8 = (bf16[64,128]{1,0:T(8,128)(2,1)S(1)}, bf16[64,128]{1,0:T(8,128)(2,1)S(1)}, u32[]{:S(2)}, u32[]{:S(2)}) collective-permute-start(bf16[64,128]{1,0:T(8,128)(2,1)S(1)} %get-tuple-element.16), channel_id=1, source_target_pairs={{0,1},{1,0},{2,3},{3,2},{4,5},{5,4},{6,7},{7,6},{8,9},{9,8},{10,11... | collective-permute-start | bytes 49160 | tf_op jit(solution)/shard_map/ppermute | solution.py:213
  6.6 5.5 %collective-permute-start.9 = (bf16[64,128]{1,0:T(8,128)(2,1)S(1)}, bf16[64,128]{1,0:T(8,128)(2,1)S(1)}, u32[]{:S(2)}, u32[]{:S(2)}) collective-permute-start(bf16[64,128]{1,0:T(8,128)(2,1)S(1)} %get-tuple-element.16), channel_id=1, source_target_pairs={{0,17},{1,16},{2,19},{3,18},{4,21},{5,20},{6,23},{7,22},{8,25},{9,... | collective-permute-start | bytes 49160 | tf_op jit(solution)/shard_map/ppermute | solution.py:213
  8.2 7.1 %collective-permute-start.1 = (bf16[512,128]{1,0:T(8,128)(2,1)S(1)}, bf16[512,128]{1,0:T(8,128)(2,1)S(1)}, u32[]{:S(2)}, u32[]{:S(2)}) collective-permute-start(bf16[512,128]{1,0:T(8,128)(2,1)S(1)} %shard_map.39.refs_0_), channel_id=1, source_target_pairs={{0,12},{1,13},{2,14},{3,15},{4,8},{5,9},{6,10},{7,11},{8,4},{9,5},... | collective-permute-start | bytes 393224 | tf_op jit(solution)/shard_map/ppermute | solution.py:213
  11.1 6.4 %collective-permute-start.2 = (bf16[512,128]{1,0:T(8,128)(2,1)S(1)}, bf16[512,128]{1,0:T(8,128)(2,1)S(1)}, u32[]{:S(2)}, u32[]{:S(2)}) collective-permute-start(bf16[512,128]{1,0:T(8,128)(2,1)S(1)} %shard_map.39.refs_0_), channel_id=1, source_target_pairs={{0,4},{1,5},{2,6},{3,7},{4,0},{5,1},{6,2},{7,3},{8,12},{9,13},{10,... | collective-permute-start | bytes 393224 | tf_op jit(solution)/shard_map/ppermute | solution.py:213
  11.6 6.0 %collective-permute-start.3 = (bf16[512,128]{1,0:T(8,128)(2,1)S(1)}, bf16[512,128]{1,0:T(8,128)(2,1)S(1)}, u32[]{:S(2)}, u32[]{:S(2)}) collective-permute-start(bf16[512,128]{1,0:T(8,128)(2,1)S(1)} %shard_map.39.refs_0_), channel_id=1, source_target_pairs={{0,8},{1,9},{2,10},{3,11},{4,12},{5,13},{6,14},{7,15},{8,0},{9,1},... | collective-permute-start | bytes 393224 | tf_op jit(solution)/shard_map/ppermute | solution.py:213
  12.2 6.6 %collective-permute-start.11 = (bf16[128,128]{1,0:T(8,128)(2,1)S(1)}, bf16[128,128]{1,0:T(8,128)(2,1)S(1)}, u32[]{:S(2)}, u32[]{:S(2)}) collective-permute-start(bf16[128,128]{1,0:T(8,128)(2,1)S(1)} %shard_map.42.refs_1_), channel_id=1, source_target_pairs={{0,8},{1,9},{2,10},{3,11},{4,12},{5,13},{6,14},{7,15},{8,0},{9,1},... | collective-permute-start | bytes 98312 | tf_op jit(solution)/shard_map/ppermute | solution.py:213
  13.8 5.2 %collective-permute-start.12 = (bf16[128,128]{1,0:T(8,128)(2,1)S(1)}, bf16[128,128]{1,0:T(8,128)(2,1)S(1)}, u32[]{:S(2)}, u32[]{:S(2)}) collective-permute-start(bf16[128,128]{1,0:T(8,128)(2,1)S(1)} %shard_map.42.refs_1_), channel_id=1, source_target_pairs={{0,12},{1,13},{2,14},{3,15},{4,8},{5,9},{6,10},{7,11},{8,4},{9,5},... | collective-permute-start | bytes 98312 | tf_op jit(solution)/shard_map/ppermute | solution.py:213
  15.3 4.1 %collective-permute-start.10 = (bf16[128,128]{1,0:T(8,128)(2,1)S(1)}, bf16[128,128]{1,0:T(8,128)(2,1)S(1)}, u32[]{:S(2)}, u32[]{:S(2)}) collective-permute-start(bf16[128,128]{1,0:T(8,128)(2,1)S(1)} %shard_map.43), channel_id=1, source_target_pairs={{0,4},{1,5},{2,6},{3,7},{4,0},{5,1},{6,2},{7,3},{8,12},{9,13},{10,... | collective-permute-start | bytes 98312 | tf_op jit(solution)/shard_map/ppermute | solution.py:213
  17.5 2.0 %collective-permute-start.4 = (bf16[32,16,128]{2,1,0:T(8,128)(2,1)S(1)}, bf16[32,16,128]{2,1,0:T(8,128)(2,1)S(1)}, u32[]{:S(2)}, u32[]{:S(2)}) collective-permute-start(bf16[32,16,128]{2,1,0:T(8,128)(2,1)S(1)} %bitcast.17), channel_id=1, source_target_pairs={{0,2},{2,0},{4,6},{6,4},{8,10},{10,8},{12,14},{14,12},{16,18},{18,... | collective-permute-start | bytes 393224 | tf_op jit(solution)/shard_map/ppermute | solution.py:293
  17.6 2.0 %collective-permute-start.7 = (bf16[32,16,128]{2,1,0:T(8,128)(2,1)S(1)}, bf16[32,16,128]{2,1,0:T(8,128)(2,1)S(1)}, u32[]{:S(2)}, u32[]{:S(2)}) collective-permute-start(bf16[32,16,128]{2,1,0:T(8,128)(2,1)S(1)} %bitcast.13), channel_id=1, source_target_pairs={{0,2},{2,0},{4,6},{6,4},{8,10},{10,8},{12,14},{14,12},{16,18},{18,... | collective-permute-start | bytes 393224 | tf_op jit(solution)/shard_map/ppermute | solution.py:293
  18.8 1.4 %collective-permute-start.5 = (bf16[32,16,128]{2,1,0:T(8,128)(2,1)S(1)}, bf16[32,16,128]{2,1,0:T(8,128)(2,1)S(1)}, u32[]{:S(2)}, u32[]{:S(2)}) collective-permute-start(bf16[32,16,128]{2,1,0:T(8,128)(2,1)S(1)} %bitcast.20), channel_id=1, source_target_pairs={{0,2},{2,0},{4,6},{6,4},{8,10},{10,8},{12,14},{14,12},{16,18},{18,... | collective-permute-start | bytes 393224 | tf_op jit(solution)/shard_map/ppermute | solution.py:293
  18.9 1.5 %collective-permute-start.6 = (bf16[32,16,128]{2,1,0:T(8,128)(2,1)S(1)}, bf16[32,16,128]{2,1,0:T(8,128)(2,1)S(1)}, u32[]{:S(2)}, u32[]{:S(2)}) collective-permute-start(bf16[32,16,128]{2,1,0:T(8,128)(2,1)S(1)} %bitcast.22), channel_id=1, source_target_pairs={{0,2},{2,0},{4,6},{6,4},{8,10},{10,8},{12,14},{14,12},{16,18},{18,... | collective-permute-start | bytes 393224 | tf_op jit(solution)/shard_map/ppermute | solution.py:293
  19.4 1.9 %collective-permute-start.13 = (bf16[32,16,128]{2,1,0:T(8,128)(2,1)S(1)}, bf16[32,16,128]{2,1,0:T(8,128)(2,1)S(1)}, u32[]{:S(2)}, u32[]{:S(2)}) collective-permute-start(bf16[32,16,128]{2,1,0:T(8,128)(2,1)S(1)} %bitcast.15), channel_id=1, source_target_pairs={{0,2},{2,0},{4,6},{6,4},{8,10},{10,8},{12,14},{14,12},{16,18},{18,... | collective-permute-start | bytes 393224 | tf_op jit(solution)/shard_map/ppermute | solution.py:293

commit v11 on v10

--- a/solution.py
+++ b/solution.py
@@ -301,8 +301,8 @@
     partial = call(
         functools.partial(own_parity, blocks=far, **dims),
         shape((depth * pairs, 3 * filters, 2 * across), f32),
-        [vmem] * (1 + far),
-        [w_mine, mine[-1]] + mine[:-1],
+        [vmem] * (1 + far) + [anywhere] * (far - 2),
+        [w_mine, mine[-1]] + mine[:-1] + behind[2:],
         cost=28,
     )
     planes = call(

time: 22.8 us -> 23 us (level)
  waiting for transfers between devices: 1.43 us -> 1.68 us
    ppermute x9, waiting for transfers between devices: 0.57 us -> 1.58 us  [shifted(): return lax.ppermute(x, ('filt', 'space'), pairs)]
    ppermute x5, waiting for transfers between devices: 0.85 us -> 0.11 us  [swapped(): return lax.ppermute(x, 'filt', [(i, i ^ 1) for i in range(size)])]
where the time goes in v11:
time: 23 us; the launch traced here: 22.7 us
  starting transfers between devices  15.5 us (67%)
  Pallas kernels  5.5 us (24%)
  waiting for transfers between devices  1.68 us (7%)
    ppermute x9, starting transfers between devices, shifted(): return lax.ppermute(x, ('filt', 'space'), pairs)  14.4 us
    pallas_call x9, Pallas kernels, call(): pl.pallas_call(body, out_shape=outs, in_specs=ins, out_specs=jax.tree.map...  5.5 us
    ppermute x9, waiting for transfers between devices, shifted(): return lax.ppermute(x, ('filt', 'space'), pairs)  1.58 us
    ppermute x5, starting transfers between devices, swapped(): return lax.ppermute(x, 'filt', [(i, i ^ 1) for i in range(size)])  1.08 us
  transfers between devices with their start and end apart: 14, of which 4 were waited for; matrix products, arithmetic and copies ran while one was open for 0% of the time, Pallas kernels for 19%

profile of v11, /device:TPU:0, one launch (start us, length us, event | category | flops | bytes accessed | tf_op | source)
XLA Modules:
  0.0 22.7 jit_solution(7102856895309750873)
XLA Ops:
  0.0 4.0 %collective-permute-start = (bf16[16,4,4,128]{3,2,1,0:T(4,128)(2,1)}, bf16[16,4,4,128]{3,2,1,0:T(4,128)(2,1)S(1)}, u32[]{:S(2)}, u32[]{:S(2)}) collective-permute-start(bf16[16,4,4,128]{3,2,1,0:T(4,128)(2,1)} %param.3), channel_id=1, source_target_pairs={{0,16},{1,17},{2,18},{3,19},{4,20},{5,21},{6,22},{7,23},{8,24},{9,... | collective-permute-start | bytes 196616 | tf_op jit(solution)/shard_map/ppermute | solution.py:213
  4.0 1.0 %shard_map.37 = (bf16[256,128]{1,0:T(8,128)(2,1)S(1)}, bf16[64,128]{1,0:T(8,128)(2,1)S(1)}, bf16[1,32]{1,0:T(2,128)(2,1)S(1)}) custom-call(bf16[256,128]{1,0:T(8,128)(2,1)} %bitcast.24, bf16[1,32]{1,0:T(2,128)(2,1)} %bitcast.25), custom_call_target="tpu_custom_call" | custom-call | flops 4096 | bytes 256 | tf_op jit(solution)/shard_map/pallas_call | solution.py:234
  5.1 1.6 %collective-permute-start.4 = (bf16[64,128]{1,0:T(8,128)(2,1)S(1)}, bf16[64,128]{1,0:T(8,128)(2,1)S(1)}, u32[]{:S(2)}, u32[]{:S(2)}) collective-permute-start(bf16[64,128]{1,0:T(8,128)(2,1)S(1)} %get-tuple-element.16), channel_id=1, source_target_pairs={{0,1},{1,0},{2,3},{3,2},{4,5},{5,4},{6,7},{7,6},{8,9},{9,8},{10,11... | collective-permute-start | bytes 49160 | tf_op jit(solution)/shard_map/ppermute | solution.py:213
  6.6 0.0 collective-permute-start.5
  6.6 1.3 %shard_map.38 = (bf16[9,96,128]{2,1,0:T(8,128)(2,1)S(1)}, bf16[9,96,128]{2,1,0:T(8,128)(2,1)S(1)}, f32[32,128]{1,0:T(8,128)S(1)}) custom-call(bf16[864,256]{1,0:T(8,128)(2,1)} %bitcast.26, bf16[1,32]{1,0:T(2,128)(2,1)S(1)} %get-tuple-element.11.bias_ref), custom_call_target="tpu_custom_call" | custom-call | flops 2147483648 | bytes 256 | tf_op jit(solution)/shard_map/pallas_call | solution.py:234
  8.0 0.0 collective-permute-done
  8.0 0.2 shard_map.39.refs_0_
  8.2 2.9 %collective-permute-start.1 = (bf16[512,128]{1,0:T(8,128)(2,1)S(1)}, bf16[512,128]{1,0:T(8,128)(2,1)S(1)}, u32[]{:S(2)}, u32[]{:S(2)}) collective-permute-start(bf16[512,128]{1,0:T(8,128)(2,1)S(1)} %shard_map.39.refs_0_), channel_id=1, source_target_pairs={{0,12},{1,13},{2,14},{3,15},{4,8},{5,9},{6,10},{7,11},{8,4},{9,5},... | collective-permute-start | bytes 393224 | tf_op jit(solution)/shard_map/ppermute | solution.py:213
  11.1 0.5 %collective-permute-start.2 = (bf16[512,128]{1,0:T(8,128)(2,1)S(1)}, bf16[512,128]{1,0:T(8,128)(2,1)S(1)}, u32[]{:S(2)}, u32[]{:S(2)}) collective-permute-start(bf16[512,128]{1,0:T(8,128)(2,1)S(1)} %shard_map.39.refs_0_), channel_id=1, source_target_pairs={{0,4},{1,5},{2,6},{3,7},{4,0},{5,1},{6,2},{7,3},{8,12},{9,13},{10,... | collective-permute-start | bytes 393224 | tf_op jit(solution)/shard_map/ppermute | solution.py:213
  11.6 0.2 collective-permute-start.3
  11.7 0.4 %collective-permute-done.5.refs_2_ = bf16[64,128]{1,0:T(8,128)(2,1)S(1)} collective-permute-done((bf16[64,128]{1,0:T(8,128)(2,1)S(1)}, bf16[64,128]{1,0:T(8,128)(2,1)S(1)}, u32[]{:S(2)}, u32[]{:S(2)}) %collective-permute-start.5) | collective-permute-done | bytes 16416 | tf_op jit(solution)/shard_map/ppermute | solution.py:213
  12.2 1.6 %collective-permute-start.6 = (bf16[128,128]{1,0:T(8,128)(2,1)S(1)}, bf16[128,128]{1,0:T(8,128)(2,1)S(1)}, u32[]{:S(2)}, u32[]{:S(2)}) collective-permute-start(bf16[128,128]{1,0:T(8,128)(2,1)S(1)} %shard_map.40.refs_1_), channel_id=1, source_target_pairs={{0,8},{1,9},{2,10},{3,11},{4,12},{5,13},{6,14},{7,15},{8,0},{9,1},... | collective-permute-start | bytes 98312 | tf_op jit(solution)/shard_map/ppermute | solution.py:213
  13.8 1.5 %collective-permute-start.7 = (bf16[128,128]{1,0:T(8,128)(2,1)S(1)}, bf16[128,128]{1,0:T(8,128)(2,1)S(1)}, u32[]{:S(2)}, u32[]{:S(2)}) collective-permute-start(bf16[128,128]{1,0:T(8,128)(2,1)S(1)} %shard_map.40.refs_1_), channel_id=1, source_target_pairs={{0,12},{1,13},{2,14},{3,15},{4,8},{5,9},{6,10},{7,11},{8,4},{9,5},... | collective-permute-start | bytes 98312 | tf_op jit(solution)/shard_map/ppermute | solution.py:213
  15.3 2.2 %collective-permute-start.12 = (bf16[128,128]{1,0:T(8,128)(2,1)S(1)}, bf16[128,128]{1,0:T(8,128)(2,1)S(1)}, u32[]{:S(2)}, u32[]{:S(2)}) collective-permute-start(bf16[128,128]{1,0:T(8,128)(2,1)S(1)} %shard_map.43), channel_id=1, source_target_pairs={{0,4},{1,5},{2,6},{3,7},{4,0},{5,1},{6,2},{7,3},{8,12},{9,13},{10,... | collective-permute-start | bytes 98312 | tf_op jit(solution)/shard_map/ppermute | solution.py:213
  17.4 0.5 %collective-permute-done.6.refs_4_.refs_3_ = bf16[128,128]{1,0:T(8,128)(2,1)S(1)} collective-permute-done((bf16[128,128]{1,0:T(8,128)(2,1)S(1)}, bf16[128,128]{1,0:T(8,128)(2,1)S(1)}, u32[]{:S(2)}, u32[]{:S(2)}) %collective-permute-start.6) | collective-permute-done | bytes 32800 | tf_op jit(solution)/shard_map/ppermute | solution.py:213
  17.9 0.6 %collective-permute-done.7.refs_5_.refs_4_ = bf16[128,128]{1,0:T(8,128)(2,1)S(1)} collective-permute-done((bf16[128,128]{1,0:T(8,128)(2,1)S(1)}, bf16[128,128]{1,0:T(8,128)(2,1)S(1)}, u32[]{:S(2)}, u32[]{:S(2)}) %collective-permute-start.7) | collective-permute-done | bytes 32800 | tf_op jit(solution)/shard_map/ppermute | solution.py:213
  18.6 0.5 %collective-permute-start.9 = (bf16[32,16,128]{2,1,0:T(8,128)(2,1)S(1)}, bf16[32,16,128]{2,1,0:T(8,128)(2,1)S(1)}, u32[]{:S(2)}, u32[]{:S(2)}) collective-permute-start(bf16[32,16,128]{2,1,0:T(8,128)(2,1)S(1)} %bitcast.19), channel_id=1, source_target_pairs={{0,2},{2,0},{4,6},{6,4},{8,10},{10,8},{12,14},{14,12},{16,18},{18,... | collective-permute-start | bytes 393224 | tf_op jit(solution)/shard_map/ppermute | solution.py:293
  19.1 0.1 collective-permute-start.10
  19.2 0.8 %shard_map.41.sum_ref.refs_0_ = f32[8,96,256]{2,1,0:T(8,128)S(1)} custom-call(bf16[9,96,128]{2,1,0:T(8,128)(2,1)S(1)} %get-tuple-element.12._.w_ref.w_mine_ref, bf16[32,16,128]{2,1,0:T(8,128)(2,1)S(1)} %bitcast.14, bf16[32,16,128]{2,1,0:T(8,128)(2,1)S(1)} %bitcast.18, bf16[32,16,128]{2,1,0:T(8,128)(2,1)S(1)} %bitcast.20, bf16[32,16,128]{2,1,0:T(8,128)(2,1)S(1)} %bitcast.22, ...), custom_call_target="tpu_custom_call" | custom-call | flops 268435456 | bytes 256 | tf_op jit(solution)/shard_map/pallas_call | solution.py:234
  19.9 0.0 collective-permute-done.12.refs_2_
  20.0 0.5 %collective-permute-start.13 = (bf16[32,16,128]{2,1,0:T(8,128)(2,1)S(1)}, bf16[32,16,128]{2,1,0:T(8,128)(2,1)S(1)}, u32[]{:S(2)}, u32[]{:S(2)}) collective-permute-start(bf16[32,16,128]{2,1,0:T(8,128)(2,1)S(1)} %bitcast.15), channel_id=1, source_target_pairs={{0,2},{2,0},{4,6},{6,4},{8,10},{10,8},{12,14},{14,12},{16,18},{18,... | collective-permute-start | bytes 393224 | tf_op jit(solution)/shard_map/ppermute | solution.py:293
  20.5 0.9 %shard_map.42.v_ref = f32[16,32,128]{2,1,0:T(8,128)S(1)} custom-call(bf16[9,96,128]{2,1,0:T(8,128)(2,1)S(1)} %get-tuple-element.13.w_ref.w_theirs_ref, f32[32,128]{1,0:T(8,128)S(1)} %get-tuple-element.14.bias_ref, f32[8,96,256]{2,1,0:T(8,128)S(1)} %shard_map.41.sum_ref.refs_0_, bf16[32,16,128]{2,1,0:T(8,128)(2,1)S(1)} %collective-permute-done.8.refs_0_, ...), custom_call_target="tpu_custom_call" | custom-call | flops 4096 | bytes 256 | tf_op jit(solution)/shard_map/pallas_call | solution.py:234
  21.4 0.1 collective-permute-done.13.refs_1_
  21.4 1.3 %shard_map.45 = bf16[128,64]{1,0:T(8,128)(2,1)} custom-call(bf16[9,96,128]{2,1,0:T(8,128)(2,1)S(1)} %get-tuple-element.12._.w_ref.w_mine_ref, bf16[9,96,128]{2,1,0:T(8,128)(2,1)S(1)} %get-tuple-element.13.w_ref.w_theirs_ref, f32[16,32,128]{2,1,0:T(8,128)S(1)} %shard_map.42.v_ref, bf16[32,16,128]{2,1,0:T(8,128)(2,1)S(1)} %bitcast.16, ...), custom_call_target="tpu_custom_call" | custom-call | flops 4096 | bytes 256 | tf_op jit(solution)/shard_map/pallas_call | solution.py:234
  (13 shorter events, 0.0 us)
Async XLA Ops:
  0.0 8.0 %collective-permute-start = (bf16[16,4,4,128]{3,2,1,0:T(4,128)(2,1)}, bf16[16,4,4,128]{3,2,1,0:T(4,128)(2,1)S(1)}, u32[]{:S(2)}, u32[]{:S(2)}) collective-permute-start(bf16[16,4,4,128]{3,2,1,0:T(4,128)(2,1)} %param.3), channel_id=1, source_target_pairs={{0,16},{1,17},{2,18},{3,19},{4,20},{5,21},{6,22},{7,23},{8,24},{9,... | collective-permute-start | bytes 196616 | tf_op jit(solution)/shard_map/ppermute | solution.py:213
  5.1 6.7 %collective-permute-start.4 = (bf16[64,128]{1,0:T(8,128)(2,1)S(1)}, bf16[64,128]{1,0:T(8,128)(2,1)S(1)}, u32[]{:S(2)}, u32[]{:S(2)}) collective-permute-start(bf16[64,128]{1,0:T(8,128)(2,1)S(1)} %get-tuple-element.16), channel_id=1, source_target_pairs={{0,1},{1,0},{2,3},{3,2},{4,5},{5,4},{6,7},{7,6},{8,9},{9,8},{10,11... | collective-permute-start | bytes 49160 | tf_op jit(solution)/shard_map/ppermute | solution.py:213
  6.6 5.5 %collective-permute-start.5 = (bf16[64,128]{1,0:T(8,128)(2,1)S(1)}, bf16[64,128]{1,0:T(8,128)(2,1)S(1)}, u32[]{:S(2)}, u32[]{:S(2)}) collective-permute-start(bf16[64,128]{1,0:T(8,128)(2,1)S(1)} %get-tuple-element.16), channel_id=1, source_target_pairs={{0,17},{1,16},{2,19},{3,18},{4,21},{5,20},{6,23},{7,22},{8,25},{9,... | collective-permute-start | bytes 49160 | tf_op jit(solution)/shard_map/ppermute | solution.py:213
  8.2 7.1 %collective-permute-start.1 = (bf16[512,128]{1,0:T(8,128)(2,1)S(1)}, bf16[512,128]{1,0:T(8,128)(2,1)S(1)}, u32[]{:S(2)}, u32[]{:S(2)}) collective-permute-start(bf16[512,128]{1,0:T(8,128)(2,1)S(1)} %shard_map.39.refs_0_), channel_id=1, source_target_pairs={{0,12},{1,13},{2,14},{3,15},{4,8},{5,9},{6,10},{7,11},{8,4},{9,5},... | collective-permute-start | bytes 393224 | tf_op jit(solution)/shard_map/ppermute | solution.py:213
  11.1 7.5 %collective-permute-start.2 = (bf16[512,128]{1,0:T(8,128)(2,1)S(1)}, bf16[512,128]{1,0:T(8,128)(2,1)S(1)}, u32[]{:S(2)}, u32[]{:S(2)}) collective-permute-start(bf16[512,128]{1,0:T(8,128)(2,1)S(1)} %shard_map.39.refs_0_), channel_id=1, source_target_pairs={{0,4},{1,5},{2,6},{3,7},{4,0},{5,1},{6,2},{7,3},{8,12},{9,13},{10,... | collective-permute-start | bytes 393224 | tf_op jit(solution)/shard_map/ppermute | solution.py:213
  11.6 7.5 %collective-permute-start.3 = (bf16[512,128]{1,0:T(8,128)(2,1)S(1)}, bf16[512,128]{1,0:T(8,128)(2,1)S(1)}, u32[]{:S(2)}, u32[]{:S(2)}) collective-permute-start(bf16[512,128]{1,0:T(8,128)(2,1)S(1)} %shard_map.39.refs_0_), channel_id=1, source_target_pairs={{0,8},{1,9},{2,10},{3,11},{4,12},{5,13},{6,14},{7,15},{8,0},{9,1},... | collective-permute-start | bytes 393224 | tf_op jit(solution)/shard_map/ppermute | solution.py:213
  12.2 5.7 %collective-permute-start.6 = (bf16[128,128]{1,0:T(8,128)(2,1)S(1)}, bf16[128,128]{1,0:T(8,128)(2,1)S(1)}, u32[]{:S(2)}, u32[]{:S(2)}) collective-permute-start(bf16[128,128]{1,0:T(8,128)(2,1)S(1)} %shard_map.40.refs_1_), channel_id=1, source_target_pairs={{0,8},{1,9},{2,10},{3,11},{4,12},{5,13},{6,14},{7,15},{8,0},{9,1},... | collective-permute-start | bytes 98312 | tf_op jit(solution)/shard_map/ppermute | solution.py:213
  13.8 4.8 %collective-permute-start.7 = (bf16[128,128]{1,0:T(8,128)(2,1)S(1)}, bf16[128,128]{1,0:T(8,128)(2,1)S(1)}, u32[]{:S(2)}, u32[]{:S(2)}) collective-permute-start(bf16[128,128]{1,0:T(8,128)(2,1)S(1)} %shard_map.40.refs_1_), channel_id=1, source_target_pairs={{0,12},{1,13},{2,14},{3,15},{4,8},{5,9},{6,10},{7,11},{8,4},{9,5},... | collective-permute-start | bytes 98312 | tf_op jit(solution)/shard_map/ppermute | solution.py:213
  15.3 4.7 %collective-permute-start.12 = (bf16[128,128]{1,0:T(8,128)(2,1)S(1)}, bf16[128,128]{1,0:T(8,128)(2,1)S(1)}, u32[]{:S(2)}, u32[]{:S(2)}) collective-permute-start(bf16[128,128]{1,0:T(8,128)(2,1)S(1)} %shard_map.43), channel_id=1, source_target_pairs={{0,4},{1,5},{2,6},{3,7},{4,0},{5,1},{6,2},{7,3},{8,12},{9,13},{10,... | collective-permute-start | bytes 98312 | tf_op jit(solution)/shard_map/ppermute | solution.py:213
  17.9 2.6 %collective-permute-start.8 = (bf16[32,16,128]{2,1,0:T(8,128)(2,1)S(1)}, bf16[32,16,128]{2,1,0:T(8,128)(2,1)S(1)}, u32[]{:S(2)}, u32[]{:S(2)}) collective-permute-start(bf16[32,16,128]{2,1,0:T(8,128)(2,1)S(1)} %bitcast.17), channel_id=1, source_target_pairs={{0,2},{2,0},{4,6},{6,4},{8,10},{10,8},{12,14},{14,12},{16,18},{18,... | collective-permute-start | bytes 393224 | tf_op jit(solution)/shard_map/ppermute | solution.py:293
  18.6 1.9 %collective-permute-start.11 = (bf16[32,16,128]{2,1,0:T(8,128)(2,1)S(1)}, bf16[32,16,128]{2,1,0:T(8,128)(2,1)S(1)}, u32[]{:S(2)}, u32[]{:S(2)}) collective-permute-start(bf16[32,16,128]{2,1,0:T(8,128)(2,1)S(1)} %bitcast.13), channel_id=1, source_target_pairs={{0,2},{2,0},{4,6},{6,4},{8,10},{10,8},{12,14},{14,12},{16,18},{18,... | collective-permute-start | bytes 393224 | tf_op jit(solution)/shard_map/ppermute | solution.py:293
  18.6 1.9 %collective-permute-start.9 = (bf16[32,16,128]{2,1,0:T(8,128)(2,1)S(1)}, bf16[32,16,128]{2,1,0:T(8,128)(2,1)S(1)}, u32[]{:S(2)}, u32[]{:S(2)}) collective-permute-start(bf16[32,16,128]{2,1,0:T(8,128)(2,1)S(1)} %bitcast.19), channel_id=1, source_target_pairs={{0,2},{2,0},{4,6},{6,4},{8,10},{10,8},{12,14},{14,12},{16,18},{18,... | collective-permute-start | bytes 393224 | tf_op jit(solution)/shard_map/ppermute | solution.py:293
  19.1 1.4 %collective-permute-start.10 = (bf16[32,16,128]{2,1,0:T(8,128)(2,1)S(1)}, bf16[32,16,128]{2,1,0:T(8,128)(2,1)S(1)}, u32[]{:S(2)}, u32[]{:S(2)}) collective-permute-start(bf16[32,16,128]{2,1,0:T(8,128)(2,1)S(1)} %bitcast.21), channel_id=1, source_target_pairs={{0,2},{2,0},{4,6},{6,4},{8,10},{10,8},{12,14},{14,12},{16,18},{18,... | collective-permute-start | bytes 393224 | tf_op jit(solution)/shard_map/ppermute | solution.py:293
  20.0 1.5 %collective-permute-start.13 = (bf16[32,16,128]{2,1,0:T(8,128)(2,1)S(1)}, bf16[32,16,128]{2,1,0:T(8,128)(2,1)S(1)}, u32[]{:S(2)}, u32[]{:S(2)}) collective-permute-start(bf16[32,16,128]{2,1,0:T(8,128)(2,1)S(1)} %bitcast.15), channel_id=1, source_target_pairs={{0,2},{2,0},{4,6},{6,4},{8,10},{10,8},{12,14},{14,12},{16,18},{18,... | collective-permute-start | bytes 393224 | tf_op jit(solution)/shard_map/ppermute | solution.py:293

commit v12 on v11

--- a/solution.py
+++ b/solution.py
@@ -302,7 +302,7 @@
         functools.partial(own_parity, blocks=far, **dims),
         shape((depth * pairs, 3 * filters, 2 * across), f32),
         [vmem] * (1 + far) + [anywhere] * (far - 2),
-        [w_mine, mine[-1]] + mine[:-1] + behind[2:],
+        [w_mine, mine[-1]] + mine[:-1] + behind[:1:-1],
         cost=28,
     )
     planes = call(

time: 23 us -> 23 us (level)
  transfers between devices with their start and end apart: 14 -> 14, of which waited for: 4 -> 4; matrix products, arithmetic and copies ran while one was open for 0% -> 0% of each run, Pallas kernels for 19% -> 18%
where the time goes in v12:
time: 23 us; the launch traced here: 22.8 us
  starting transfers between devices  15.5 us (67%)
  Pallas kernels  5.5 us (24%)
  waiting for transfers between devices  1.78 us (8%)
    ppermute x9, starting transfers between devices, shifted(): return lax.ppermute(x, ('filt', 'space'), pairs)  14.4 us
    pallas_call x9, Pallas kernels, call(): pl.pallas_call(body, out_shape=outs, in_specs=ins, out_specs=jax.tree.map...  5.5 us
    ppermute x9, waiting for transfers between devices, shifted(): return lax.ppermute(x, ('filt', 'space'), pairs)  1.68 us
    ppermute x5, starting transfers between devices, swapped(): return lax.ppermute(x, 'filt', [(i, i ^ 1) for i in range(size)])  1.09 us
  transfers between devices with their start and end apart: 14, of which 4 were waited for; matrix products, arithmetic and copies ran while one was open for 0% of the time, Pallas kernels for 18%

profile of v12, /device:TPU:0, one launch (start us, length us, event | category | flops | bytes accessed | tf_op | source)
XLA Modules:
  0.0 22.8 jit_solution(14833259772560311264)
XLA Ops:
  0.0 4.0 %collective-permute-start = (bf16[16,4,4,128]{3,2,1,0:T(4,128)(2,1)}, bf16[16,4,4,128]{3,2,1,0:T(4,128)(2,1)S(1)}, u32[]{:S(2)}, u32[]{:S(2)}) collective-permute-start(bf16[16,4,4,128]{3,2,1,0:T(4,128)(2,1)} %param.3), channel_id=1, source_target_pairs={{0,16},{1,17},{2,18},{3,19},{4,20},{5,21},{6,22},{7,23},{8,24},{9,... | collective-permute-start | bytes 196616 | tf_op jit(solution)/shard_map/ppermute | solution.py:213
  4.0 1.0 %shard_map.37 = (bf16[256,128]{1,0:T(8,128)(2,1)S(1)}, bf16[64,128]{1,0:T(8,128)(2,1)S(1)}, bf16[1,32]{1,0:T(2,128)(2,1)S(1)}) custom-call(bf16[256,128]{1,0:T(8,128)(2,1)} %bitcast.24, bf16[1,32]{1,0:T(2,128)(2,1)} %bitcast.25), custom_call_target="tpu_custom_call" | custom-call | flops 4096 | bytes 256 | tf_op jit(solution)/shard_map/pallas_call | solution.py:234
  5.1 1.6 %collective-permute-start.4 = (bf16[64,128]{1,0:T(8,128)(2,1)S(1)}, bf16[64,128]{1,0:T(8,128)(2,1)S(1)}, u32[]{:S(2)}, u32[]{:S(2)}) collective-permute-start(bf16[64,128]{1,0:T(8,128)(2,1)S(1)} %get-tuple-element.16), channel_id=1, source_target_pairs={{0,1},{1,0},{2,3},{3,2},{4,5},{5,4},{6,7},{7,6},{8,9},{9,8},{10,11... | collective-permute-start | bytes 49160 | tf_op jit(solution)/shard_map/ppermute | solution.py:213
  6.6 0.0 collective-permute-start.5
  6.6 1.3 %shard_map.38 = (bf16[9,96,128]{2,1,0:T(8,128)(2,1)S(1)}, bf16[9,96,128]{2,1,0:T(8,128)(2,1)S(1)}, f32[32,128]{1,0:T(8,128)S(1)}) custom-call(bf16[864,256]{1,0:T(8,128)(2,1)} %bitcast.26, bf16[1,32]{1,0:T(2,128)(2,1)S(1)} %get-tuple-element.11.bias_ref), custom_call_target="tpu_custom_call" | custom-call | flops 2147483648 | bytes 256 | tf_op jit(solution)/shard_map/pallas_call | solution.py:234
  8.0 0.2 shard_map.39.refs_0_
  8.2 2.9 %collective-permute-start.1 = (bf16[512,128]{1,0:T(8,128)(2,1)S(1)}, bf16[512,128]{1,0:T(8,128)(2,1)S(1)}, u32[]{:S(2)}, u32[]{:S(2)}) collective-permute-start(bf16[512,128]{1,0:T(8,128)(2,1)S(1)} %shard_map.39.refs_0_), channel_id=1, source_target_pairs={{0,12},{1,13},{2,14},{3,15},{4,8},{5,9},{6,10},{7,11},{8,4},{9,5},... | collective-permute-start | bytes 393224 | tf_op jit(solution)/shard_map/ppermute | solution.py:213
  11.1 0.5 %collective-permute-start.2 = (bf16[512,128]{1,0:T(8,128)(2,1)S(1)}, bf16[512,128]{1,0:T(8,128)(2,1)S(1)}, u32[]{:S(2)}, u32[]{:S(2)}) collective-permute-start(bf16[512,128]{1,0:T(8,128)(2,1)S(1)} %shard_map.39.refs_0_), channel_id=1, source_target_pairs={{0,4},{1,5},{2,6},{3,7},{4,0},{5,1},{6,2},{7,3},{8,12},{9,13},{10,... | collective-permute-start | bytes 393224 | tf_op jit(solution)/shard_map/ppermute | solution.py:213
  11.6 0.2 collective-permute-start.3
  11.7 0.0 collective-permute-done.4.refs_1_
  11.7 0.4 %collective-permute-done.5.refs_2_ = bf16[64,128]{1,0:T(8,128)(2,1)S(1)} collective-permute-done((bf16[64,128]{1,0:T(8,128)(2,1)S(1)}, bf16[64,128]{1,0:T(8,128)(2,1)S(1)}, u32[]{:S(2)}, u32[]{:S(2)}) %collective-permute-start.5) | collective-permute-done | bytes 16416 | tf_op jit(solution)/shard_map/ppermute | solution.py:213
  12.2 2.5 %collective-permute-start.6 = (bf16[128,128]{1,0:T(8,128)(2,1)S(1)}, bf16[128,128]{1,0:T(8,128)(2,1)S(1)}, u32[]{:S(2)}, u32[]{:S(2)}) collective-permute-start(bf16[128,128]{1,0:T(8,128)(2,1)S(1)} %shard_map.40.refs_1_), channel_id=1, source_target_pairs={{0,12},{1,13},{2,14},{3,15},{4,8},{5,9},{6,10},{7,11},{8,4},{9,5},... | collective-permute-start | bytes 98312 | tf_op jit(solution)/shard_map/ppermute | solution.py:213
  14.7 0.5 %collective-permute-start.7 = (bf16[128,128]{1,0:T(8,128)(2,1)S(1)}, bf16[128,128]{1,0:T(8,128)(2,1)S(1)}, u32[]{:S(2)}, u32[]{:S(2)}) collective-permute-start(bf16[128,128]{1,0:T(8,128)(2,1)S(1)} %shard_map.40.refs_1_), channel_id=1, source_target_pairs={{0,8},{1,9},{2,10},{3,11},{4,12},{5,13},{6,14},{7,15},{8,0},{9,1},... | collective-permute-start | bytes 98312 | tf_op jit(solution)/shard_map/ppermute | solution.py:213
  15.3 0.0 collective-permute-done.1
  15.3 2.1 %collective-permute-start.12 = (bf16[128,128]{1,0:T(8,128)(2,1)S(1)}, bf16[128,128]{1,0:T(8,128)(2,1)S(1)}, u32[]{:S(2)}, u32[]{:S(2)}) collective-permute-start(bf16[128,128]{1,0:T(8,128)(2,1)S(1)} %shard_map.43), channel_id=1, source_target_pairs={{0,4},{1,5},{2,6},{3,7},{4,0},{5,1},{6,2},{7,3},{8,12},{9,13},{10,... | collective-permute-start | bytes 98312 | tf_op jit(solution)/shard_map/ppermute | solution.py:213
  17.4 0.6 %collective-permute-done.6.refs_4_ = bf16[128,128]{1,0:T(8,128)(2,1)S(1)} collective-permute-done((bf16[128,128]{1,0:T(8,128)(2,1)S(1)}, bf16[128,128]{1,0:T(8,128)(2,1)S(1)}, u32[]{:S(2)}, u32[]{:S(2)}) %collective-permute-start.6) | collective-permute-done | bytes 32800 | tf_op jit(solution)/shard_map/ppermute | solution.py:213
  18.0 0.7 %collective-permute-done.7.refs_5_.refs_3_ = bf16[128,128]{1,0:T(8,128)(2,1)S(1)} collective-permute-done((bf16[128,128]{1,0:T(8,128)(2,1)S(1)}, bf16[128,128]{1,0:T(8,128)(2,1)S(1)}, u32[]{:S(2)}, u32[]{:S(2)}) %collective-permute-start.7) | collective-permute-done | bytes 32800 | tf_op jit(solution)/shard_map/ppermute | solution.py:213
  18.6 0.5 %collective-permute-start.9 = (bf16[32,16,128]{2,1,0:T(8,128)(2,1)S(1)}, bf16[32,16,128]{2,1,0:T(8,128)(2,1)S(1)}, u32[]{:S(2)}, u32[]{:S(2)}) collective-permute-start(bf16[32,16,128]{2,1,0:T(8,128)(2,1)S(1)} %bitcast.19), channel_id=1, source_target_pairs={{0,2},{2,0},{4,6},{6,4},{8,10},{10,8},{12,14},{14,12},{16,18},{18,... | collective-permute-start | bytes 393224 | tf_op jit(solution)/shard_map/ppermute | solution.py:293
  19.2 0.1 collective-permute-start.10
  19.2 0.8 %shard_map.41.sum_ref.refs_0_ = f32[8,96,256]{2,1,0:T(8,128)S(1)} custom-call(bf16[9,96,128]{2,1,0:T(8,128)(2,1)S(1)} %get-tuple-element.12._.w_ref.w_mine_ref, bf16[32,16,128]{2,1,0:T(8,128)(2,1)S(1)} %bitcast.14, bf16[32,16,128]{2,1,0:T(8,128)(2,1)S(1)} %bitcast.18, bf16[32,16,128]{2,1,0:T(8,128)(2,1)S(1)} %bitcast.20, bf16[32,16,128]{2,1,0:T(8,128)(2,1)S(1)} %bitcast.22, ...), custom_call_target="tpu_custom_call" | custom-call | flops 268435456 | bytes 256 | tf_op jit(solution)/shard_map/pallas_call | solution.py:234
  20.0 0.5 %collective-permute-start.13 = (bf16[32,16,128]{2,1,0:T(8,128)(2,1)S(1)}, bf16[32,16,128]{2,1,0:T(8,128)(2,1)S(1)}, u32[]{:S(2)}, u32[]{:S(2)}) collective-permute-start(bf16[32,16,128]{2,1,0:T(8,128)(2,1)S(1)} %bitcast.15), channel_id=1, source_target_pairs={{0,2},{2,0},{4,6},{6,4},{8,10},{10,8},{12,14},{14,12},{16,18},{18,... | collective-permute-start | bytes 393224 | tf_op jit(solution)/shard_map/ppermute | solution.py:293
  20.6 0.9 %shard_map.42.v_ref = f32[16,32,128]{2,1,0:T(8,128)S(1)} custom-call(bf16[9,96,128]{2,1,0:T(8,128)(2,1)S(1)} %get-tuple-element.13.w_ref.w_theirs_ref, f32[32,128]{1,0:T(8,128)S(1)} %get-tuple-element.14.bias_ref, f32[8,96,256]{2,1,0:T(8,128)S(1)} %shard_map.41.sum_ref.refs_0_, bf16[32,16,128]{2,1,0:T(8,128)(2,1)S(1)} %collective-permute-done.8.refs_0_, ...), custom_call_target="tpu_custom_call" | custom-call | flops 4096 | bytes 256 | tf_op jit(solution)/shard_map/pallas_call | solution.py:234
  21.4 0.1 collective-permute-done.13.refs_1_
  21.5 1.3 %shard_map.45 = bf16[128,64]{1,0:T(8,128)(2,1)} custom-call(bf16[9,96,128]{2,1,0:T(8,128)(2,1)S(1)} %get-tuple-element.12._.w_ref.w_mine_ref, bf16[9,96,128]{2,1,0:T(8,128)(2,1)S(1)} %get-tuple-element.13.w_ref.w_theirs_ref, f32[16,32,128]{2,1,0:T(8,128)S(1)} %shard_map.42.v_ref, bf16[32,16,128]{2,1,0:T(8,128)(2,1)S(1)} %bitcast.16, ...), custom_call_target="tpu_custom_call" | custom-call | flops 4096 | bytes 256 | tf_op jit(solution)/shard_map/pallas_call | solution.py:234
  (13 shorter events, 0.0 us)
Async XLA Ops:
  0.0 8.0 %collective-permute-start = (bf16[16,4,4,128]{3,2,1,0:T(4,128)(2,1)}, bf16[16,4,4,128]{3,2,1,0:T(4,128)(2,1)S(1)}, u32[]{:S(2)}, u32[]{:S(2)}) collective-permute-start(bf16[16,4,4,128]{3,2,1,0:T(4,128)(2,1)} %param.3), channel_id=1, source_target_pairs={{0,16},{1,17},{2,18},{3,19},{4,20},{5,21},{6,22},{7,23},{8,24},{9,... | collective-permute-start | bytes 196616 | tf_op jit(solution)/shard_map/ppermute | solution.py:213
  5.1 6.7 %collective-permute-start.4 = (bf16[64,128]{1,0:T(8,128)(2,1)S(1)}, bf16[64,128]{1,0:T(8,128)(2,1)S(1)}, u32[]{:S(2)}, u32[]{:S(2)}) collective-permute-start(bf16[64,128]{1,0:T(8,128)(2,1)S(1)} %get-tuple-element.16), channel_id=1, source_target_pairs={{0,1},{1,0},{2,3},{3,2},{4,5},{5,4},{6,7},{7,6},{8,9},{9,8},{10,11... | collective-permute-start | bytes 49160 | tf_op jit(solution)/shard_map/ppermute | solution.py:213
  6.6 5.5 %collective-permute-start.5 = (bf16[64,128]{1,0:T(8,128)(2,1)S(1)}, bf16[64,128]{1,0:T(8,128)(2,1)S(1)}, u32[]{:S(2)}, u32[]{:S(2)}) collective-permute-start(bf16[64,128]{1,0:T(8,128)(2,1)S(1)} %get-tuple-element.16), channel_id=1, source_target_pairs={{0,17},{1,16},{2,19},{3,18},{4,21},{5,20},{6,23},{7,22},{8,25},{9,... | collective-permute-start | bytes 49160 | tf_op jit(solution)/shard_map/ppermute | solution.py:213
  8.2 7.1 %collective-permute-start.1 = (bf16[512,128]{1,0:T(8,128)(2,1)S(1)}, bf16[512,128]{1,0:T(8,128)(2,1)S(1)}, u32[]{:S(2)}, u32[]{:S(2)}) collective-permute-start(bf16[512,128]{1,0:T(8,128)(2,1)S(1)} %shard_map.39.refs_0_), channel_id=1, source_target_pairs={{0,12},{1,13},{2,14},{3,15},{4,8},{5,9},{6,10},{7,11},{8,4},{9,5},... | collective-permute-start | bytes 393224 | tf_op jit(solution)/shard_map/ppermute | solution.py:213
  11.1 7.6 %collective-permute-start.2 = (bf16[512,128]{1,0:T(8,128)(2,1)S(1)}, bf16[512,128]{1,0:T(8,128)(2,1)S(1)}, u32[]{:S(2)}, u32[]{:S(2)}) collective-permute-start(bf16[512,128]{1,0:T(8,128)(2,1)S(1)} %shard_map.39.refs_0_), channel_id=1, source_target_pairs={{0,4},{1,5},{2,6},{3,7},{4,0},{5,1},{6,2},{7,3},{8,12},{9,13},{10,... | collective-permute-start | bytes 393224 | tf_op jit(solution)/shard_map/ppermute | solution.py:213
  11.6 7.6 %collective-permute-start.3 = (bf16[512,128]{1,0:T(8,128)(2,1)S(1)}, bf16[512,128]{1,0:T(8,128)(2,1)S(1)}, u32[]{:S(2)}, u32[]{:S(2)}) collective-permute-start(bf16[512,128]{1,0:T(8,128)(2,1)S(1)} %shard_map.39.refs_0_), channel_id=1, source_target_pairs={{0,8},{1,9},{2,10},{3,11},{4,12},{5,13},{6,14},{7,15},{8,0},{9,1},... | collective-permute-start | bytes 393224 | tf_op jit(solution)/shard_map/ppermute | solution.py:213
  12.2 5.8 %collective-permute-start.6 = (bf16[128,128]{1,0:T(8,128)(2,1)S(1)}, bf16[128,128]{1,0:T(8,128)(2,1)S(1)}, u32[]{:S(2)}, u32[]{:S(2)}) collective-permute-start(bf16[128,128]{1,0:T(8,128)(2,1)S(1)} %shard_map.40.refs_1_), channel_id=1, source_target_pairs={{0,12},{1,13},{2,14},{3,15},{4,8},{5,9},{6,10},{7,11},{8,4},{9,5},... | collective-permute-start | bytes 98312 | tf_op jit(solution)/shard_map/ppermute | solution.py:213
  14.7 3.9 %collective-permute-start.7 = (bf16[128,128]{1,0:T(8,128)(2,1)S(1)}, bf16[128,128]{1,0:T(8,128)(2,1)S(1)}, u32[]{:S(2)}, u32[]{:S(2)}) collective-permute-start(bf16[128,128]{1,0:T(8,128)(2,1)S(1)} %shard_map.40.refs_1_), channel_id=1, source_target_pairs={{0,8},{1,9},{2,10},{3,11},{4,12},{5,13},{6,14},{7,15},{8,0},{9,1},... | collective-permute-start | bytes 98312 | tf_op jit(solution)/shard_map/ppermute | solution.py:213
  15.3 4.7 %collective-permute-start.12 = (bf16[128,128]{1,0:T(8,128)(2,1)S(1)}, bf16[128,128]{1,0:T(8,128)(2,1)S(1)}, u32[]{:S(2)}, u32[]{:S(2)}) collective-permute-start(bf16[128,128]{1,0:T(8,128)(2,1)S(1)} %shard_map.43), channel_id=1, source_target_pairs={{0,4},{1,5},{2,6},{3,7},{4,0},{5,1},{6,2},{7,3},{8,12},{9,13},{10,... | collective-permute-start | bytes 98312 | tf_op jit(solution)/shard_map/ppermute | solution.py:213
  18.0 2.6 %collective-permute-start.8 = (bf16[32,16,128]{2,1,0:T(8,128)(2,1)S(1)}, bf16[32,16,128]{2,1,0:T(8,128)(2,1)S(1)}, u32[]{:S(2)}, u32[]{:S(2)}) collective-permute-start(bf16[32,16,128]{2,1,0:T(8,128)(2,1)S(1)} %bitcast.17), channel_id=1, source_target_pairs={{0,2},{2,0},{4,6},{6,4},{8,10},{10,8},{12,14},{14,12},{16,18},{18,... | collective-permute-start | bytes 393224 | tf_op jit(solution)/shard_map/ppermute | solution.py:293
  18.6 1.9 %collective-permute-start.11 = (bf16[32,16,128]{2,1,0:T(8,128)(2,1)S(1)}, bf16[32,16,128]{2,1,0:T(8,128)(2,1)S(1)}, u32[]{:S(2)}, u32[]{:S(2)}) collective-permute-start(bf16[32,16,128]{2,1,0:T(8,128)(2,1)S(1)} %bitcast.13), channel_id=1, source_target_pairs={{0,2},{2,0},{4,6},{6,4},{8,10},{10,8},{12,14},{14,12},{16,18},{18,... | collective-permute-start | bytes 393224 | tf_op jit(solution)/shard_map/ppermute | solution.py:293
  18.6 1.9 %collective-permute-start.9 = (bf16[32,16,128]{2,1,0:T(8,128)(2,1)S(1)}, bf16[32,16,128]{2,1,0:T(8,128)(2,1)S(1)}, u32[]{:S(2)}, u32[]{:S(2)}) collective-permute-start(bf16[32,16,128]{2,1,0:T(8,128)(2,1)S(1)} %bitcast.19), channel_id=1, source_target_pairs={{0,2},{2,0},{4,6},{6,4},{8,10},{10,8},{12,14},{14,12},{16,18},{18,... | collective-permute-start | bytes 393224 | tf_op jit(solution)/shard_map/ppermute | solution.py:293
  19.2 1.4 %collective-permute-start.10 = (bf16[32,16,128]{2,1,0:T(8,128)(2,1)S(1)}, bf16[32,16,128]{2,1,0:T(8,128)(2,1)S(1)}, u32[]{:S(2)}, u32[]{:S(2)}) collective-permute-start(bf16[32,16,128]{2,1,0:T(8,128)(2,1)S(1)} %bitcast.21), channel_id=1, source_target_pairs={{0,2},{2,0},{4,6},{6,4},{8,10},{10,8},{12,14},{14,12},{16,18},{18,... | collective-permute-start | bytes 393224 | tf_op jit(solution)/shard_map/ppermute | solution.py:293
  20.0 1.5 %collective-permute-start.13 = (bf16[32,16,128]{2,1,0:T(8,128)(2,1)S(1)}, bf16[32,16,128]{2,1,0:T(8,128)(2,1)S(1)}, u32[]{:S(2)}, u32[]{:S(2)}) collective-permute-start(bf16[32,16,128]{2,1,0:T(8,128)(2,1)S(1)} %bitcast.15), channel_id=1, source_target_pairs={{0,2},{2,0},{4,6},{6,4},{8,10},{10,8},{12,14},{14,12},{16,18},{18,... | collective-permute-start | bytes 393224 | tf_op jit(solution)/shard_map/ppermute | solution.py:293

commit v13 on v12

--- a/solution.py
+++ b/solution.py
@@ -301,8 +301,8 @@
     partial = call(
         functools.partial(own_parity, blocks=far, **dims),
         shape((depth * pairs, 3 * filters, 2 * across), f32),
-        [vmem] * (1 + far) + [anywhere] * (far - 2),
-        [w_mine, mine[-1]] + mine[:-1] + behind[:1:-1],
+        [vmem] * (1 + far) + [anywhere] * (far - 3),
+        [w_mine, mine[-1]] + mine[:-1] + behind[2:-1],
         cost=28,
     )
     planes = call(

time: 23 us -> 23.2 us (level)
    ppermute x9, waiting for transfers between devices: 1.68 us -> 0.93 us  [shifted(): return lax.ppermute(x, ('filt', 'space'), pairs)]
    ppermute x5, waiting for transfers between devices: 0.11 us -> 0.84 us  [swapped(): return lax.ppermute(x, 'filt', [(i, i ^ 1) for i in range(size)])]
  transfers between devices with their start and end apart: 14 -> 14, of which waited for: 4 -> 3; matrix products, arithmetic and copies ran while one was open for 0% -> 0% of each run, Pallas kernels for 18% -> 18%
where the time goes in v13:
time: 23.2 us; the launch traced here: 23 us
  starting transfers between devices  15.6 us (67%)
  Pallas kernels  5.51 us (24%)
  waiting for transfers between devices  1.77 us (8%)
    ppermute x9, starting transfers between devices, shifted(): return lax.ppermute(x, ('filt', 'space'), pairs)  14.4 us
    pallas_call x9, Pallas kernels, call(): pl.pallas_call(body, out_shape=outs, in_specs=ins, out_specs=jax.tree.map...  5.51 us
    ppermute x5, starting transfers between devices, swapped(): return lax.ppermute(x, 'filt', [(i, i ^ 1) for i in range(size)])  1.22 us
    ppermute x9, waiting for transfers between devices, shifted(): return lax.ppermute(x, ('filt', 'space'), pairs)  0.93 us
    ppermute x5, waiting for transfers between devices, swapped(): return lax.ppermute(x, 'filt', [(i, i ^ 1) for i in range(size)])  0.84 us
  transfers between devices with their start and end apart: 14, of which 3 were waited for; matrix products, arithmetic and copies ran while one was open for 0% of the time, Pallas kernels for 18%

profile of v13, /device:TPU:0, one launch (start us, length us, event | category | flops | bytes accessed | tf_op | source)
XLA Modules:
  0.0 23.0 jit_solution(14635318412574015965)
XLA Ops:
  0.0 4.0 %collective-permute-start = (bf16[16,4,4,128]{3,2,1,0:T(4,128)(2,1)}, bf16[16,4,4,128]{3,2,1,0:T(4,128)(2,1)S(1)}, u32[]{:S(2)}, u32[]{:S(2)}) collective-permute-start(bf16[16,4,4,128]{3,2,1,0:T(4,128)(2,1)} %param.3), channel_id=1, source_target_pairs={{0,16},{1,17},{2,18},{3,19},{4,20},{5,21},{6,22},{7,23},{8,24},{9,... | collective-permute-start | bytes 196616 | tf_op jit(solution)/shard_map/ppermute | solution.py:213
  4.0 1.0 %shard_map.37 = (bf16[256,128]{1,0:T(8,128)(2,1)S(1)}, bf16[64,128]{1,0:T(8,128)(2,1)S(1)}, bf16[1,32]{1,0:T(2,128)(2,1)S(1)}) custom-call(bf16[256,128]{1,0:T(8,128)(2,1)} %bitcast.24, bf16[1,32]{1,0:T(2,128)(2,1)} %bitcast.25), custom_call_target="tpu_custom_call" | custom-call | flops 4096 | bytes 256 | tf_op jit(solution)/shard_map/pallas_call | solution.py:234
  5.1 1.6 %collective-permute-start.4 = (bf16[64,128]{1,0:T(8,128)(2,1)S(1)}, bf16[64,128]{1,0:T(8,128)(2,1)S(1)}, u32[]{:S(2)}, u32[]{:S(2)}) collective-permute-start(bf16[64,128]{1,0:T(8,128)(2,1)S(1)} %get-tuple-element.16), channel_id=1, source_target_pairs={{0,1},{1,0},{2,3},{3,2},{4,5},{5,4},{6,7},{7,6},{8,9},{9,8},{10,11... | collective-permute-start | bytes 49160 | tf_op jit(solution)/shard_map/ppermute | solution.py:213
  6.6 1.3 %shard_map.38 = (bf16[9,96,128]{2,1,0:T(8,128)(2,1)S(1)}, bf16[9,96,128]{2,1,0:T(8,128)(2,1)S(1)}, f32[32,128]{1,0:T(8,128)S(1)}) custom-call(bf16[864,256]{1,0:T(8,128)(2,1)} %bitcast.26, bf16[1,32]{1,0:T(2,128)(2,1)S(1)} %get-tuple-element.11.bias_ref), custom_call_target="tpu_custom_call" | custom-call | flops 2147483648 | bytes 256 | tf_op jit(solution)/shard_map/pallas_call | solution.py:234
  8.0 0.0 collective-permute-done
  8.0 0.2 shard_map.39.refs_0_
  8.2 2.9 %collective-permute-start.1 = (bf16[512,128]{1,0:T(8,128)(2,1)S(1)}, bf16[512,128]{1,0:T(8,128)(2,1)S(1)}, u32[]{:S(2)}, u32[]{:S(2)}) collective-permute-start(bf16[512,128]{1,0:T(8,128)(2,1)S(1)} %shard_map.39.refs_0_), channel_id=1, source_target_pairs={{0,12},{1,13},{2,14},{3,15},{4,8},{5,9},{6,10},{7,11},{8,4},{9,5},... | collective-permute-start | bytes 393224 | tf_op jit(solution)/shard_map/ppermute | solution.py:213
  11.1 0.5 %collective-permute-start.2 = (bf16[512,128]{1,0:T(8,128)(2,1)S(1)}, bf16[512,128]{1,0:T(8,128)(2,1)S(1)}, u32[]{:S(2)}, u32[]{:S(2)}) collective-permute-start(bf16[512,128]{1,0:T(8,128)(2,1)S(1)} %shard_map.39.refs_0_), channel_id=1, source_target_pairs={{0,4},{1,5},{2,6},{3,7},{4,0},{5,1},{6,2},{7,3},{8,12},{9,13},{10,... | collective-permute-start | bytes 393224 | tf_op jit(solution)/shard_map/ppermute | solution.py:213
  11.6 0.2 collective-permute-start.3
  11.7 0.4 %collective-permute-done.5.refs_2_ = bf16[64,128]{1,0:T(8,128)(2,1)S(1)} collective-permute-done((bf16[64,128]{1,0:T(8,128)(2,1)S(1)}, bf16[64,128]{1,0:T(8,128)(2,1)S(1)}, u32[]{:S(2)}, u32[]{:S(2)}) %collective-permute-start.5) | collective-permute-done | bytes 16416 | tf_op jit(solution)/shard_map/ppermute | solution.py:213
  12.2 1.6 %collective-permute-start.6 = (bf16[128,128]{1,0:T(8,128)(2,1)S(1)}, bf16[128,128]{1,0:T(8,128)(2,1)S(1)}, u32[]{:S(2)}, u32[]{:S(2)}) collective-permute-start(bf16[128,128]{1,0:T(8,128)(2,1)S(1)} %shard_map.40.refs_1_), channel_id=1, source_target_pairs={{0,8},{1,9},{2,10},{3,11},{4,12},{5,13},{6,14},{7,15},{8,0},{9,1},... | collective-permute-start | bytes 98312 | tf_op jit(solution)/shard_map/ppermute | solution.py:213
  13.8 1.5 %collective-permute-start.12 = (bf16[128,128]{1,0:T(8,128)(2,1)S(1)}, bf16[128,128]{1,0:T(8,128)(2,1)S(1)}, u32[]{:S(2)}, u32[]{:S(2)}) collective-permute-start(bf16[128,128]{1,0:T(8,128)(2,1)S(1)} %shard_map.40.refs_1_), channel_id=1, source_target_pairs={{0,12},{1,13},{2,14},{3,15},{4,8},{5,9},{6,10},{7,11},{8,4},{9,5},... | collective-permute-start | bytes 98312 | tf_op jit(solution)/shard_map/ppermute | solution.py:213
  15.3 2.2 %collective-permute-start.11 = (bf16[128,128]{1,0:T(8,128)(2,1)S(1)}, bf16[128,128]{1,0:T(8,128)(2,1)S(1)}, u32[]{:S(2)}, u32[]{:S(2)}) collective-permute-start(bf16[128,128]{1,0:T(8,128)(2,1)S(1)} %shard_map.43), channel_id=1, source_target_pairs={{0,4},{1,5},{2,6},{3,7},{4,0},{5,1},{6,2},{7,3},{8,12},{9,13},{10,... | collective-permute-start | bytes 98312 | tf_op jit(solution)/shard_map/ppermute | solution.py:213
  17.4 0.5 %collective-permute-done.6.refs_4_.refs_3_ = bf16[128,128]{1,0:T(8,128)(2,1)S(1)} collective-permute-done((bf16[128,128]{1,0:T(8,128)(2,1)S(1)}, bf16[128,128]{1,0:T(8,128)(2,1)S(1)}, u32[]{:S(2)}, u32[]{:S(2)}) %collective-permute-start.6) | collective-permute-done | bytes 32800 | tf_op jit(solution)/shard_map/ppermute | solution.py:213
  17.9 0.0 collective-permute-start.7
  17.9 0.5 %collective-permute-start.8 = (bf16[32,16,128]{2,1,0:T(8,128)(2,1)S(1)}, bf16[32,16,128]{2,1,0:T(8,128)(2,1)S(1)}, u32[]{:S(2)}, u32[]{:S(2)}) collective-permute-start(bf16[32,16,128]{2,1,0:T(8,128)(2,1)S(1)} %bitcast.19), channel_id=1, source_target_pairs={{0,2},{2,0},{4,6},{6,4},{8,10},{10,8},{12,14},{14,12},{16,18},{18,... | collective-permute-start | bytes 393224 | tf_op jit(solution)/shard_map/ppermute | solution.py:293
  18.4 0.1 collective-permute-start.9
  18.5 0.8 %shard_map.41.sum_ref.refs_0_ = f32[8,96,256]{2,1,0:T(8,128)S(1)} custom-call(bf16[9,96,128]{2,1,0:T(8,128)(2,1)S(1)} %get-tuple-element.12._.w_ref.w_mine_ref, bf16[32,16,128]{2,1,0:T(8,128)(2,1)S(1)} %bitcast.13, bf16[32,16,128]{2,1,0:T(8,128)(2,1)S(1)} %bitcast.18, bf16[32,16,128]{2,1,0:T(8,128)(2,1)S(1)} %bitcast.20, bf16[32,16,128]{2,1,0:T(8,128)(2,1)S(1)} %bitcast.22, ...), custom_call_target="tpu_custom_call" | custom-call | flops 268435456 | bytes 256 | tf_op jit(solution)/shard_map/pallas_call | solution.py:234
  19.3 0.0 collective-permute-done.12.refs_4_
  19.3 0.5 %collective-permute-start.10 = (bf16[32,16,128]{2,1,0:T(8,128)(2,1)S(1)}, bf16[32,16,128]{2,1,0:T(8,128)(2,1)S(1)}, u32[]{:S(2)}, u32[]{:S(2)}) collective-permute-start(bf16[32,16,128]{2,1,0:T(8,128)(2,1)S(1)} %bitcast.14), channel_id=1, source_target_pairs={{0,2},{2,0},{4,6},{6,4},{8,10},{10,8},{12,14},{14,12},{16,18},{18,... | collective-permute-start | bytes 393224 | tf_op jit(solution)/shard_map/ppermute | solution.py:293
  19.8 0.1 collective-permute-start.13
  20.0 0.8 %collective-permute-done.10.refs_3_ = bf16[32,16,128]{2,1,0:T(8,128)(2,1)S(1)} collective-permute-done((bf16[32,16,128]{2,1,0:T(8,128)(2,1)S(1)}, bf16[32,16,128]{2,1,0:T(8,128)(2,1)S(1)}, u32[]{:S(2)}, u32[]{:S(2)}) %collective-permute-start.10) | collective-permute-done | bytes 131104 | tf_op jit(solution)/shard_map/ppermute | solution.py:293
  20.8 0.9 %shard_map.42.v_ref = f32[16,32,128]{2,1,0:T(8,128)S(1)} custom-call(bf16[9,96,128]{2,1,0:T(8,128)(2,1)S(1)} %get-tuple-element.13.w_ref.w_theirs_ref, f32[32,128]{1,0:T(8,128)S(1)} %get-tuple-element.14.bias_ref, f32[8,96,256]{2,1,0:T(8,128)S(1)} %shard_map.41.sum_ref.refs_0_, bf16[32,16,128]{2,1,0:T(8,128)(2,1)S(1)} %collective-permute-done.7.refs_0_, ...), custom_call_target="tpu_custom_call" | custom-call | flops 4096 | bytes 256 | tf_op jit(solution)/shard_map/pallas_call | solution.py:234
  21.7 1.3 %shard_map.45 = bf16[128,64]{1,0:T(8,128)(2,1)} custom-call(bf16[9,96,128]{2,1,0:T(8,128)(2,1)S(1)} %get-tuple-element.12._.w_ref.w_mine_ref, bf16[9,96,128]{2,1,0:T(8,128)(2,1)S(1)} %get-tuple-element.13.w_ref.w_theirs_ref, f32[16,32,128]{2,1,0:T(8,128)S(1)} %shard_map.42.v_ref, bf16[32,16,128]{2,1,0:T(8,128)(2,1)S(1)} %bitcast.16, ...), custom_call_target="tpu_custom_call" | custom-call | flops 4096 | bytes 256 | tf_op jit(solution)/shard_map/pallas_call | solution.py:234
  (13 shorter events, 0.0 us)
Async XLA Ops:
  0.0 8.0 %collective-permute-start = (bf16[16,4,4,128]{3,2,1,0:T(4,128)(2,1)}, bf16[16,4,4,128]{3,2,1,0:T(4,128)(2,1)S(1)}, u32[]{:S(2)}, u32[]{:S(2)}) collective-permute-start(bf16[16,4,4,128]{3,2,1,0:T(4,128)(2,1)} %param.3), channel_id=1, source_target_pairs={{0,16},{1,17},{2,18},{3,19},{4,20},{5,21},{6,22},{7,23},{8,24},{9,... | collective-permute-start | bytes 196616 | tf_op jit(solution)/shard_map/ppermute | solution.py:213
  5.1 6.7 %collective-permute-start.4 = (bf16[64,128]{1,0:T(8,128)(2,1)S(1)}, bf16[64,128]{1,0:T(8,128)(2,1)S(1)}, u32[]{:S(2)}, u32[]{:S(2)}) collective-permute-start(bf16[64,128]{1,0:T(8,128)(2,1)S(1)} %get-tuple-element.16), channel_id=1, source_target_pairs={{0,1},{1,0},{2,3},{3,2},{4,5},{5,4},{6,7},{7,6},{8,9},{9,8},{10,11... | collective-permute-start | bytes 49160 | tf_op jit(solution)/shard_map/ppermute | solution.py:213
  6.6 5.5 %collective-permute-start.5 = (bf16[64,128]{1,0:T(8,128)(2,1)S(1)}, bf16[64,128]{1,0:T(8,128)(2,1)S(1)}, u32[]{:S(2)}, u32[]{:S(2)}) collective-permute-start(bf16[64,128]{1,0:T(8,128)(2,1)S(1)} %get-tuple-element.16), channel_id=1, source_target_pairs={{0,17},{1,16},{2,19},{3,18},{4,21},{5,20},{6,23},{7,22},{8,25},{9,... | collective-permute-start | bytes 49160 | tf_op jit(solution)/shard_map/ppermute | solution.py:213
  8.2 7.1 %collective-permute-start.1 = (bf16[512,128]{1,0:T(8,128)(2,1)S(1)}, bf16[512,128]{1,0:T(8,128)(2,1)S(1)}, u32[]{:S(2)}, u32[]{:S(2)}) collective-permute-start(bf16[512,128]{1,0:T(8,128)(2,1)S(1)} %shard_map.39.refs_0_), channel_id=1, source_target_pairs={{0,12},{1,13},{2,14},{3,15},{4,8},{5,9},{6,10},{7,11},{8,4},{9,5},... | collective-permute-start | bytes 393224 | tf_op jit(solution)/shard_map/ppermute | solution.py:213
  11.1 6.8 %collective-permute-start.2 = (bf16[512,128]{1,0:T(8,128)(2,1)S(1)}, bf16[512,128]{1,0:T(8,128)(2,1)S(1)}, u32[]{:S(2)}, u32[]{:S(2)}) collective-permute-start(bf16[512,128]{1,0:T(8,128)(2,1)S(1)} %shard_map.39.refs_0_), channel_id=1, source_target_pairs={{0,4},{1,5},{2,6},{3,7},{4,0},{5,1},{6,2},{7,3},{8,12},{9,13},{10,... | collective-permute-start | bytes 393224 | tf_op jit(solution)/shard_map/ppermute | solution.py:213
  11.6 6.8 %collective-permute-start.3 = (bf16[512,128]{1,0:T(8,128)(2,1)S(1)}, bf16[512,128]{1,0:T(8,128)(2,1)S(1)}, u32[]{:S(2)}, u32[]{:S(2)}) collective-permute-start(bf16[512,128]{1,0:T(8,128)(2,1)S(1)} %shard_map.39.refs_0_), channel_id=1, source_target_pairs={{0,8},{1,9},{2,10},{3,11},{4,12},{5,13},{6,14},{7,15},{8,0},{9,1},... | collective-permute-start | bytes 393224 | tf_op jit(solution)/shard_map/ppermute | solution.py:213
  12.2 5.7 %collective-permute-start.6 = (bf16[128,128]{1,0:T(8,128)(2,1)S(1)}, bf16[128,128]{1,0:T(8,128)(2,1)S(1)}, u32[]{:S(2)}, u32[]{:S(2)}) collective-permute-start(bf16[128,128]{1,0:T(8,128)(2,1)S(1)} %shard_map.40.refs_1_), channel_id=1, source_target_pairs={{0,8},{1,9},{2,10},{3,11},{4,12},{5,13},{6,14},{7,15},{8,0},{9,1},... | collective-permute-start | bytes 98312 | tf_op jit(solution)/shard_map/ppermute | solution.py:213
  13.8 5.5 %collective-permute-start.12 = (bf16[128,128]{1,0:T(8,128)(2,1)S(1)}, bf16[128,128]{1,0:T(8,128)(2,1)S(1)}, u32[]{:S(2)}, u32[]{:S(2)}) collective-permute-start(bf16[128,128]{1,0:T(8,128)(2,1)S(1)} %shard_map.40.refs_1_), channel_id=1, source_target_pairs={{0,12},{1,13},{2,14},{3,15},{4,8},{5,9},{6,10},{7,11},{8,4},{9,5},... | collective-permute-start | bytes 98312 | tf_op jit(solution)/shard_map/ppermute | solution.py:213
  15.3 4.5 %collective-permute-start.11 = (bf16[128,128]{1,0:T(8,128)(2,1)S(1)}, bf16[128,128]{1,0:T(8,128)(2,1)S(1)}, u32[]{:S(2)}, u32[]{:S(2)}) collective-permute-start(bf16[128,128]{1,0:T(8,128)(2,1)S(1)} %shard_map.43), channel_id=1, source_target_pairs={{0,4},{1,5},{2,6},{3,7},{4,0},{5,1},{6,2},{7,3},{8,12},{9,13},{10,... | collective-permute-start | bytes 98312 | tf_op jit(solution)/shard_map/ppermute | solution.py:213
  17.9 2.0 %collective-permute-start.7 = (bf16[32,16,128]{2,1,0:T(8,128)(2,1)S(1)}, bf16[32,16,128]{2,1,0:T(8,128)(2,1)S(1)}, u32[]{:S(2)}, u32[]{:S(2)}) collective-permute-start(bf16[32,16,128]{2,1,0:T(8,128)(2,1)S(1)} %bitcast.17), channel_id=1, source_target_pairs={{0,2},{2,0},{4,6},{6,4},{8,10},{10,8},{12,14},{14,12},{16,18},{18,... | collective-permute-start | bytes 393224 | tf_op jit(solution)/shard_map/ppermute | solution.py:293
  17.9 2.0 %collective-permute-start.8 = (bf16[32,16,128]{2,1,0:T(8,128)(2,1)S(1)}, bf16[32,16,128]{2,1,0:T(8,128)(2,1)S(1)}, u32[]{:S(2)}, u32[]{:S(2)}) collective-permute-start(bf16[32,16,128]{2,1,0:T(8,128)(2,1)S(1)} %bitcast.19), channel_id=1, source_target_pairs={{0,2},{2,0},{4,6},{6,4},{8,10},{10,8},{12,14},{14,12},{16,18},{18,... | collective-permute-start | bytes 393224 | tf_op jit(solution)/shard_map/ppermute | solution.py:293
  18.4 1.5 %collective-permute-start.9 = (bf16[32,16,128]{2,1,0:T(8,128)(2,1)S(1)}, bf16[32,16,128]{2,1,0:T(8,128)(2,1)S(1)}, u32[]{:S(2)}, u32[]{:S(2)}) collective-permute-start(bf16[32,16,128]{2,1,0:T(8,128)(2,1)S(1)} %bitcast.21), channel_id=1, source_target_pairs={{0,2},{2,0},{4,6},{6,4},{8,10},{10,8},{12,14},{14,12},{16,18},{18,... | collective-permute-start | bytes 393224 | tf_op jit(solution)/shard_map/ppermute | solution.py:293
  19.3 1.5 %collective-permute-start.10 = (bf16[32,16,128]{2,1,0:T(8,128)(2,1)S(1)}, bf16[32,16,128]{2,1,0:T(8,128)(2,1)S(1)}, u32[]{:S(2)}, u32[]{:S(2)}) collective-permute-start(bf16[32,16,128]{2,1,0:T(8,128)(2,1)S(1)} %bitcast.14), channel_id=1, source_target_pairs={{0,2},{2,0},{4,6},{6,4},{8,10},{10,8},{12,14},{14,12},{16,18},{18,... | collective-permute-start | bytes 393224 | tf_op jit(solution)/shard_map/ppermute | solution.py:293
  19.8 1.8 %collective-permute-start.13 = (bf16[32,16,128]{2,1,0:T(8,128)(2,1)S(1)}, bf16[32,16,128]{2,1,0:T(8,128)(2,1)S(1)}, u32[]{:S(2)}, u32[]{:S(2)}) collective-permute-start(bf16[32,16,128]{2,1,0:T(8,128)(2,1)S(1)} %bitcast.15), channel_id=1, source_target_pairs={{0,2},{2,0},{4,6},{6,4},{8,10},{10,8},{12,14},{14,12},{16,18},{18,... | collective-permute-start | bytes 393224 | tf_op jit(solution)/shard_map/ppermute | solution.py:293

commit v14 on v11

--- a/solution.py
+++ b/solution.py
@@ -105,6 +105,11 @@
         at += ref.shape[0]
 
 
+def join_turned(first, *refs):
+    half = (len(refs) - 1) // 2
+    join(first, *refs[half:-1], *refs[:half], refs[-1])
+
+
 def channels(refs, per_block, row):
     return jnp.concatenate(
         [ref[k * per_block + row] for ref in refs for k in range(ref.shape[0] // per_block)],
@@ -276,10 +281,10 @@
         cost=31,
     )
     planes = call(
-        join,
+        join_turned,
         shape((2 * extra * beside, across), bf16),
         [anywhere] + [vmem] * (2 * extra),
-        [pair] + own_planes + far_planes,
+        [pair] + far_planes + own_planes,
         cost=31,
     )
 

time: 23 us -> 22.9 us (level)
  waiting for transfers between devices: 1.68 us -> 1.37 us
    ppermute x9, waiting for transfers between devices: 1.58 us -> 1.27 us  [shifted(): return lax.ppermute(x, ('filt', 'space'), pairs)]
    ppermute x9, starting transfers between devices: 14.4 us -> 14.7 us  [shifted(): return lax.ppermute(x, ('filt', 'space'), pairs)]
  transfers between devices with their start and end apart: 14 -> 14, of which waited for: 4 -> 3; matrix products, arithmetic and copies ran while one was open for 0% -> 0% of each run, Pallas kernels for 19% -> 19%
where the time goes in v14:
time: 22.9 us; the launch traced here: 22.7 us
  starting transfers between devices  15.7 us (69%)
  Pallas kernels  5.5 us (24%)
  waiting for transfers between devices  1.37 us (6%)
    ppermute x9, starting transfers between devices, shifted(): return lax.ppermute(x, ('filt', 'space'), pairs)  14.7 us
    pallas_call x9, Pallas kernels, call(): pl.pallas_call(body, out_shape=outs, in_specs=ins, out_specs=jax.tree.map...  5.5 us
    ppermute x9, waiting for transfers between devices, shifted(): return lax.ppermute(x, ('filt', 'space'), pairs)  1.27 us
    ppermute x5, starting transfers between devices, swapped(): return lax.ppermute(x, 'filt', [(i, i ^ 1) for i in range(size)])  1.09 us
  transfers between devices with their start and end apart: 14, of which 3 were waited for; matrix products, arithmetic and copies ran while one was open for 0% of the time, Pallas kernels for 19%

profile of v14, /device:TPU:0, one launch (start us, length us, event | category | flops | bytes accessed | tf_op | source)
XLA Modules:
  0.0 22.7 jit_solution(3939719845381637079)
XLA Ops:
  0.0 4.0 %collective-permute-start = (bf16[16,4,4,128]{3,2,1,0:T(4,128)(2,1)}, bf16[16,4,4,128]{3,2,1,0:T(4,128)(2,1)S(1)}, u32[]{:S(2)}, u32[]{:S(2)}) collective-permute-start(bf16[16,4,4,128]{3,2,1,0:T(4,128)(2,1)} %param.3), channel_id=1, source_target_pairs={{0,16},{1,17},{2,18},{3,19},{4,20},{5,21},{6,22},{7,23},{8,24},{9,... | collective-permute-start | bytes 196616 | tf_op jit(solution)/shard_map/ppermute | solution.py:218
  4.0 1.0 %shard_map.37 = (bf16[256,128]{1,0:T(8,128)(2,1)S(1)}, bf16[64,128]{1,0:T(8,128)(2,1)S(1)}, bf16[1,32]{1,0:T(2,128)(2,1)S(1)}) custom-call(bf16[256,128]{1,0:T(8,128)(2,1)} %bitcast.24, bf16[1,32]{1,0:T(2,128)(2,1)} %bitcast.25), custom_call_target="tpu_custom_call" | custom-call | flops 4096 | bytes 256 | tf_op jit(solution)/shard_map/pallas_call | solution.py:239
  5.1 1.3 %collective-permute-start.4 = (bf16[64,128]{1,0:T(8,128)(2,1)S(1)}, bf16[64,128]{1,0:T(8,128)(2,1)S(1)}, u32[]{:S(2)}, u32[]{:S(2)}) collective-permute-start(bf16[64,128]{1,0:T(8,128)(2,1)S(1)} %get-tuple-element.16), channel_id=1, source_target_pairs={{0,17},{1,16},{2,19},{3,18},{4,21},{5,20},{6,23},{7,22},{8,25},{9,... | collective-permute-start | bytes 49160 | tf_op jit(solution)/shard_map/ppermute | solution.py:218
  6.4 0.3 %collective-permute-start.5 = (bf16[64,128]{1,0:T(8,128)(2,1)S(1)}, bf16[64,128]{1,0:T(8,128)(2,1)S(1)}, u32[]{:S(2)}, u32[]{:S(2)}) collective-permute-start(bf16[64,128]{1,0:T(8,128)(2,1)S(1)} %get-tuple-element.16), channel_id=1, source_target_pairs={{0,1},{1,0},{2,3},{3,2},{4,5},{5,4},{6,7},{7,6},{8,9},{9,8},{10,11... | collective-permute-start | bytes 49160 | tf_op jit(solution)/shard_map/ppermute | solution.py:218
  6.7 1.3 %shard_map.38 = (bf16[9,96,128]{2,1,0:T(8,128)(2,1)S(1)}, bf16[9,96,128]{2,1,0:T(8,128)(2,1)S(1)}, f32[32,128]{1,0:T(8,128)S(1)}) custom-call(bf16[864,256]{1,0:T(8,128)(2,1)} %bitcast.26, bf16[1,32]{1,0:T(2,128)(2,1)S(1)} %get-tuple-element.11.bias_ref), custom_call_target="tpu_custom_call" | custom-call | flops 2147483648 | bytes 256 | tf_op jit(solution)/shard_map/pallas_call | solution.py:239
  8.0 0.0 collective-permute-done
  8.1 0.2 shard_map.39.first
  8.3 2.8 %collective-permute-start.1 = (bf16[512,128]{1,0:T(8,128)(2,1)S(1)}, bf16[512,128]{1,0:T(8,128)(2,1)S(1)}, u32[]{:S(2)}, u32[]{:S(2)}) collective-permute-start(bf16[512,128]{1,0:T(8,128)(2,1)S(1)} %shard_map.39.first), channel_id=1, source_target_pairs={{0,12},{1,13},{2,14},{3,15},{4,8},{5,9},{6,10},{7,11},{8,4},{9,5},... | collective-permute-start | bytes 393224 | tf_op jit(solution)/shard_map/ppermute | solution.py:218
  11.1 0.5 %collective-permute-start.2 = (bf16[512,128]{1,0:T(8,128)(2,1)S(1)}, bf16[512,128]{1,0:T(8,128)(2,1)S(1)}, u32[]{:S(2)}, u32[]{:S(2)}) collective-permute-start(bf16[512,128]{1,0:T(8,128)(2,1)S(1)} %shard_map.39.first), channel_id=1, source_target_pairs={{0,4},{1,5},{2,6},{3,7},{4,0},{5,1},{6,2},{7,3},{8,12},{9,13},{10,... | collective-permute-start | bytes 393224 | tf_op jit(solution)/shard_map/ppermute | solution.py:218
  11.6 0.2 collective-permute-start.3
  11.8 0.0 collective-permute-done.4.refs_0_
  11.8 0.0 collective-permute-done.5.refs_1_
  11.8 1.9 %collective-permute-start.6 = (bf16[128,128]{1,0:T(8,128)(2,1)S(1)}, bf16[128,128]{1,0:T(8,128)(2,1)S(1)}, u32[]{:S(2)}, u32[]{:S(2)}) collective-permute-start(bf16[128,128]{1,0:T(8,128)(2,1)S(1)} %shard_map.40.refs_1_), channel_id=1, source_target_pairs={{0,8},{1,9},{2,10},{3,11},{4,12},{5,13},{6,14},{7,15},{8,0},{9,1},... | collective-permute-start | bytes 98312 | tf_op jit(solution)/shard_map/ppermute | solution.py:218
  13.7 1.4 %collective-permute-start.7 = (bf16[128,128]{1,0:T(8,128)(2,1)S(1)}, bf16[128,128]{1,0:T(8,128)(2,1)S(1)}, u32[]{:S(2)}, u32[]{:S(2)}) collective-permute-start(bf16[128,128]{1,0:T(8,128)(2,1)S(1)} %shard_map.40.refs_1_), channel_id=1, source_target_pairs={{0,12},{1,13},{2,14},{3,15},{4,8},{5,9},{6,10},{7,11},{8,4},{9,5},... | collective-permute-start | bytes 98312 | tf_op jit(solution)/shard_map/ppermute | solution.py:218
  15.1 2.2 %collective-permute-start.12 = (bf16[128,128]{1,0:T(8,128)(2,1)S(1)}, bf16[128,128]{1,0:T(8,128)(2,1)S(1)}, u32[]{:S(2)}, u32[]{:S(2)}) collective-permute-start(bf16[128,128]{1,0:T(8,128)(2,1)S(1)} %shard_map.43), channel_id=1, source_target_pairs={{0,4},{1,5},{2,6},{3,7},{4,0},{5,1},{6,2},{7,3},{8,12},{9,13},{10,... | collective-permute-start | bytes 98312 | tf_op jit(solution)/shard_map/ppermute | solution.py:218
  17.3 0.7 %collective-permute-done.6.refs_4_.refs_3_ = bf16[128,128]{1,0:T(8,128)(2,1)S(1)} collective-permute-done((bf16[128,128]{1,0:T(8,128)(2,1)S(1)}, bf16[128,128]{1,0:T(8,128)(2,1)S(1)}, u32[]{:S(2)}, u32[]{:S(2)}) %collective-permute-start.6) | collective-permute-done | bytes 32800 | tf_op jit(solution)/shard_map/ppermute | solution.py:218
  17.9 0.6 %collective-permute-done.7.refs_5_.refs_4_ = bf16[128,128]{1,0:T(8,128)(2,1)S(1)} collective-permute-done((bf16[128,128]{1,0:T(8,128)(2,1)S(1)}, bf16[128,128]{1,0:T(8,128)(2,1)S(1)}, u32[]{:S(2)}, u32[]{:S(2)}) %collective-permute-start.7) | collective-permute-done | bytes 32800 | tf_op jit(solution)/shard_map/ppermute | solution.py:218
  18.5 0.5 %collective-permute-start.9 = (bf16[32,16,128]{2,1,0:T(8,128)(2,1)S(1)}, bf16[32,16,128]{2,1,0:T(8,128)(2,1)S(1)}, u32[]{:S(2)}, u32[]{:S(2)}) collective-permute-start(bf16[32,16,128]{2,1,0:T(8,128)(2,1)S(1)} %bitcast.19), channel_id=1, source_target_pairs={{0,2},{2,0},{4,6},{6,4},{8,10},{10,8},{12,14},{14,12},{16,18},{18,... | collective-permute-start | bytes 393224 | tf_op jit(solution)/shard_map/ppermute | solution.py:298
  19.0 0.1 collective-permute-start.10
  19.1 0.8 %shard_map.41.sum_ref.refs_0_ = f32[8,96,256]{2,1,0:T(8,128)S(1)} custom-call(bf16[9,96,128]{2,1,0:T(8,128)(2,1)S(1)} %get-tuple-element.12._.w_ref.w_mine_ref, bf16[32,16,128]{2,1,0:T(8,128)(2,1)S(1)} %bitcast.14, bf16[32,16,128]{2,1,0:T(8,128)(2,1)S(1)} %bitcast.18, bf16[32,16,128]{2,1,0:T(8,128)(2,1)S(1)} %bitcast.20, bf16[32,16,128]{2,1,0:T(8,128)(2,1)S(1)} %bitcast.22, ...), custom_call_target="tpu_custom_call" | custom-call | flops 268435456 | bytes 256 | tf_op jit(solution)/shard_map/pallas_call | solution.py:239
  19.9 0.5 %collective-permute-start.13 = (bf16[32,16,128]{2,1,0:T(8,128)(2,1)S(1)}, bf16[32,16,128]{2,1,0:T(8,128)(2,1)S(1)}, u32[]{:S(2)}, u32[]{:S(2)}) collective-permute-start(bf16[32,16,128]{2,1,0:T(8,128)(2,1)S(1)} %bitcast.15), channel_id=1, source_target_pairs={{0,2},{2,0},{4,6},{6,4},{8,10},{10,8},{12,14},{14,12},{16,18},{18,... | collective-permute-start | bytes 393224 | tf_op jit(solution)/shard_map/ppermute | solution.py:298
  20.4 0.9 %shard_map.42.v_ref = f32[16,32,128]{2,1,0:T(8,128)S(1)} custom-call(bf16[9,96,128]{2,1,0:T(8,128)(2,1)S(1)} %get-tuple-element.13.w_ref.w_theirs_ref, f32[32,128]{1,0:T(8,128)S(1)} %get-tuple-element.14.bias_ref, f32[8,96,256]{2,1,0:T(8,128)S(1)} %shard_map.41.sum_ref.refs_0_, bf16[32,16,128]{2,1,0:T(8,128)(2,1)S(1)} %collective-permute-done.8.refs_0_, ...), custom_call_target="tpu_custom_call" | custom-call | flops 4096 | bytes 256 | tf_op jit(solution)/shard_map/pallas_call | solution.py:239
  21.3 0.1 collective-permute-done.13.refs_1_
  21.4 1.3 %shard_map.45 = bf16[128,64]{1,0:T(8,128)(2,1)} custom-call(bf16[9,96,128]{2,1,0:T(8,128)(2,1)S(1)} %get-tuple-element.12._.w_ref.w_mine_ref, bf16[9,96,128]{2,1,0:T(8,128)(2,1)S(1)} %get-tuple-element.13.w_ref.w_theirs_ref, f32[16,32,128]{2,1,0:T(8,128)S(1)} %shard_map.42.v_ref, bf16[32,16,128]{2,1,0:T(8,128)(2,1)S(1)} %bitcast.16, ...), custom_call_target="tpu_custom_call" | custom-call | flops 4096 | bytes 256 | tf_op jit(solution)/shard_map/pallas_call | solution.py:239
  (13 shorter events, 0.0 us)
Async XLA Ops:
  0.0 8.0 %collective-permute-start = (bf16[16,4,4,128]{3,2,1,0:T(4,128)(2,1)}, bf16[16,4,4,128]{3,2,1,0:T(4,128)(2,1)S(1)}, u32[]{:S(2)}, u32[]{:S(2)}) collective-permute-start(bf16[16,4,4,128]{3,2,1,0:T(4,128)(2,1)} %param.3), channel_id=1, source_target_pairs={{0,16},{1,17},{2,18},{3,19},{4,20},{5,21},{6,22},{7,23},{8,24},{9,... | collective-permute-start | bytes 196616 | tf_op jit(solution)/shard_map/ppermute | solution.py:218
  5.1 6.7 %collective-permute-start.4 = (bf16[64,128]{1,0:T(8,128)(2,1)S(1)}, bf16[64,128]{1,0:T(8,128)(2,1)S(1)}, u32[]{:S(2)}, u32[]{:S(2)}) collective-permute-start(bf16[64,128]{1,0:T(8,128)(2,1)S(1)} %get-tuple-element.16), channel_id=1, source_target_pairs={{0,17},{1,16},{2,19},{3,18},{4,21},{5,20},{6,23},{7,22},{8,25},{9,... | collective-permute-start | bytes 49160 | tf_op jit(solution)/shard_map/ppermute | solution.py:218
  6.4 5.4 %collective-permute-start.5 = (bf16[64,128]{1,0:T(8,128)(2,1)S(1)}, bf16[64,128]{1,0:T(8,128)(2,1)S(1)}, u32[]{:S(2)}, u32[]{:S(2)}) collective-permute-start(bf16[64,128]{1,0:T(8,128)(2,1)S(1)} %get-tuple-element.16), channel_id=1, source_target_pairs={{0,1},{1,0},{2,3},{3,2},{4,5},{5,4},{6,7},{7,6},{8,9},{9,8},{10,11... | collective-permute-start | bytes 49160 | tf_op jit(solution)/shard_map/ppermute | solution.py:218
  8.3 6.8 %collective-permute-start.1 = (bf16[512,128]{1,0:T(8,128)(2,1)S(1)}, bf16[512,128]{1,0:T(8,128)(2,1)S(1)}, u32[]{:S(2)}, u32[]{:S(2)}) collective-permute-start(bf16[512,128]{1,0:T(8,128)(2,1)S(1)} %shard_map.39.first), channel_id=1, source_target_pairs={{0,12},{1,13},{2,14},{3,15},{4,8},{5,9},{6,10},{7,11},{8,4},{9,5},... | collective-permute-start | bytes 393224 | tf_op jit(solution)/shard_map/ppermute | solution.py:218
  11.1 7.4 %collective-permute-start.2 = (bf16[512,128]{1,0:T(8,128)(2,1)S(1)}, bf16[512,128]{1,0:T(8,128)(2,1)S(1)}, u32[]{:S(2)}, u32[]{:S(2)}) collective-permute-start(bf16[512,128]{1,0:T(8,128)(2,1)S(1)} %shard_map.39.first), channel_id=1, source_target_pairs={{0,4},{1,5},{2,6},{3,7},{4,0},{5,1},{6,2},{7,3},{8,12},{9,13},{10,... | collective-permute-start | bytes 393224 | tf_op jit(solution)/shard_map/ppermute | solution.py:218
  11.6 7.4 %collective-permute-start.3 = (bf16[512,128]{1,0:T(8,128)(2,1)S(1)}, bf16[512,128]{1,0:T(8,128)(2,1)S(1)}, u32[]{:S(2)}, u32[]{:S(2)}) collective-permute-start(bf16[512,128]{1,0:T(8,128)(2,1)S(1)} %shard_map.39.first), channel_id=1, source_target_pairs={{0,8},{1,9},{2,10},{3,11},{4,12},{5,13},{6,14},{7,15},{8,0},{9,1},... | collective-permute-start | bytes 393224 | tf_op jit(solution)/shard_map/ppermute | solution.py:218
  11.8 6.1 %collective-permute-start.6 = (bf16[128,128]{1,0:T(8,128)(2,1)S(1)}, bf16[128,128]{1,0:T(8,128)(2,1)S(1)}, u32[]{:S(2)}, u32[]{:S(2)}) collective-permute-start(bf16[128,128]{1,0:T(8,128)(2,1)S(1)} %shard_map.40.refs_1_), channel_id=1, source_target_pairs={{0,8},{1,9},{2,10},{3,11},{4,12},{5,13},{6,14},{7,15},{8,0},{9,1},... | collective-permute-start | bytes 98312 | tf_op jit(solution)/shard_map/ppermute | solution.py:218
  13.7 4.8 %collective-permute-start.7 = (bf16[128,128]{1,0:T(8,128)(2,1)S(1)}, bf16[128,128]{1,0:T(8,128)(2,1)S(1)}, u32[]{:S(2)}, u32[]{:S(2)}) collective-permute-start(bf16[128,128]{1,0:T(8,128)(2,1)S(1)} %shard_map.40.refs_1_), channel_id=1, source_target_pairs={{0,12},{1,13},{2,14},{3,15},{4,8},{5,9},{6,10},{7,11},{8,4},{9,5},... | collective-permute-start | bytes 98312 | tf_op jit(solution)/shard_map/ppermute | solution.py:218
  15.1 4.8 %collective-permute-start.12 = (bf16[128,128]{1,0:T(8,128)(2,1)S(1)}, bf16[128,128]{1,0:T(8,128)(2,1)S(1)}, u32[]{:S(2)}, u32[]{:S(2)}) collective-permute-start(bf16[128,128]{1,0:T(8,128)(2,1)S(1)} %shard_map.43), channel_id=1, source_target_pairs={{0,4},{1,5},{2,6},{3,7},{4,0},{5,1},{6,2},{7,3},{8,12},{9,13},{10,... | collective-permute-start | bytes 98312 | tf_op jit(solution)/shard_map/ppermute | solution.py:218
  17.9 2.5 %collective-permute-start.8 = (bf16[32,16,128]{2,1,0:T(8,128)(2,1)S(1)}, bf16[32,16,128]{2,1,0:T(8,128)(2,1)S(1)}, u32[]{:S(2)}, u32[]{:S(2)}) collective-permute-start(bf16[32,16,128]{2,1,0:T(8,128)(2,1)S(1)} %bitcast.17), channel_id=1, source_target_pairs={{0,2},{2,0},{4,6},{6,4},{8,10},{10,8},{12,14},{14,12},{16,18},{18,... | collective-permute-start | bytes 393224 | tf_op jit(solution)/shard_map/ppermute | solution.py:298
  18.5 1.9 %collective-permute-start.11 = (bf16[32,16,128]{2,1,0:T(8,128)(2,1)S(1)}, bf16[32,16,128]{2,1,0:T(8,128)(2,1)S(1)}, u32[]{:S(2)}, u32[]{:S(2)}) collective-permute-start(bf16[32,16,128]{2,1,0:T(8,128)(2,1)S(1)} %bitcast.13), channel_id=1, source_target_pairs={{0,2},{2,0},{4,6},{6,4},{8,10},{10,8},{12,14},{14,12},{16,18},{18,... | collective-permute-start | bytes 393224 | tf_op jit(solution)/shard_map/ppermute | solution.py:298
  18.5 1.9 %collective-permute-start.9 = (bf16[32,16,128]{2,1,0:T(8,128)(2,1)S(1)}, bf16[32,16,128]{2,1,0:T(8,128)(2,1)S(1)}, u32[]{:S(2)}, u32[]{:S(2)}) collective-permute-start(bf16[32,16,128]{2,1,0:T(8,128)(2,1)S(1)} %bitcast.19), channel_id=1, source_target_pairs={{0,2},{2,0},{4,6},{6,4},{8,10},{10,8},{12,14},{14,12},{16,18},{18,... | collective-permute-start | bytes 393224 | tf_op jit(solution)/shard_map/ppermute | solution.py:298
  19.0 1.4 %collective-permute-start.10 = (bf16[32,16,128]{2,1,0:T(8,128)(2,1)S(1)}, bf16[32,16,128]{2,1,0:T(8,128)(2,1)S(1)}, u32[]{:S(2)}, u32[]{:S(2)}) collective-permute-start(bf16[32,16,128]{2,1,0:T(8,128)(2,1)S(1)} %bitcast.21), channel_id=1, source_target_pairs={{0,2},{2,0},{4,6},{6,4},{8,10},{10,8},{12,14},{14,12},{16,18},{18,... | collective-permute-start | bytes 393224 | tf_op jit(solution)/shard_map/ppermute | solution.py:298
  19.9 1.5 %collective-permute-start.13 = (bf16[32,16,128]{2,1,0:T(8,128)(2,1)S(1)}, bf16[32,16,128]{2,1,0:T(8,128)(2,1)S(1)}, u32[]{:S(2)}, u32[]{:S(2)}) collective-permute-start(bf16[32,16,128]{2,1,0:T(8,128)(2,1)S(1)} %bitcast.15), channel_id=1, source_target_pairs={{0,2},{2,0},{4,6},{6,4},{8,10},{10,8},{12,14},{14,12},{16,18},{18,... | collective-permute-start | bytes 393224 | tf_op jit(solution)/shard_map/ppermute | solution.py:298
